TPU v7x, 512 devices: a whole 4x8x8 slice. The times are simulated.
512 devices in a mesh: section: 8 (over z_lo, x), expert: 64 (over z_hi, y, core).
Axes of the slice: x: 4, y: 8, z: 8 (z_hi: 4, z_lo: 2; z = z_hi * 2 + z_lo), core: 2. Of those that a mesh axis runs over, the one named last changes fastest.
Arguments:
- fwd_act: bfloat16 [8, 8192, 2048], P('section', 'expert'), may hold values from -6 to 6
- fwd_ids: int32 [8, 8192, 8], P('section', 'expert'), may hold values from 0 to 127, all different within a row; in each aligned block of 128 rows (0 to 127, 128 to 255, ..., all dimensions but the last counted through in order) at most 10 rows name the same one
- fwd_gates: float32 [8, 8192, 8], P('section', 'expert'), may hold values from 0.1 to 1
- bwd_input: bfloat16 [8, 8192, 2048], P('section', 'expert'), may hold values from -6 to 6
- bwd_ids: int32 [8, 8192, 8], P('section', 'expert'), may hold values from 0 to 127, all different within a row; in each aligned block of 128 rows (0 to 127, 128 to 255, ..., all dimensions but the last counted through in order) at most 10 rows name the same one
- bwd_gates: float32 [8, 8192, 8], P('section', 'expert'), may hold values from 0.1 to 1
- bwd_grad: bfloat16 [8, 8192, 2048], P('section', 'expert'), may hold values from -6 to 6
- w_gate: bfloat16 [8, 2048, 12288], P('section', None, 'expert'), may hold values from -0.125 to 0.125
- w_up: bfloat16 [8, 2048, 12288], P('section', None, 'expert'), may hold values from -0.125 to 0.125
- w_down: bfloat16 [8, 12288, 2048], P('section', 'expert'), may hold values from -0.21875 to 0.21875
Outputs:
- routed_out: bfloat16 [8, 8192, 2048], P('section', 'expert')
- input_grad: bfloat16 [8, 8192, 2048], P('section', 'expert')
Inputs may be any that keep to these rules, and one draw needn't show every extreme that they name: `fwd_ids`: each row names 8 different experts; among the 128 rows of one device no expert is named more than 10 times. `bwd_ids`: each row names 8 different experts; among the 128 rows of one device no expert is named more than 10 times.
All inputs are finite; a program needn't handle non-finite values.
Results may differ from a plain program's by a relative error of at most 0.0064.
Values may be sent and summed in bfloat16 or wider, within the bound.
No kernel may reach another device: no remote copies, remote signals or barrier semaphores. Data moves between devices by JAX's collectives and lax.ppermute only.
A program may use at most 128 MiB of HBM per device.

v0:
```python
import jax
import jax.numpy as jnp
from jax import lax
from jax.sharding import PartitionSpec as P

SHARDS = 4
CAP = 10


def from_behind(x, axis, by):
    devices = lax.axis_size(axis)
    pairs = [(i, i + by) for i in range(devices) if 0 <= i + by < devices]
    return lax.ppermute(x, axis, pairs)


def slot_tables(route_ids, route_gates, experts):
    local_rows = route_ids.shape[0]
    per_token = route_ids.shape[1]
    flat_ids = route_ids.reshape(-1)
    chosen = (flat_ids[:, None] == jnp.arange(experts, dtype=jnp.int32)[None, :]).astype(jnp.int32)
    before = jnp.cumsum(chosen, axis=0) - chosen
    slot_of = jnp.sum(before * chosen, axis=1)
    expert_safe = jnp.where(flat_ids < experts, flat_ids, experts)
    token_of = jnp.arange(local_rows * per_token, dtype=jnp.int32) // per_token
    table = (
        jnp.full((experts + 1, CAP), local_rows, jnp.int32).at[expert_safe, slot_of].set(token_of)
    )
    weights = (
        jnp.zeros((experts + 1, CAP), jnp.float32)
        .at[expert_safe, slot_of]
        .set(route_gates.reshape(-1))
    )
    return (table[:experts], weights[:experts])


def pick_rows(states, table):
    padded = jnp.concatenate([states, jnp.zeros((1, states.shape[1]), states.dtype)], axis=0)
    return padded[table]


def spread(per_expert):
    experts, slots, width = per_expert.shape
    copies = jnp.broadcast_to(per_expert[:, None], (experts, SHARDS, slots, width))
    return copies.reshape(experts * SHARDS, slots, width)


def prepare(per_expert):
    return spread(per_expert)


def expert_forward(received, gate_dev, up_dev, down_dev):
    sources, slots, width = received.shape
    flat = received.reshape(sources * slots, width)
    gate_pre = jnp.dot(flat, gate_dev, preferred_element_type=jnp.float32)
    up_pre = jnp.dot(flat, up_dev, preferred_element_type=jnp.float32)
    act = (jax.nn.silu(gate_pre) * up_pre).astype(jnp.bfloat16)
    partial_out = jnp.dot(act, down_dev, preferred_element_type=jnp.float32).astype(jnp.bfloat16)
    return partial_out.reshape(sources, slots, width)


def expert_backward(received, scaled, gate_dev, up_dev, down_dev):
    sources, slots, width = received.shape
    flat = received.reshape(sources * slots, width)
    scaled_flat = scaled.reshape(sources * slots, width)
    gate_back = jnp.dot(flat, gate_dev, preferred_element_type=jnp.float32)
    up_back = jnp.dot(flat, up_dev, preferred_element_type=jnp.float32)
    contract = (((1,), (1,)), ((), ()))
    dact = lax.dot_general(scaled_flat, down_dev, contract, preferred_element_type=jnp.float32)
    sigma = jax.nn.sigmoid(gate_back)
    dgate = (dact * up_back * sigma * (1.0 + gate_back * (1.0 - sigma))).astype(jnp.bfloat16)
    dup = (dact * jax.nn.silu(gate_back)).astype(jnp.bfloat16)
    partial_in = lax.dot_general(dgate, gate_dev, contract, preferred_element_type=jnp.float32)
    partial_in = partial_in + lax.dot_general(
        dup, up_dev, contract, preferred_element_type=jnp.float32
    )
    return partial_in.astype(jnp.bfloat16).reshape(sources, slots, width)


def send_back(partial_rows, experts):
    returned = lax.all_to_all(partial_rows, "expert", split_axis=0, concat_axis=0, tiled=True)
    sources, slots, width = returned.shape
    return jnp.sum(returned.reshape(experts, SHARDS, slots, width).astype(jnp.float32), axis=1)


def combine(summed, table, local_rows):
    width = summed.shape[2]
    result = (
        jnp.zeros((local_rows + 1, width), jnp.float32)
        .at[table.reshape(-1)]
        .add(summed.reshape(-1, width))
    )
    return result[:local_rows]


def shards(
    fwd_act, fwd_ids, fwd_gates, bwd_input, bwd_ids, bwd_gates, bwd_grad, w_gate, w_up, w_down
):
    section_at = lax.axis_index("section")
    sections = lax.axis_size("section")
    experts = lax.axis_size("expert") // SHARDS
    local_rows = fwd_act.shape[1]
    shifted = from_behind(fwd_act, "section", 1)
    inbound = jnp.where(section_at == 0, fwd_act, shifted)[0]
    arriving = from_behind(bwd_grad, "section", -1)
    grads = jnp.where(section_at == sections - 1, bwd_grad, arriving)[0]
    gate_dev = w_gate[0]
    up_dev = w_up[0]
    down_dev = w_down[0]
    fwd_table, fwd_weight = slot_tables(fwd_ids[0], fwd_gates[0], experts)
    bwd_table, bwd_weight = slot_tables(bwd_ids[0], bwd_gates[0], experts)
    fwd_send = prepare(pick_rows(inbound, fwd_table))
    bwd_send = prepare(pick_rows(bwd_input[0], bwd_table))
    scaled = (pick_rows(grads, bwd_table).astype(jnp.float32) * bwd_weight[:, :, None]).astype(
        jnp.bfloat16
    )
    scaled_send = prepare(scaled)
    stacked = lax.all_to_all(fwd_send, "expert", split_axis=0, concat_axis=0, tiled=True)[None]
    fwd_summed = send_back(expert_forward(stacked[0], gate_dev, up_dev, down_dev), experts)
    stacked = jnp.stack(
        [
            lax.all_to_all(bwd_send, "expert", split_axis=0, concat_axis=0, tiled=True),
            lax.all_to_all(scaled_send, "expert", split_axis=0, concat_axis=0, tiled=True),
        ],
        axis=0,
    )
    bwd_summed = send_back(
        expert_backward(stacked[0], stacked[1], gate_dev, up_dev, down_dev), experts
    )
    routed_out = combine(fwd_weight[:, :, None] * fwd_summed, fwd_table, local_rows).astype(
        jnp.bfloat16
    )
    input_grad = combine(bwd_summed, bwd_table, local_rows).astype(jnp.bfloat16)
    return (routed_out[None], input_grad[None])


def solution(mesh):
    in_specs = (
        P("section", "expert", None),
        P("section", "expert", None),
        P("section", "expert", None),
        P("section", "expert", None),
        P("section", "expert", None),
        P("section", "expert", None),
        P("section", "expert", None),
        P("section", None, "expert"),
        P("section", None, "expert"),
        P("section", "expert", None),
    )
    out_specs = (P("section", "expert", None), P("section", "expert", None))
    return jax.shard_map(shards, mesh=mesh, in_specs=in_specs, out_specs=out_specs, check_vma=False)
```

profile of v0, /device:TPU:1, one launch (start us, length us, event | category | flops | bytes accessed | tf_op | source)
XLA Modules:
  0.0 726.8 jit_solution(10941804394296502462)
XLA Ops:
  2.9 4.5 reduce-window.14
  7.9 4.5 reduce-window.16
  15.0 4.3 scatter_custom_fusion.4
  25.0 17.9 %all-to-all-start.3 = ((bf16[64,10,2048]{2,1,0:T(8,128)(2,1)}), bf16[64,10,2048]{2,1,0:T(8,128)(2,1)}, u32[]{:S(2)}, u32[]{:S(2)}) async-start(bf16[64,10,2048]{2,1,0:T(8,128)(2,1)} %bitcast.90), calls=%async_computation.3 | async-start | bytes 8388608 | tf_op jit(solution)/shard_map/all_to_all | solution.py:121
  44.5 4.3 scatter_custom_fusion.5
  49.0 9.0 %collective-permute-done.1 = bf16[1,128,2048]{2,1,0:T(8,128)(2,1)S(1)} collective-permute-done((bf16[1,128,2048]{2,1,0:T(8,128)(2,1)S(1)}, bf16[1,128,2048]{2,1,0:T(8,128)(2,1)S(1)}, u32[]{:S(2)}, u32[]{:S(2)}) %collective-permute-start.1) | collective-permute-done | bytes 524320 | tf_op jit(solution)/shard_map/ppermute | solution.py:13
  60.5 90.8 %all-to-all-done.3 = bf16[64,10,2048]{2,1,0:T(8,128)(2,1)} async-done(((bf16[64,10,2048]{2,1,0:T(8,128)(2,1)}), bf16[64,10,2048]{2,1,0:T(8,128)(2,1)}, u32[]{:S(2)}, u32[]{:S(2)}) %all-to-all-start.3) | async-done | bytes 2621472 | tf_op jit(solution)/shard_map/all_to_all | solution.py:121
  155.0 29.5 %all-to-all-start.2 = ((bf16[64,10,2048]{2,1,0:T(8,128)(2,1)}), bf16[64,10,2048]{2,1,0:T(8,128)(2,1)}, u32[]{:S(2)}, u32[]{:S(2)}) async-start(bf16[64,10,2048]{2,1,0:T(8,128)(2,1)} %bitcast.91), calls=%async_computation.2 | async-start | bytes 8388608 | tf_op jit(solution)/shard_map/all_to_all | solution.py:122
  184.6 4.1 collective-permute-start
  188.7 4.4 scatter_custom_fusion.2
  193.5 6.0 collective-permute-done
  200.8 82.7 %all-to-all-done.2 = bf16[64,10,2048]{2,1,0:T(8,128)(2,1)} async-done(((bf16[64,10,2048]{2,1,0:T(8,128)(2,1)}), bf16[64,10,2048]{2,1,0:T(8,128)(2,1)}, u32[]{:S(2)}, u32[]{:S(2)}) %all-to-all-start.2) | async-done | bytes 2621472 | tf_op jit(solution)/shard_map/all_to_all | solution.py:122
  286.1 40.3 %all-to-all-start = ((bf16[64,10,2048]{2,1,0:T(8,128)(2,1)}), bf16[64,10,2048]{2,1,0:T(8,128)(2,1)}, u32[]{:S(2)}, u32[]{:S(2)}) async-start(bf16[64,10,2048]{2,1,0:T(8,128)(2,1)} %bitcast.92), calls=%async_computation | async-start | bytes 8388608 | tf_op jit(solution)/shard_map/all_to_all | solution.py:117
  333.4 5.5 reshape_squeeze_stack.6
  342.7 5.9 fusion.6
  355.1 94.2 %all-to-all-done = bf16[64,10,2048]{2,1,0:T(8,128)(2,1)} async-done(((bf16[64,10,2048]{2,1,0:T(8,128)(2,1)}), bf16[64,10,2048]{2,1,0:T(8,128)(2,1)}, u32[]{:S(2)}, u32[]{:S(2)}) %all-to-all-start) | async-done | bytes 2621472 | tf_op jit(solution)/shard_map/all_to_all | solution.py:117
  449.2 42.1 %all-to-all-start.4 = ((bf16[64,10,2048]{2,1,0:T(8,128)(2,1)}), bf16[64,10,2048]{2,1,0:T(8,128)(2,1)}, u32[]{:S(2)}, u32[]{:S(2)}) async-start(bf16[64,10,2048]{2,1,0:T(8,128)(2,1)} %reshape.227), calls=%async_computation.4 | async-start | bytes 8388608 | tf_op jit(solution)/shard_map/all_to_all | solution.py:80
  491.3 4.1 reshape_squeeze_broadcast_in_dim.3
  498.3 5.0 convolution_convert_fusion
  503.4 5.4 reshape.222
  508.7 82.1 %all-to-all-done.4 = bf16[64,10,2048]{2,1,0:T(8,128)(2,1)} async-done(((bf16[64,10,2048]{2,1,0:T(8,128)(2,1)}), bf16[64,10,2048]{2,1,0:T(8,128)(2,1)}, u32[]{:S(2)}, u32[]{:S(2)}) %all-to-all-start.4) | async-done | bytes 2621472 | tf_op jit(solution)/shard_map/all_to_all | solution.py:80
  590.8 29.6 %all-to-all-start.1 = ((bf16[64,10,2048]{2,1,0:T(8,128)(2,1)}), bf16[64,10,2048]{2,1,0:T(8,128)(2,1)}, u32[]{:S(2)}, u32[]{:S(2)}) async-start(bf16[64,10,2048]{2,1,0:T(8,128)(2,1)} %reshape.222), calls=%async_computation.1 | async-start | bytes 8388608 | tf_op jit(solution)/shard_map/all_to_all | solution.py:80
  621.0 4.7 scatter_custom_fusion.3
  634.9 82.9 %all-to-all-done.1 = bf16[64,10,2048]{2,1,0:T(8,128)(2,1)} async-done(((bf16[64,10,2048]{2,1,0:T(8,128)(2,1)}), bf16[64,10,2048]{2,1,0:T(8,128)(2,1)}, u32[]{:S(2)}, u32[]{:S(2)}) %all-to-all-start.1) | async-done | bytes 2621472 | tf_op jit(solution)/shard_map/all_to_all | solution.py:80
  (99 shorter events, 61.9 us)
Async XLA Ops:
  0.6 342.1 %copy-start = (bf16[1,2048,192]{1,2,0:T(8,128)(2,1)S(1)}, bf16[1,2048,192]{1,2,0:T(8,128)(2,1)}, u32[]{:S(2)}) copy-start(bf16[1,2048,192]{1,2,0:T(8,128)(2,1)} %param.18) | copy-start | bytes 2359300
  25.0 18.0 %copy-start.1 = (bf16[1,128,2048]{2,1,0:T(8,128)(2,1)S(1)}, bf16[1,128,2048]{2,1,0:T(8,128)(2,1)}, u32[]{:S(2)}) copy-start(bf16[1,128,2048]{2,1,0:T(8,128)(2,1)} %param.16) | copy-start | bytes 1572868
  25.0 19.3 %copy-start.4 = (f32[1,128,8]{1,2,0:T(8,128)S(1)}, f32[1,128,8]{1,2,0:T(8,128)}, u32[]{:S(2)}) copy-start(f32[1,128,8]{1,2,0:T(8,128)} %param.15) | copy-start | bytes 12292
  25.0 126.3 %all-to-all-start.3 = ((bf16[64,10,2048]{2,1,0:T(8,128)(2,1)}), bf16[64,10,2048]{2,1,0:T(8,128)(2,1)}, u32[]{:S(2)}, u32[]{:S(2)}) async-start(bf16[64,10,2048]{2,1,0:T(8,128)(2,1)} %bitcast.90), calls=%async_computation.3 | async-start | bytes 8388608 | tf_op jit(solution)/shard_map/all_to_all | solution.py:121
  43.0 15.0 %collective-permute-start.1 = (bf16[1,128,2048]{2,1,0:T(8,128)(2,1)S(1)}, bf16[1,128,2048]{2,1,0:T(8,128)(2,1)S(1)}, u32[]{:S(2)}, u32[]{:S(2)}) collective-permute-start(bf16[1,128,2048]{2,1,0:T(8,128)(2,1)S(1)} %copy-done.1), channel_id=1, source_target_pairs={{64,0},{128,64},{192,128},{256,192},{320,256},{384,320},{448,384},... | collective-permute-start | bytes 1572872 | tf_op jit(solution)/shard_map/ppermute | solution.py:13
  155.0 29.5 %copy-start.2 = (bf16[1,128,2048]{2,1,0:T(8,128)(2,1)S(1)}, bf16[1,128,2048]{2,1,0:T(8,128)(2,1)}, u32[]{:S(2)}) copy-start(bf16[1,128,2048]{2,1,0:T(8,128)(2,1)} %param.10) | copy-start | bytes 1572868
  155.0 128.5 %all-to-all-start.2 = ((bf16[64,10,2048]{2,1,0:T(8,128)(2,1)}), bf16[64,10,2048]{2,1,0:T(8,128)(2,1)}, u32[]{:S(2)}, u32[]{:S(2)}) async-start(bf16[64,10,2048]{2,1,0:T(8,128)(2,1)} %bitcast.91), calls=%async_computation.2 | async-start | bytes 8388608 | tf_op jit(solution)/shard_map/all_to_all | solution.py:122
  184.6 14.9 %collective-permute-start = (bf16[1,128,2048]{2,1,0:T(8,128)(2,1)S(1)}, bf16[1,128,2048]{2,1,0:T(8,128)(2,1)S(1)}, u32[]{:S(2)}, u32[]{:S(2)}) collective-permute-start(bf16[1,128,2048]{2,1,0:T(8,128)(2,1)S(1)} %copy-done.2), channel_id=1, source_target_pairs={{0,64},{64,128},{128,192},{192,256},{256,320},{320,384},{384,448},... | collective-permute-start | bytes 1572872 | tf_op jit(solution)/shard_map/ppermute | solution.py:13
  286.1 163.1 %all-to-all-start = ((bf16[64,10,2048]{2,1,0:T(8,128)(2,1)}), bf16[64,10,2048]{2,1,0:T(8,128)(2,1)}, u32[]{:S(2)}, u32[]{:S(2)}) async-start(bf16[64,10,2048]{2,1,0:T(8,128)(2,1)} %bitcast.92), calls=%async_computation | async-start | bytes 8388608 | tf_op jit(solution)/shard_map/all_to_all | solution.py:117
  449.2 141.6 %all-to-all-start.4 = ((bf16[64,10,2048]{2,1,0:T(8,128)(2,1)}), bf16[64,10,2048]{2,1,0:T(8,128)(2,1)}, u32[]{:S(2)}, u32[]{:S(2)}) async-start(bf16[64,10,2048]{2,1,0:T(8,128)(2,1)} %reshape.227), calls=%async_computation.4 | async-start | bytes 8388608 | tf_op jit(solution)/shard_map/all_to_all | solution.py:80
  508.7 111.7 %copy-start.3 = (s32[16,10]{0,1:T(8,128)S(1)}, s32[16,10]{0,1:T(8,128)}, u32[]{:S(2)}) copy-start(s32[16,10]{0,1:T(8,128)} %get-tuple-element.7) | copy-start | bytes 1924
  508.7 112.1 %copy-start.5 = (f32[1,128,8]{1,2,0:T(8,128)S(1)}, f32[1,128,8]{1,2,0:T(8,128)}, u32[]{:S(2)}) copy-start(f32[1,128,8]{1,2,0:T(8,128)} %param.12) | copy-start | bytes 12292
  590.8 126.9 %all-to-all-start.1 = ((bf16[64,10,2048]{2,1,0:T(8,128)(2,1)}), bf16[64,10,2048]{2,1,0:T(8,128)(2,1)}, u32[]{:S(2)}, u32[]{:S(2)}) async-start(bf16[64,10,2048]{2,1,0:T(8,128)(2,1)} %reshape.222), calls=%async_computation.1 | async-start | bytes 8388608 | tf_op jit(solution)/shard_map/all_to_all | solution.py:80
where the time goes:
time: 734 us; the launch traced here: 727 us
  waiting for transfers between devices  448 us (61%)
  starting transfers between devices  165 us (22%)
  local copies, waits for them, and re-layouts  61.9 us (8%)
  other arithmetic  27.2 us (4%)
  matrix products  24.2 us (3%)
    all_to_all x2, waiting for transfers between devices, send_back(): lax.all_to_all(partial_rows, 'expert', split_axis=0, concat_axis=0, tiled...  165 us
    all_to_all x1, waiting for transfers between devices, shards(): lax.all_to_all(fwd_send, 'expert', split_axis=0, concat_axis=0, tiled=True)  94.2 us
    all_to_all x1, waiting for transfers between devices, shards(): lax.all_to_all(bwd_send, 'expert', split_axis=0, concat_axis=0, tiled=True)  90.8 us
    all_to_all x1, waiting for transfers between devices, shards(): lax.all_to_all(scaled_send, 'expert', split_axis=0, concat_axis=0, tiled=...  82.7 us
    all_to_all x2, starting transfers between devices, send_back(): lax.all_to_all(partial_rows, 'expert', split_axis=0, concat_axis=0, tiled...  71.7 us
    all_to_all x1, starting transfers between devices, shards(): lax.all_to_all(fwd_send, 'expert', split_axis=0, concat_axis=0, tiled=True)  40.3 us
    all_to_all x1, starting transfers between devices, shards(): lax.all_to_all(scaled_send, 'expert', split_axis=0, concat_axis=0, tiled=...  29.5 us
    unnamed x24, local copies, waits for them, and re-layouts  19.9 us
  transfers between devices with their start and end apart: 7, of which 7 were waited for; matrix products, arithmetic and copies ran while one was open for 10% of the time, Pallas kernels for 0%

commit v1 on v0

v1 whole, which is shorter than its diff:
```python
import functools

import jax
import jax.numpy as jnp
from jax import lax
from jax.experimental import pallas as pl
from jax.experimental.pallas import tpu as pltpu
from jax.sharding import Mesh
from jax.sharding import PartitionSpec as P

EXPERTS = 16
SHARDS = 4
CAP = 10
TILE = 16
CHUNKS = 8
ROWS = EXPERTS * CAP
SPAN = EXPERTS * TILE
PACKED = CAP * CHUNKS
TILES = PACKED // TILE
NONE = -100.0

MEETS = [
    (j, c, TILE * j - CAP * c)
    for j in range(TILES)
    for c in range(CHUNKS)
    if -TILE < TILE * j - CAP * c < CAP
]

BF16 = jnp.bfloat16
F32 = jnp.float32
NT = (((1,), (1,)), ((), ()))
VMEM = pl.BlockSpec(memory_space=pltpu.VMEM)
SMEM = pl.BlockSpec(memory_space=pltpu.SMEM)


def iota(shape, dim):
    return lax.broadcasted_iota(jnp.int32, shape, dim)


def dot(a, b):
    return jnp.dot(a, b, preferred_element_type=F32)


def dot_nt(a, b):
    return lax.dot_general(a, b, NT, preferred_element_type=F32)


def halves(values):
    upper = values.astype(BF16)
    return upper, (values - upper.astype(F32)).astype(BF16)


def call(body, outs, n_in, scratch=(), smem=0, flops=0, size=0, vmem=40):
    return pl.pallas_call(
        body,
        out_shape=outs,
        in_specs=[SMEM] * smem + [VMEM] * (n_in - smem),
        out_specs=jax.tree.map(lambda _: VMEM, outs),
        scratch_shapes=list(scratch),
        compiler_params=pltpu.CompilerParams(vmem_limit_bytes=vmem * 2**20),
        cost_estimate=pl.CostEstimate(flops=flops, bytes_accessed=size, transcendentals=0),
    )


def keys_by_expert(ids, gates, turn):
    tokens, top = ids.shape
    turn[:, :top] = ids.astype(F32)
    turn[:, top : 2 * top] = gates
    turned = turn[...].T
    expert = iota((EXPERTS, tokens), 0).astype(F32)
    chosen = jnp.zeros((EXPERTS, tokens), F32)
    gate = jnp.zeros((EXPERTS, tokens), F32)
    for k in range(top):
        hit = turned[k : k + 1] == expert
        chosen = chosen + hit.astype(F32)
        gate = gate + jnp.where(hit, turned[top + k : top + k + 1], 0.0)
    earlier = (iota((tokens, tokens), 0) < iota((tokens, tokens), 1)).astype(F32).astype(BF16)
    slot = dot(chosen.astype(BF16), earlier)
    return jnp.where(chosen > 0, slot, NONE), gate


def spread_rows(values):
    experts, tokens = values.shape
    wide = jnp.broadcast_to(values[:, None, :], (experts, TILE, tokens))
    return wide.reshape(experts * TILE, tokens)


def pick_body(weighted, *refs):
    if weighted is None:
        ids, gates, own, out, turn = refs
        states = own
    else:
        edge, ids, gates, own, shifted, out, turn, states = refs
        at_edge = edge[0] == 1

        @pl.when(at_edge)
        def _():
            states[...] = own[...]

        @pl.when(jnp.logical_not(at_edge))
        def _():
            states[...] = shifted[...]

    key, gate = keys_by_expert(ids[...], gates[...], turn)
    key = spread_rows(key)
    row = lax.rem(iota(key.shape, 0), TILE).astype(F32)
    parts = [1.0]
    if weighted:
        parts = [h.astype(F32) for h in halves(spread_rows(gate))]
    width = own.shape[1] // CHUNKS
    for j in range(TILES):
        total = jnp.zeros((SPAN, width), F32)
        for _, c, shift in [m for m in MEETS if m[0] == j]:
            hit = key == row + float(shift)
            piece = states[:, c * width : (c + 1) * width]
            for part in parts:
                total = total + dot(jnp.where(hit, part, 0.0).astype(BF16), piece)
        out[:, j * TILE : (j + 1) * TILE, :] = total.astype(BF16).reshape(EXPERTS, TILE, width)


def pick(ids, gates, own, shifted=None, edge=None, weighted=False):
    tokens, width = own.shape
    out = jax.ShapeDtypeStruct((EXPERTS, PACKED, width // CHUNKS), BF16)
    scratch = [pltpu.VMEM((tokens, 128), F32)]
    cost = {"flops": 400_000_000, "size": 2_000_000}
    if shifted is None:
        return call(functools.partial(pick_body, None), out, 3, scratch, **cost)(ids, gates, own)
    scratch.append(pltpu.VMEM((tokens, width), BF16))
    return call(functools.partial(pick_body, weighted), out, 5, scratch, smem=1, **cost)(
        edge, ids, gates, own, shifted
    )


def combine_body(weighted, ids, gates, back, out):
    tokens, top = ids.shape
    lane = iota((tokens, 128), 1)
    chosen = jnp.zeros((tokens, 128), F32)
    gate = jnp.zeros((tokens, 128), F32)
    for k in range(top):
        hit = ids[:, k : k + 1] == lane
        chosen = chosen + hit.astype(F32)
        gate = gate + jnp.where(hit, gates[:, k : k + 1], 0.0)
    earlier = (iota((tokens, tokens), 1) < iota((tokens, tokens), 0)).astype(F32).astype(BF16)
    slot = dot(earlier, chosen.astype(BF16))
    key = jnp.where(chosen > 0, slot, NONE)
    widen = (iota((128, SPAN), 0) == iota((128, SPAN), 1) // TILE).astype(F32).astype(BF16)
    key = dot(key.astype(BF16), widen)
    row = lax.rem(iota(key.shape, 1), TILE).astype(F32)
    parts = [1.0]
    if weighted:
        parts = [dot(h, widen) for h in halves(gate)]
    width = out.shape[1] // CHUNKS
    for c in range(CHUNKS):
        total = jnp.zeros((tokens, width), F32)
        for j, _, shift in [m for m in MEETS if m[1] == c]:
            hit = key == row + float(shift)
            rows = back[:, j * TILE : (j + 1) * TILE, :].reshape(SPAN, width)
            for part in parts:
                total = total + dot(jnp.where(hit, part, 0.0).astype(BF16), rows)
        out[:, c * width : (c + 1) * width] = total.astype(BF16)


def combine(ids, gates, back, weighted):
    tokens = ids.shape[0]
    out = jax.ShapeDtypeStruct((tokens, back.shape[2] * CHUNKS), BF16)
    body = functools.partial(combine_body, weighted)
    return call(body, out, 3, flops=400_000_000, size=2_000_000)(ids, gates, back)


def line_up_body(gate, up, down, out):
    hidden = gate.shape[1]
    same = (iota((hidden, hidden), 0) == iota((hidden, hidden), 1)).astype(F32).astype(BF16)
    out[0] = dot_nt(same, gate[...]).astype(BF16)
    out[1] = dot_nt(same, up[...]).astype(BF16)
    out[2] = down[...]


def line_up(gate, up, down):
    out = jax.ShapeDtypeStruct((3,) + down.shape, BF16)
    return call(line_up_body, out, 3, flops=400_000_000, size=5_000_000)(gate, up, down)


def unpack_rows(packed, rows):
    width = packed.shape[2]
    at = iota((ROWS, SPAN), 0)
    lane = iota((ROWS, SPAN), 1)
    source, line = lane // TILE, lax.rem(lane, TILE)
    for c in range(CHUNKS):
        total = jnp.zeros((ROWS, width), F32)
        for j, _, shift in [m for m in MEETS if m[1] == c]:
            slot = line + shift
            hit = (at == source * CAP + slot) & (slot >= 0) & (slot < CAP)
            tile = packed[:, j * TILE : (j + 1) * TILE, :].reshape(SPAN, width)
            total = total + dot(hit.astype(F32).astype(BF16), tile)
        rows[:, c * width : (c + 1) * width] = total.astype(BF16)


def pack_rows(rows, packed):
    width = packed.shape[2]
    at = iota((SPAN, ROWS), 1)
    place = iota((SPAN, ROWS), 0)
    source, line = place // TILE, lax.rem(place, TILE)
    for j in range(TILES):
        total = jnp.zeros((SPAN, width), F32)
        for _, c, shift in [m for m in MEETS if m[0] == j]:
            slot = line + shift
            hit = (at == source * CAP + slot) & (slot >= 0) & (slot < CAP)
            piece = rows[:, c * width : (c + 1) * width].astype(BF16)
            total = total + dot(hit.astype(F32).astype(BF16), piece)
        packed[:, j * TILE : (j + 1) * TILE, :] = total.astype(BF16).reshape(EXPERTS, TILE, width)


def forward_body(*refs):
    got, weights, out, rows, total = refs[0], refs[1 : 1 + SHARDS], *refs[1 + SHARDS :]
    unpack_rows(got, rows)
    for n, w in enumerate(weights):
        gate_pre = dot_nt(rows[...], w[0])
        up_pre = dot_nt(rows[...], w[1])
        act = (gate_pre / (1.0 + jnp.exp(-gate_pre)) * up_pre).astype(BF16)
        part = dot(act, w[2])
        total[...] = part if n == 0 else total[...] + part
    pack_rows(total, out)


def backward_body(*refs):
    got, got_scaled, weights = refs[0], refs[1], refs[2 : 2 + SHARDS]
    out, rows, scaled, total = refs[2 + SHARDS :]
    unpack_rows(got, rows)
    unpack_rows(got_scaled, scaled)
    for n, w in enumerate(weights):
        gate_back = dot_nt(rows[...], w[0])
        up_back = dot_nt(rows[...], w[1])
        dact = dot_nt(scaled[...], w[2])
        sigma = 1.0 / (1.0 + jnp.exp(-gate_back))
        dgate = (dact * up_back * sigma * (1.0 + gate_back * (1.0 - sigma))).astype(BF16)
        dup = (dact * (gate_back * sigma)).astype(BF16)
        part = dot(dgate, w[0]) + dot(dup, w[1])
        total[...] = part if n == 0 else total[...] + part
    pack_rows(total, out)


def experts_of(body, got, weights):
    width = got[0].shape[2] * CHUNKS
    scratch = [pltpu.VMEM((ROWS, width), BF16) for _ in got] + [pltpu.VMEM((ROWS, width), F32)]
    out = jax.ShapeDtypeStruct(got[0].shape, BF16)
    return call(
        body, out, len(got) + len(weights), scratch, flops=4_000_000_000, size=12_000_000
    )(*got, *weights)


def from_behind(x, axis, by):
    devices = lax.axis_size(axis)
    pairs = [(i, i + by) for i in range(devices) if 0 <= i + by < devices]
    return lax.ppermute(x, axis, pairs)


def swap(x, axis):
    return lax.ppermute(x, axis, [(0, 1), (1, 0)])


def exchange(x):
    return lax.all_to_all(x, ("plane", "pair"), split_axis=0, concat_axis=0, tiled=True)


def shards(
    fwd_act, fwd_ids, fwd_gates, bwd_input, bwd_ids, bwd_gates, bwd_grad, w_gate, w_up, w_down
):
    section_at = lax.axis_index("section")
    sections = lax.axis_size("section")
    first = (section_at == 0).astype(jnp.int32).reshape(1)
    last = (section_at == sections - 1).astype(jnp.int32).reshape(1)
    arriving = from_behind(bwd_grad[0], "section", -1)
    shifted = from_behind(fwd_act[0], "section", 1)

    own = line_up(w_gate[0], w_up[0], w_down[0])
    across = swap(own, "half")
    weights = [own, swap(own, "core"), across, swap(across, "core")]

    bwd_got = exchange(pick(bwd_ids[0], bwd_gates[0], bwd_input[0]))
    scaled_got = exchange(
        pick(bwd_ids[0], bwd_gates[0], bwd_grad[0], arriving, last, weighted=True)
    )
    fwd_got = exchange(pick(fwd_ids[0], fwd_gates[0], fwd_act[0], shifted, first))

    bwd_back = exchange(experts_of(backward_body, [bwd_got, scaled_got], weights))
    fwd_back = exchange(experts_of(forward_body, [fwd_got], weights))
    input_grad = combine(bwd_ids[0], bwd_gates[0], bwd_back, False)
    routed_out = combine(fwd_ids[0], fwd_gates[0], fwd_back, True)
    return (routed_out[None], input_grad[None])


def solution(mesh):
    sections, devices = mesh.devices.shape
    planes = 4
    parted = Mesh(
        mesh.devices.reshape(sections, planes, devices // planes // 4, 2, 2),
        ("section", "plane", "pair", "half", "core"),
    )
    expert = ("plane", "pair", "half", "core")
    rows = P("section", expert, None)
    columns = P("section", None, expert)
    return jax.shard_map(
        shards,
        mesh=parted,
        in_specs=(rows,) * 7 + (columns, columns, rows),
        out_specs=(rows, rows),
        check_vma=False,
    )
```

time: 734 us -> 212 us (0.29)
  the two profiles are of different devices: /device:TPU:1 before, /device:TPU:64 now
where the time goes in v1:
time: 212 us
  waiting for transfers between devices  119 us (56%)
  starting transfers between devices  57.5 us (27%)
  Pallas kernels  30.6 us (14%)
  local copies, waits for them, and re-layouts  3.39 us (2%)
    all_to_all x5, waiting for transfers between devices, exchange(): lax.all_to_all(x, ('plane', 'pair'), split_axis=0, concat_axis=0, tiled=T...  60.7 us
    all_to_all x5, starting transfers between devices, exchange(): lax.all_to_all(x, ('plane', 'pair'), split_axis=0, concat_axis=0, tiled=T...  42 us
    ppermute x3, waiting for transfers between devices, swap(): return lax.ppermute(x, axis, [(0, 1), (1, 0)])  34.1 us
    ppermute x2, waiting for transfers between devices, from_behind(): return lax.ppermute(x, axis, pairs)  24.5 us
    pallas_call x2, Pallas kernels, experts_of(): call(body, out, len(got) + len(weights), scratch, flops=4000000000, size=...  19 us
    ppermute x2, starting transfers between devices, from_behind(): return lax.ppermute(x, axis, pairs)  8.06 us
    ppermute x3, starting transfers between devices, swap(): return lax.ppermute(x, axis, [(0, 1), (1, 0)])  7.43 us
  transfers between devices with their start and end apart: 10, of which 6 were waited for; matrix products, arithmetic and copies ran while one was open for 0% of the time, Pallas kernels for 12%

profile of v1, /device:TPU:64, one launch (start us, length us, event | category | flops | bytes accessed | tf_op | source)
XLA Modules:
  0.0 211.5 jit_solution(2586147137324651275)
XLA Ops:
  3.6 2.3 %shard_map.114.refs_1_.refs_2_ = bf16[3,192,2048]{2,1,0:T(8,128)(2,1)} custom-call(bf16[2048,192]{1,0:T(8,128)(2,1)S(1)} %bitcast.14, bf16[2048,192]{1,0:T(8,128)(2,1)S(1)} %bitcast.15, bf16[192,2048]{1,0:T(8,128)(2,1)S(1)} %bitcast.16), custom_call_target="tpu_custom_call" | custom-call | flops 400000000 | bytes 5000000 | tf_op jit(solution)/shard_map/pallas_call | solution.py:180
  5.9 3.6 %collective-permute-start.2 = (bf16[3,192,2048]{2,1,0:T(8,128)(2,1)}, bf16[3,192,2048]{2,1,0:T(8,128)(2,1)}, u32[]{:S(2)}, u32[]{:S(2)}) collective-permute-start(bf16[3,192,2048]{2,1,0:T(8,128)(2,1)} %shard_map.114.refs_1_.refs_2_), channel_id=1, source_target_pairs={{0,2},{2,0},{1,3},{3,1},{4,6},{6,4},{5,7},{7,5},{8,10},{10,8},{9,1... | collective-permute-start | bytes 7077896 | tf_op jit(solution)/shard_map/ppermute | solution.py:258
  9.8 1.7 shard_map.117
  11.4 14.0 %all-to-all-start.2 = ((bf16[16,80,256]{2,1,0:T(8,128)(2,1)}), bf16[16,80,256]{2,1,0:T(8,128)(2,1)S(1)}, u32[]{:S(2)}, u32[]{:S(2)}) async-start(bf16[16,80,256]{2,1,0:T(8,128)(2,1)} %shard_map.117), calls=%async_computation.2 | async-start | bytes 1310720 | tf_op jit(solution)/shard_map/all_to_all | solution.py:262
  25.5 4.7 %collective-permute-start.4 = (bf16[128,2048]{1,0:T(8,128)(2,1)S(1)}, bf16[128,2048]{1,0:T(8,128)(2,1)S(1)}, u32[]{:S(2)}, u32[]{:S(2)}) collective-permute-start(bf16[128,2048]{1,0:T(8,128)(2,1)S(1)} %bitcast.17), channel_id=1, source_target_pairs={{64,0},{128,64},{192,128},{256,192},{320,256},{384,320},{448,384},... | collective-permute-start | bytes 1572872 | tf_op jit(solution)/shard_map/ppermute | solution.py:254
  30.1 1.9 collective-permute-start.1
  32.1 34.1 %collective-permute-done.2.refs_3_.refs_4_ = bf16[3,192,2048]{2,1,0:T(8,128)(2,1)} collective-permute-done((bf16[3,192,2048]{2,1,0:T(8,128)(2,1)}, bf16[3,192,2048]{2,1,0:T(8,128)(2,1)}, u32[]{:S(2)}, u32[]{:S(2)}) %collective-permute-start.2) | collective-permute-done | bytes 2359328 | tf_op jit(solution)/shard_map/ppermute | solution.py:258
  66.2 1.9 collective-permute-start.3
  68.1 2.1 %shard_map.118 = bf16[16,80,256]{2,1,0:T(8,128)(2,1)} custom-call(s32[1]{0:T(128)} %bitcast.11.refs_0_, s32[128,8]{1,0:T(8,128)S(1)} %bitcast.22, f32[128,8]{1,0:T(8,128)S(1)} %bitcast.25, bf16[128,2048]{1,0:T(8,128)(2,1)S(1)} %bitcast.18, bf16[128,2048]{1,0:T(8,128)(2,1)S(1)} %collective-permute-done.4.refs_4_), custom_call_target="tpu_custom_call" | custom-call | flops 400000000 | bytes 2000000 | tf_op jit(solution)/shard_map/pallas_call | solution.py:129
  70.2 16.9 %all-to-all-done.2.refs_0_ = bf16[16,80,256]{2,1,0:T(8,128)(2,1)S(1)} async-done(((bf16[16,80,256]{2,1,0:T(8,128)(2,1)}), bf16[16,80,256]{2,1,0:T(8,128)(2,1)S(1)}, u32[]{:S(2)}, u32[]{:S(2)}) %all-to-all-start.2) | async-done | bytes 655392 | tf_op jit(solution)/shard_map/all_to_all | solution.py:262
  87.1 4.1 %all-to-all-start.3 = ((bf16[16,80,256]{2,1,0:T(8,128)(2,1)}), bf16[16,80,256]{2,1,0:T(8,128)(2,1)S(1)}, u32[]{:S(2)}, u32[]{:S(2)}) async-start(bf16[16,80,256]{2,1,0:T(8,128)(2,1)} %shard_map.118), calls=%async_computation.3 | async-start | bytes 1310720 | tf_op jit(solution)/shard_map/all_to_all | solution.py:262
  91.2 3.4 %collective-permute-start = (bf16[128,2048]{1,0:T(8,128)(2,1)S(1)}, bf16[128,2048]{1,0:T(8,128)(2,1)S(1)}, u32[]{:S(2)}, u32[]{:S(2)}) collective-permute-start(bf16[128,2048]{1,0:T(8,128)(2,1)S(1)} %bitcast.19), channel_id=1, source_target_pairs={{0,64},{64,128},{128,192},{192,256},{256,320},{320,384},{384,448},... | collective-permute-start | bytes 1572872 | tf_op jit(solution)/shard_map/ppermute | solution.py:254
  94.9 24.5 %collective-permute-done.refs_4_ = bf16[128,2048]{1,0:T(8,128)(2,1)S(1)} collective-permute-done((bf16[128,2048]{1,0:T(8,128)(2,1)S(1)}, bf16[128,2048]{1,0:T(8,128)(2,1)S(1)}, u32[]{:S(2)}, u32[]{:S(2)}) %collective-permute-start) | collective-permute-done | bytes 524320 | tf_op jit(solution)/shard_map/ppermute | solution.py:254
  119.3 1.7 shard_map.113
  121.1 10.2 %all-to-all-start = ((bf16[16,80,256]{2,1,0:T(8,128)(2,1)}), bf16[16,80,256]{2,1,0:T(8,128)(2,1)S(1)}, u32[]{:S(2)}, u32[]{:S(2)}) async-start(bf16[16,80,256]{2,1,0:T(8,128)(2,1)} %shard_map.113), calls=%async_computation | async-start | bytes 1310720 | tf_op jit(solution)/shard_map/all_to_all | solution.py:262
  131.3 10.4 %shard_map.119 = bf16[16,80,256]{2,1,0:T(8,128)(2,1)} custom-call(bf16[16,80,256]{2,1,0:T(8,128)(2,1)S(1)} %all-to-all-done.2.refs_0_, bf16[16,80,256]{2,1,0:T(8,128)(2,1)S(1)} %all-to-all-done.3.refs_1_, bf16[3,192,2048]{2,1,0:T(8,128)(2,1)} %shard_map.114.refs_1_.refs_2_, bf16[3,192,2048]{2,1,0:T(8,128)(2,1)} %collective-permute-done.1.refs_2_.refs_3_, ...), custom_call_target="tpu_custom_call" | custom-call | flops 4000000000 | bytes 12000000 | tf_op jit(solution)/shard_map/pallas_call | solution.py:246
  141.7 12.9 %all-to-all-done.refs_0_ = bf16[16,80,256]{2,1,0:T(8,128)(2,1)S(1)} async-done(((bf16[16,80,256]{2,1,0:T(8,128)(2,1)}), bf16[16,80,256]{2,1,0:T(8,128)(2,1)S(1)}, u32[]{:S(2)}, u32[]{:S(2)}) %all-to-all-start) | async-done | bytes 655392 | tf_op jit(solution)/shard_map/all_to_all | solution.py:262
  154.7 6.8 %all-to-all-start.4 = ((bf16[16,80,256]{2,1,0:T(8,128)(2,1)}), bf16[16,80,256]{2,1,0:T(8,128)(2,1)S(1)}, u32[]{:S(2)}, u32[]{:S(2)}) async-start(bf16[16,80,256]{2,1,0:T(8,128)(2,1)} %shard_map.119), calls=%async_computation.4 | async-start | bytes 1310720 | tf_op jit(solution)/shard_map/all_to_all | solution.py:262
  161.5 8.6 %shard_map.115 = bf16[16,80,256]{2,1,0:T(8,128)(2,1)} custom-call(bf16[16,80,256]{2,1,0:T(8,128)(2,1)S(1)} %all-to-all-done.refs_0_, bf16[3,192,2048]{2,1,0:T(8,128)(2,1)} %shard_map.114.refs_1_.refs_2_, bf16[3,192,2048]{2,1,0:T(8,128)(2,1)} %collective-permute-done.1.refs_2_.refs_3_, bf16[3,192,2048]{2,1,0:T(8,128)(2,1)} %collective-permute-done.2.refs_3_.refs_4_, ...), custom_call_target="tpu_custom_call" | custom-call | flops 4000000000 | bytes 12000000 | tf_op jit(solution)/shard_map/pallas_call | solution.py:246
  170.0 12.4 %all-to-all-done.4.back = bf16[16,80,256]{2,1,0:T(8,128)(2,1)S(1)} async-done(((bf16[16,80,256]{2,1,0:T(8,128)(2,1)}), bf16[16,80,256]{2,1,0:T(8,128)(2,1)S(1)}, u32[]{:S(2)}, u32[]{:S(2)}) %all-to-all-start.4) | async-done | bytes 655392 | tf_op jit(solution)/shard_map/all_to_all | solution.py:262
  182.5 6.9 %all-to-all-start.1 = ((bf16[16,80,256]{2,1,0:T(8,128)(2,1)}), bf16[16,80,256]{2,1,0:T(8,128)(2,1)S(1)}, u32[]{:S(2)}, u32[]{:S(2)}) async-start(bf16[16,80,256]{2,1,0:T(8,128)(2,1)} %shard_map.115), calls=%async_computation.1 | async-start | bytes 1310720 | tf_op jit(solution)/shard_map/all_to_all | solution.py:262
  189.3 1.7 shard_map.120
  191.1 18.4 %all-to-all-done.1.back = bf16[16,80,256]{2,1,0:T(8,128)(2,1)S(1)} async-done(((bf16[16,80,256]{2,1,0:T(8,128)(2,1)}), bf16[16,80,256]{2,1,0:T(8,128)(2,1)S(1)}, u32[]{:S(2)}, u32[]{:S(2)}) %all-to-all-start.1) | async-done | bytes 655392 | tf_op jit(solution)/shard_map/all_to_all | solution.py:262
  209.5 2.0 shard_map.116
  (26 shorter events, 3.4 us)
Async XLA Ops:
  0.6 3.0 %copy-start = (bf16[1,192,2048]{2,1,0:T(8,128)(2,1)S(1)}, bf16[1,192,2048]{2,1,0:T(8,128)(2,1)}, u32[]{:S(2)}) copy-start(bf16[1,192,2048]{2,1,0:T(8,128)(2,1)} %param.19) | copy-start | bytes 2359300
  3.6 5.9 %copy-start.4 = (s32[1,128,8]{1,2,0:T(8,128)S(1)}, s32[1,128,8]{1,2,0:T(8,128)}, u32[]{:S(2)}) copy-start(s32[1,128,8]{1,2,0:T(8,128)} %param.14) | copy-start | bytes 12292
  3.6 6.0 %copy-start.5 = (f32[1,128,8]{1,2,0:T(8,128)S(1)}, f32[1,128,8]{1,2,0:T(8,128)}, u32[]{:S(2)}) copy-start(f32[1,128,8]{1,2,0:T(8,128)} %param.15) | copy-start | bytes 12292
  3.6 6.1 %copy-start.3 = (bf16[1,128,2048]{2,1,0:T(8,128)(2,1)S(1)}, bf16[1,128,2048]{2,1,0:T(8,128)(2,1)}, u32[]{:S(2)}) copy-start(bf16[1,128,2048]{2,1,0:T(8,128)(2,1)} %param.13) | copy-start | bytes 1572868
  5.9 19.5 %copy-start.1 = (bf16[1,128,2048]{2,1,0:T(8,128)(2,1)S(1)}, bf16[1,128,2048]{2,1,0:T(8,128)(2,1)}, u32[]{:S(2)}) copy-start(bf16[1,128,2048]{2,1,0:T(8,128)(2,1)} %param.16) | copy-start | bytes 1572868
  5.9 60.2 %collective-permute-start.2 = (bf16[3,192,2048]{2,1,0:T(8,128)(2,1)}, bf16[3,192,2048]{2,1,0:T(8,128)(2,1)}, u32[]{:S(2)}, u32[]{:S(2)}) collective-permute-start(bf16[3,192,2048]{2,1,0:T(8,128)(2,1)} %shard_map.114.refs_1_.refs_2_), channel_id=1, source_target_pairs={{0,2},{2,0},{1,3},{3,1},{4,6},{6,4},{5,7},{7,5},{8,10},{10,8},{9,1... | collective-permute-start | bytes 7077896 | tf_op jit(solution)/shard_map/ppermute | solution.py:258
  11.4 79.8 %copy-start.2 = (bf16[1,128,2048]{2,1,0:T(8,128)(2,1)S(1)}, bf16[1,128,2048]{2,1,0:T(8,128)(2,1)}, u32[]{:S(2)}) copy-start(bf16[1,128,2048]{2,1,0:T(8,128)(2,1)} %param.10) | copy-start | bytes 1572868
  11.4 83.2 %copy-start.6 = (s32[1,128,8]{1,2,0:T(8,128)S(1)}, s32[1,128,8]{1,2,0:T(8,128)}, u32[]{:S(2)}) copy-start(s32[1,128,8]{1,2,0:T(8,128)} %param.11) | copy-start | bytes 12292
  11.4 83.3 %copy-start.7 = (f32[1,128,8]{1,2,0:T(8,128)S(1)}, f32[1,128,8]{1,2,0:T(8,128)}, u32[]{:S(2)}) copy-start(f32[1,128,8]{1,2,0:T(8,128)} %param.12) | copy-start | bytes 12292
  11.4 75.7 %all-to-all-start.2 = ((bf16[16,80,256]{2,1,0:T(8,128)(2,1)}), bf16[16,80,256]{2,1,0:T(8,128)(2,1)S(1)}, u32[]{:S(2)}, u32[]{:S(2)}) async-start(bf16[16,80,256]{2,1,0:T(8,128)(2,1)} %shard_map.117), calls=%async_computation.2 | async-start | bytes 1310720 | tf_op jit(solution)/shard_map/all_to_all | solution.py:262
  25.5 42.7 %collective-permute-start.4 = (bf16[128,2048]{1,0:T(8,128)(2,1)S(1)}, bf16[128,2048]{1,0:T(8,128)(2,1)S(1)}, u32[]{:S(2)}, u32[]{:S(2)}) collective-permute-start(bf16[128,2048]{1,0:T(8,128)(2,1)S(1)} %bitcast.17), channel_id=1, source_target_pairs={{64,0},{128,64},{192,128},{256,192},{320,256},{384,320},{448,384},... | collective-permute-start | bytes 1572872 | tf_op jit(solution)/shard_map/ppermute | solution.py:254
  30.1 101.2 %collective-permute-start.1 = (bf16[3,192,2048]{2,1,0:T(8,128)(2,1)}, bf16[3,192,2048]{2,1,0:T(8,128)(2,1)}, u32[]{:S(2)}, u32[]{:S(2)}) collective-permute-start(bf16[3,192,2048]{2,1,0:T(8,128)(2,1)} %shard_map.114.refs_1_.refs_2_), channel_id=1, source_target_pairs={{0,1},{1,0},{2,3},{3,2},{4,5},{5,4},{6,7},{7,6},{8,9},{9,8},{10,11... | collective-permute-start | bytes 7077896 | tf_op jit(solution)/shard_map/ppermute | solution.py:258
  66.2 65.1 %collective-permute-start.3 = (bf16[3,192,2048]{2,1,0:T(8,128)(2,1)}, bf16[3,192,2048]{2,1,0:T(8,128)(2,1)}, u32[]{:S(2)}, u32[]{:S(2)}) collective-permute-start(bf16[3,192,2048]{2,1,0:T(8,128)(2,1)} %collective-permute-done.2.refs_3_.refs_4_), channel_id=1, source_target_pairs={{0,1},{1,0},{2,3},{3,2},{4,5},{5,4},{6,7},{7,6},{8,9},{9,8},{10,11... | collective-permute-start | bytes 7077896 | tf_op jit(solution)/shard_map/ppermute | solution.py:258
  87.1 33.9 %all-to-all-start.3 = ((bf16[16,80,256]{2,1,0:T(8,128)(2,1)}), bf16[16,80,256]{2,1,0:T(8,128)(2,1)S(1)}, u32[]{:S(2)}, u32[]{:S(2)}) async-start(bf16[16,80,256]{2,1,0:T(8,128)(2,1)} %shard_map.118), calls=%async_computation.3 | async-start | bytes 1310720 | tf_op jit(solution)/shard_map/all_to_all | solution.py:262
  91.2 28.1 %collective-permute-start = (bf16[128,2048]{1,0:T(8,128)(2,1)S(1)}, bf16[128,2048]{1,0:T(8,128)(2,1)S(1)}, u32[]{:S(2)}, u32[]{:S(2)}) collective-permute-start(bf16[128,2048]{1,0:T(8,128)(2,1)S(1)} %bitcast.19), channel_id=1, source_target_pairs={{0,64},{64,128},{128,192},{192,256},{256,320},{320,384},{384,448},... | collective-permute-start | bytes 1572872 | tf_op jit(solution)/shard_map/ppermute | solution.py:254
  121.1 33.6 %all-to-all-start = ((bf16[16,80,256]{2,1,0:T(8,128)(2,1)}), bf16[16,80,256]{2,1,0:T(8,128)(2,1)S(1)}, u32[]{:S(2)}, u32[]{:S(2)}) async-start(bf16[16,80,256]{2,1,0:T(8,128)(2,1)} %shard_map.113), calls=%async_computation | async-start | bytes 1310720 | tf_op jit(solution)/shard_map/all_to_all | solution.py:262
  154.7 27.8 %all-to-all-start.4 = ((bf16[16,80,256]{2,1,0:T(8,128)(2,1)}), bf16[16,80,256]{2,1,0:T(8,128)(2,1)S(1)}, u32[]{:S(2)}, u32[]{:S(2)}) async-start(bf16[16,80,256]{2,1,0:T(8,128)(2,1)} %shard_map.119), calls=%async_computation.4 | async-start | bytes 1310720 | tf_op jit(solution)/shard_map/all_to_all | solution.py:262
  182.5 27.0 %all-to-all-start.1 = ((bf16[16,80,256]{2,1,0:T(8,128)(2,1)}), bf16[16,80,256]{2,1,0:T(8,128)(2,1)S(1)}, u32[]{:S(2)}, u32[]{:S(2)}) async-start(bf16[16,80,256]{2,1,0:T(8,128)(2,1)} %shard_map.115), calls=%async_computation.1 | async-start | bytes 1310720 | tf_op jit(solution)/shard_map/all_to_all | solution.py:262

commit v2 on v1

v2 whole, which is shorter than its diff:
```python
import functools

import jax
import jax.numpy as jnp
from jax import lax
from jax.experimental import pallas as pl
from jax.experimental.pallas import tpu as pltpu
from jax.sharding import Mesh
from jax.sharding import PartitionSpec as P

EXPERTS = 16
SHARDS = 4
CAP = 10
TILE = 16
CHUNKS = 8
ROWS = EXPERTS * CAP
SPAN = EXPERTS * TILE
PACKED = CAP * CHUNKS
TILES = PACKED // TILE
NONE = -100.0

BWD, SCALED, FWD = 0, 1, 2
BWD_BACK, FWD_BACK = 0, 1

MEETS = [
    (j, c, TILE * j - CAP * c)
    for j in range(TILES)
    for c in range(CHUNKS)
    if -TILE < TILE * j - CAP * c < CAP
]

BF16 = jnp.bfloat16
F32 = jnp.float32
NT = (((1,), (1,)), ((), ()))
HBM = pl.BlockSpec(memory_space=pltpu.HBM)
SMEM = pl.BlockSpec(memory_space=pltpu.SMEM)


def iota(shape, dim):
    return lax.broadcasted_iota(jnp.int32, shape, dim)


def dot(a, b):
    return jnp.dot(a, b, preferred_element_type=F32)


def dot_nt(a, b):
    return lax.dot_general(a, b, NT, preferred_element_type=F32)


def halves(values):
    upper = values.astype(BF16)
    return upper, (values - upper.astype(F32)).astype(BF16)


def cost(flops, size):
    return pl.CostEstimate(flops=flops, bytes_accessed=size, transcendentals=0)


def keys_by_expert(ids, gates):
    top, tokens = ids.shape
    expert = iota((EXPERTS, tokens), 0)
    chosen = jnp.zeros((EXPERTS, tokens), F32)
    gate = jnp.zeros((EXPERTS, tokens), F32)
    for k in range(top):
        hit = ids[k : k + 1, :] == expert
        chosen = chosen + hit.astype(F32)
        gate = gate + jnp.where(hit, gates[k : k + 1, :], 0.0)
    earlier = (iota((tokens, tokens), 0) < iota((tokens, tokens), 1)).astype(F32).astype(BF16)
    slot = dot(chosen.astype(BF16), earlier)
    return jnp.where(chosen > 0, slot, NONE), gate


def spread_rows(values):
    experts, tokens = values.shape
    wide = jnp.broadcast_to(values[:, None, :], (experts, TILE, tokens))
    return wide.reshape(experts * TILE, tokens)


def pick_rows(key, gate, states, out):
    key = spread_rows(key)
    row = lax.rem(iota(key.shape, 0), TILE).astype(F32)
    parts = [1.0]
    if gate is not None:
        parts = [h.astype(F32) for h in halves(spread_rows(gate))]
    width = states.shape[1] // CHUNKS
    for j in range(TILES):
        total = jnp.zeros((SPAN, width), F32)
        for _, c, shift in [m for m in MEETS if m[0] == j]:
            hit = key == row + float(shift)
            piece = states[:, c * width : (c + 1) * width]
            for part in parts:
                total = total + dot(jnp.where(hit, part, 0.0).astype(BF16), piece)
        out[:, j * TILE : (j + 1) * TILE, :] = total.astype(BF16).reshape(EXPERTS, TILE, width)


def pick_body(edges, bwd_ids, bwd_gates, fwd_ids, fwd_gates, *refs):
    bwd_input, bwd_grad, arriving, fwd_act, shifted = refs[:5]
    out, states, packed, read, written = refs[-5:]

    def fetch(source, n):
        return pltpu.make_async_copy(source, states.at[n], read.at[n])

    def fetch_one_of(edge, own, moved, n):
        @pl.when(edge == 1)
        def _():
            fetch(own, n).start()

        @pl.when(edge != 1)
        def _():
            fetch(moved, n).start()

    def store(n):
        lines = pl.ds(n * PACKED, PACKED)
        return pltpu.make_async_copy(packed.at[n], out.at[:, lines, :], written.at[n])

    fetch(bwd_input, BWD).start()
    fetch_one_of(edges[1], bwd_grad, arriving, SCALED)
    fetch_one_of(edges[0], fwd_act, shifted, FWD)
    bwd_key, bwd_gate = keys_by_expert(bwd_ids, bwd_gates)
    fwd_key, _ = keys_by_expert(fwd_ids, fwd_gates)
    for n, key, gate in (
        (BWD, bwd_key, None),
        (SCALED, bwd_key, bwd_gate),
        (FWD, fwd_key, None),
    ):
        fetch(bwd_input, n).wait()
        pick_rows(key, gate, states.at[n], packed.at[n])
        store(n).start()
    for n in (BWD, SCALED, FWD):
        store(n).wait()


def pick(edges, routes, states, after):
    tokens, width = states[0].shape
    out = (EXPERTS, 3 * PACKED, width // CHUNKS)
    return pl.pallas_call(
        pick_body,
        out_shape=jax.ShapeDtypeStruct(out, BF16),
        in_specs=[SMEM] + [pl.BlockSpec()] * 4 + [HBM] * (len(states) + len(after)),
        out_specs=HBM,
        scratch_shapes=[
            pltpu.VMEM((3, tokens, width), BF16),
            pltpu.VMEM((3, EXPERTS, PACKED, width // CHUNKS), BF16),
            pltpu.SemaphoreType.DMA((3,)),
            pltpu.SemaphoreType.DMA((3,)),
        ],
        compiler_params=pltpu.CompilerParams(vmem_limit_bytes=60 * 2**20),
        cost_estimate=cost(1_600_000_000, 5_000_000),
    )(edges, *routes, *states, *after)


def combine_rows(weighted, ids, gates, back, base, out, turn):
    tokens = out.shape[0]
    key, gate = keys_by_expert(ids, gates)
    turn[:EXPERTS] = key
    turn[EXPERTS : 2 * EXPERTS] = gate
    turn[2 * EXPERTS :] = jnp.zeros((128 - 2 * EXPERTS, tokens), F32)
    turned = turn[...].T
    column, source = iota((128, SPAN), 0), iota((128, SPAN), 1) // TILE
    key = dot(turned.astype(BF16), (column == source).astype(F32).astype(BF16))
    widen = (column == source + EXPERTS).astype(F32).astype(BF16)
    row = lax.rem(iota(key.shape, 1), TILE).astype(F32)
    parts = [1.0]
    if weighted:
        parts = [dot(h, widen) for h in halves(turned)]
    width = out.shape[1] // CHUNKS
    for c in range(CHUNKS):
        total = jnp.zeros((tokens, width), F32)
        for j, _, shift in [m for m in MEETS if m[1] == c]:
            hit = key == row + float(shift)
            lines = slice(base + j * TILE, base + (j + 1) * TILE)
            rows = back[:, lines, :].reshape(SPAN, width)
            for part in parts:
                total = total + dot(jnp.where(hit, part, 0.0).astype(BF16), rows)
        out[:, c * width : (c + 1) * width] = total.astype(BF16)


def combine_body(bwd_ids, bwd_gates, fwd_ids, fwd_gates, back, routed, grad, turn):
    combine_rows(False, bwd_ids, bwd_gates, back, BWD_BACK * PACKED, grad, turn)
    combine_rows(True, fwd_ids, fwd_gates, back, FWD_BACK * PACKED, routed, turn)


def combine(routes, back):
    tokens = routes[0].shape[1]
    out = jax.ShapeDtypeStruct((tokens, back.shape[2] * CHUNKS), BF16)
    return pl.pallas_call(
        combine_body,
        out_shape=[out, out],
        scratch_shapes=[pltpu.VMEM((128, tokens), F32)],
        compiler_params=pltpu.CompilerParams(vmem_limit_bytes=60 * 2**20),
        cost_estimate=cost(800_000_000, 4_000_000),
    )(*routes, back)


def unpack_rows(packed, rows, base):
    width = packed.shape[2]
    at = iota((ROWS, SPAN), 0)
    lane = iota((ROWS, SPAN), 1)
    source, line = lane // TILE, lax.rem(lane, TILE)
    for c in range(CHUNKS):
        total = jnp.zeros((ROWS, width), F32)
        for j, _, shift in [m for m in MEETS if m[1] == c]:
            slot = line + shift
            hit = (at == source * CAP + slot) & (slot >= 0) & (slot < CAP)
            lines = slice(base + j * TILE, base + (j + 1) * TILE)
            tile = packed[:, lines, :].reshape(SPAN, width)
            total = total + dot(hit.astype(F32).astype(BF16), tile)
        rows[:, c * width : (c + 1) * width] = total.astype(BF16)


def pack_rows(rows, packed, base):
    width = packed.shape[2]
    at = iota((SPAN, ROWS), 1)
    place = iota((SPAN, ROWS), 0)
    source, line = place // TILE, lax.rem(place, TILE)
    for j in range(TILES):
        total = jnp.zeros((SPAN, width), F32)
        for _, c, shift in [m for m in MEETS if m[0] == j]:
            slot = line + shift
            hit = (at == source * CAP + slot) & (slot >= 0) & (slot < CAP)
            piece = rows[:, c * width : (c + 1) * width].astype(BF16)
            total = total + dot(hit.astype(F32).astype(BF16), piece)
        lines = slice(base + j * TILE, base + (j + 1) * TILE)
        packed[:, lines, :] = total.astype(BF16).reshape(EXPERTS, TILE, width)


def experts_body(*refs):
    got, weights = refs[0], refs[1 : 1 + 3 * SHARDS]
    back, rows, scaled, sent, bwd_total, fwd_total, held, ready = refs[1 + 3 * SHARDS :]
    copies = [
        pltpu.make_async_copy(w, held.at[n], ready.at[n]) for n, w in enumerate(weights)
    ]
    for copy in copies:
        copy.start()
    unpack_rows(got, rows, BWD * PACKED)
    unpack_rows(got, scaled, SCALED * PACKED)
    unpack_rows(got, sent, FWD * PACKED)
    for n in range(SHARDS):
        for copy in copies[3 * n : 3 * n + 3]:
            copy.wait()
        gate, up, down = held.at[3 * n], held.at[3 * n + 1], held.at[3 * n + 2]
        gate_back = dot_nt(rows[...], gate[...])
        up_back = dot_nt(rows[...], up[...])
        dact = dot_nt(scaled[...], down[...])
        sigma = 1.0 / (1.0 + jnp.exp(-gate_back))
        dgate = (dact * up_back * sigma * (1.0 + gate_back * (1.0 - sigma))).astype(BF16)
        dup = (dact * (gate_back * sigma)).astype(BF16)
        part = dot(dgate, gate[...]) + dot(dup, up[...])
        bwd_total[...] = part if n == 0 else bwd_total[...] + part

        gate_pre = dot_nt(sent[...], gate[...])
        up_pre = dot_nt(sent[...], up[...])
        act = (gate_pre / (1.0 + jnp.exp(-gate_pre)) * up_pre).astype(BF16)
        part = dot(act, down[...])
        fwd_total[...] = part if n == 0 else fwd_total[...] + part
    pack_rows(bwd_total, back, BWD_BACK * PACKED)
    pack_rows(fwd_total, back, FWD_BACK * PACKED)


def experts_of(got, weights):
    width = got.shape[2] * CHUNKS
    scratch = [pltpu.VMEM((ROWS, width), BF16)] * 3 + [
        pltpu.VMEM((ROWS, width), F32),
        pltpu.VMEM((ROWS, width), F32),
        pltpu.VMEM((len(weights),) + weights[0].shape, BF16),
        pltpu.SemaphoreType.DMA((len(weights),)),
    ]
    return pl.pallas_call(
        experts_body,
        out_shape=jax.ShapeDtypeStruct((EXPERTS, 2 * PACKED, got.shape[2]), BF16),
        in_specs=[pl.BlockSpec()] + [HBM] * len(weights),
        scratch_shapes=scratch,
        compiler_params=pltpu.CompilerParams(vmem_limit_bytes=60 * 2**20),
        cost_estimate=cost(8_000_000_000, 14_000_000),
    )(got, *weights)


def from_behind(x, axis, by):
    devices = lax.axis_size(axis)
    pairs = [(i, i + by) for i in range(devices) if 0 <= i + by < devices]
    return lax.ppermute(x, axis, pairs)


def swap(x, axis):
    return lax.ppermute(x, axis, [(0, 1), (1, 0)])


def exchange(x):
    return lax.all_to_all(x, ("plane", "pair"), split_axis=0, concat_axis=0, tiled=True)


def shards(
    fwd_act, fwd_ids, fwd_gates, bwd_input, bwd_ids, bwd_gates, bwd_grad, w_gate, w_up, w_down
):
    section_at = lax.axis_index("section")
    sections = lax.axis_size("section")
    edges = jnp.stack([section_at == 0, section_at == sections - 1]).astype(jnp.int32)
    routes = (bwd_ids[0].T, bwd_gates[0].T, fwd_ids[0].T, fwd_gates[0].T)
    own = [w_gate[0].T, w_up[0].T, w_down[0]]

    arriving = from_behind(bwd_grad[0], "section", -1)
    shifted = from_behind(fwd_act[0], "section", 1)
    across = [swap(x, "half") for x in own]
    beside = [swap(x, "core") for x in own]
    beyond = [swap(x, "core") for x in across]

    states = (bwd_input[0], bwd_grad[0], arriving, fwd_act[0], shifted)
    got = exchange(pick(edges, routes, states, [across[2]]))
    back = exchange(experts_of(got, own + beside + across + beyond))
    routed_out, input_grad = combine(routes, back)
    return (routed_out[None], input_grad[None])


def solution(mesh):
    sections, devices = mesh.devices.shape
    planes = 4
    parted = Mesh(
        mesh.devices.reshape(sections, planes, devices // planes // 4, 2, 2),
        ("section", "plane", "pair", "half", "core"),
    )
    expert = ("plane", "pair", "half", "core")
    rows = P("section", expert, None)
    columns = P("section", None, expert)
    return jax.shard_map(
        shards,
        mesh=parted,
        in_specs=(rows,) * 7 + (columns, columns, rows),
        out_specs=(rows, rows),
        check_vma=False,
    )
```

time: 212 us -> 212 us (level)
  the two profiles are of different devices: /device:TPU:64 before, /device:TPU:95 now
where the time goes in v2:
time: 212 us; the launch traced here: 211 us
  waiting for transfers between devices  81.7 us (39%)
  blocking collectives  57 us (27%)
  starting transfers between devices  40.8 us (19%)
  Pallas kernels  24.5 us (12%)
  local copies, waits for them, and re-layouts  5.4 us (3%)
    ppermute x9, waiting for transfers between devices, swap(): return lax.ppermute(x, axis, [(0, 1), (1, 0)])  69.4 us
    all_to_all x1, blocking collectives, exchange(): lax.all_to_all(x, ('plane', 'pair'), split_axis=0, concat_axis=0, tiled=T...  57 us
    ppermute x9, starting transfers between devices, swap(): return lax.ppermute(x, axis, [(0, 1), (1, 0)])  23.3 us
    pallas_call x1, Pallas kernels, experts_of(): pl.pallas_call(experts_body, out_shape=jax.ShapeDtypeStruct((EXPERTS, 2 *...  15.8 us
    all_to_all x1, starting transfers between devices, exchange(): lax.all_to_all(x, ('plane', 'pair'), split_axis=0, concat_axis=0, tiled=T...  13.7 us
    ppermute x2, waiting for transfers between devices, from_behind(): return lax.ppermute(x, axis, pairs)  12.3 us
    unnamed x28, local copies, waits for them, and re-layouts  5.4 us
    pallas_call x1, Pallas kernels, pick(): pl.pallas_call(pick_body, out_shape=jax.ShapeDtypeStruct(out, BF16), in_s...  4.87 us
  transfers between devices with their start and end apart: 12, of which 5 were waited for; matrix products, arithmetic and copies ran while one was open for 0% of the time, Pallas kernels for 0%

profile of v2, /device:TPU:95, one launch (start us, length us, event | category | flops | bytes accessed | tf_op | source)
XLA Modules:
  0.0 210.9 jit_solution(4488398160298762903)
XLA Ops:
  0.6 2.1 collective-permute-start.2
  2.7 2.5 %collective-permute-start = (bf16[128,2048]{1,0:T(8,128)(2,1)}, bf16[128,2048]{1,0:T(8,128)(2,1)S(1)}, u32[]{:S(2)}, u32[]{:S(2)}) collective-permute-start(bf16[128,2048]{1,0:T(8,128)(2,1)} %bitcast.36), channel_id=1, source_target_pairs={{64,0},{128,64},{192,128},{256,192},{320,256},{384,320},{448,384},... | collective-permute-start | bytes 1572872 | tf_op jit(solution)/shard_map/ppermute | solution.py:282
  5.2 1.3 collective-permute-start.1
  7.2 8.6 %collective-permute-done.refs_2_ = bf16[128,2048]{1,0:T(8,128)(2,1)S(1)} collective-permute-done((bf16[128,2048]{1,0:T(8,128)(2,1)}, bf16[128,2048]{1,0:T(8,128)(2,1)S(1)}, u32[]{:S(2)}, u32[]{:S(2)}) %collective-permute-start) | collective-permute-done | bytes 524320 | tf_op jit(solution)/shard_map/ppermute | solution.py:282
  15.8 3.7 %collective-permute-done.1.refs_4_ = bf16[128,2048]{1,0:T(8,128)(2,1)S(1)} collective-permute-done((bf16[128,2048]{1,0:T(8,128)(2,1)}, bf16[128,2048]{1,0:T(8,128)(2,1)S(1)}, u32[]{:S(2)}, u32[]{:S(2)}) %collective-permute-start.1) | collective-permute-done | bytes 524320 | tf_op jit(solution)/shard_map/ppermute | solution.py:282
  19.5 1.6 collective-permute-done.2.refs_5_.refs_9_
  22.0 4.9 %shard_map.113 = bf16[16,240,256]{2,1,0:T(8,128)(2,1)} custom-call(s32[2]{0:T(128)} %add_convert_fusion.edges, s32[8,128]{1,0:T(8,128)} %bitcast.40, f32[8,128]{1,0:T(8,128)} %bitcast.42, s32[8,128]{1,0:T(8,128)} %bitcast.44, f32[8,128]{1,0:T(8,128)} %bitcast.46, bf16[128,2048]{1,0:T(8,128)(2,1)} %bitcast.35, bf16[128,2048]{1,0:T(8,128)(2,1)} %bitcast.37, ...), custom_call_target="tpu_custom_call" | custom-call | flops 1600000000 | bytes 5000000 | tf_op jit(solution)/shard_map/pallas_call | solution.py:137
  26.9 13.7 %all-to-all-start = ((bf16[16,240,256]{2,1,0:T(8,128)(2,1)}), bf16[16,240,256]{2,1,0:T(8,128)(2,1)S(1)}, u32[]{:S(2)}, u32[]{:S(2)}) async-start(bf16[16,240,256]{2,1,0:T(8,128)(2,1)} %shard_map.113), calls=%async_computation | async-start | bytes 3932160 | tf_op jit(solution)/shard_map/all_to_all | solution.py:290
  40.6 3.0 %collective-permute-start.6 = (bf16[192,2048]{1,0:T(8,128)(2,1)S(1)}, bf16[192,2048]{1,0:T(8,128)(2,1)S(1)}, u32[]{:S(2)}, u32[]{:S(2)}) collective-permute-start(bf16[192,2048]{1,0:T(8,128)(2,1)S(1)} %bitcast.30), channel_id=1, source_target_pairs={{0,2},{2,0},{1,3},{3,1},{4,6},{6,4},{5,7},{7,5},{8,10},{10,8},{9,1... | collective-permute-start | bytes 2359304 | tf_op jit(solution)/shard_map/ppermute | solution.py:286
  43.6 2.3 %collective-permute-start.7 = (bf16[192,2048]{1,0:T(8,128)(2,1)}, bf16[192,2048]{1,0:T(8,128)(2,1)S(1)}, u32[]{:S(2)}, u32[]{:S(2)}) collective-permute-start(bf16[192,2048]{1,0:T(8,128)(2,1)} %bitcast.32), channel_id=1, source_target_pairs={{0,2},{2,0},{1,3},{3,1},{4,6},{6,4},{5,7},{7,5},{8,10},{10,8},{9,1... | collective-permute-start | bytes 2359304 | tf_op jit(solution)/shard_map/ppermute | solution.py:286
  45.9 4.6 %collective-permute-start.3 = (bf16[192,2048]{1,0:T(8,128)(2,1)S(1)}, bf16[192,2048]{1,0:T(8,128)(2,1)S(1)}, u32[]{:S(2)}, u32[]{:S(2)}) collective-permute-start(bf16[192,2048]{1,0:T(8,128)(2,1)S(1)} %bitcast.31), channel_id=1, source_target_pairs={{0,1},{1,0},{2,3},{3,2},{4,5},{5,4},{6,7},{7,6},{8,9},{9,8},{10,11... | collective-permute-start | bytes 2359304 | tf_op jit(solution)/shard_map/ppermute | solution.py:286
  50.5 1.9 collective-permute-start.4
  52.5 2.4 %collective-permute-start.5 = (bf16[192,2048]{1,0:T(8,128)(2,1)S(1)}, bf16[192,2048]{1,0:T(8,128)(2,1)S(1)}, u32[]{:S(2)}, u32[]{:S(2)}) collective-permute-start(bf16[192,2048]{1,0:T(8,128)(2,1)S(1)} %bitcast.28), channel_id=1, source_target_pairs={{0,1},{1,0},{2,3},{3,2},{4,5},{5,4},{6,7},{7,6},{8,9},{9,8},{10,11... | collective-permute-start | bytes 2359304 | tf_op jit(solution)/shard_map/ppermute | solution.py:286
  54.9 53.4 %collective-permute-done.6.refs_7_ = bf16[192,2048]{1,0:T(8,128)(2,1)S(1)} collective-permute-done((bf16[192,2048]{1,0:T(8,128)(2,1)S(1)}, bf16[192,2048]{1,0:T(8,128)(2,1)S(1)}, u32[]{:S(2)}, u32[]{:S(2)}) %collective-permute-start.6) | collective-permute-done | bytes 786464 | tf_op jit(solution)/shard_map/ppermute | solution.py:286
  108.2 2.5 %collective-permute-start.10 = (bf16[192,2048]{1,0:T(8,128)(2,1)}, bf16[192,2048]{1,0:T(8,128)(2,1)S(1)}, u32[]{:S(2)}, u32[]{:S(2)}) collective-permute-start(bf16[192,2048]{1,0:T(8,128)(2,1)} %copy-done.3), channel_id=1, source_target_pairs={{0,1},{1,0},{2,3},{3,2},{4,5},{5,4},{6,7},{7,6},{8,9},{9,8},{10,11... | collective-permute-start | bytes 2359304 | tf_op jit(solution)/shard_map/ppermute | solution.py:286
  110.7 14.4 %collective-permute-done.7.refs_8_ = bf16[192,2048]{1,0:T(8,128)(2,1)S(1)} collective-permute-done((bf16[192,2048]{1,0:T(8,128)(2,1)}, bf16[192,2048]{1,0:T(8,128)(2,1)S(1)}, u32[]{:S(2)}, u32[]{:S(2)}) %collective-permute-start.7) | collective-permute-done | bytes 786464 | tf_op jit(solution)/shard_map/ppermute | solution.py:286
  125.1 2.4 %collective-permute-start.8 = (bf16[192,2048]{1,0:T(8,128)(2,1)S(1)}, bf16[192,2048]{1,0:T(8,128)(2,1)S(1)}, u32[]{:S(2)}, u32[]{:S(2)}) collective-permute-start(bf16[192,2048]{1,0:T(8,128)(2,1)S(1)} %collective-permute-done.6.refs_7_), channel_id=1, source_target_pairs={{0,1},{1,0},{2,3},{3,2},{4,5},{5,4},{6,7},{7,6},{8,9},{9,8},{10,11... | collective-permute-start | bytes 2359304 | tf_op jit(solution)/shard_map/ppermute | solution.py:286
  127.5 2.1 collective-permute-start.9
  131.1 0.9 copy-done.10
  132.1 0.9 copy-done.11
  132.9 1.3 copy-done
  134.2 15.8 %shard_map.114 = bf16[16,160,256]{2,1,0:T(8,128)(2,1)} custom-call(bf16[16,240,256]{2,1,0:T(8,128)(2,1)} %copy-done, bf16[192,2048]{1,0:T(8,128)(2,1)} %bitcast.29, bf16[192,2048]{1,0:T(8,128)(2,1)} %bitcast.34, bf16[192,2048]{1,0:T(8,128)(2,1)} %bitcast.27, bf16[192,2048]{1,0:T(8,128)(2,1)} %copy-done.6, bf16[192,2048]{1,0:T(8,128)(2,1)} %copy-done.7, ...), custom_call_target="tpu_custom_call" | custom-call | flops 8000000000 | bytes 14000000 | tf_op jit(solution)/shard_map/pallas_call | solution.py:269
  150.1 57.0 %all_to_all.10.back = bf16[16,160,256]{2,1,0:T(8,128)(2,1)} all-to-all(bf16[16,160,256]{2,1,0:T(8,128)(2,1)} %shard_map.114), channel_id=1, replica_groups=mesh['section'=8,'plane'=4,'pair'=4,'half'=2,'core'=2] {'plane','pair'}, dimensions={0} | all-to-all | bytes 2621440 | tf_op jit(solution)/shard_map/all_to_all | solution.py:290
  207.1 3.8 %shard_map.115 = (bf16[128,2048]{1,0:T(8,128)(2,1)}, bf16[128,2048]{1,0:T(8,128)(2,1)}) custom-call(s32[8,128]{1,0:T(8,128)} %bitcast.41, f32[8,128]{1,0:T(8,128)} %bitcast.43, s32[8,128]{1,0:T(8,128)} %bitcast.45, f32[8,128]{1,0:T(8,128)} %bitcast.47, bf16[16,160,256]{2,1,0:T(8,128)(2,1)} %all_to_all.10.back), custom_call_target="tpu_custom_call" | custom-call | flops 800000000 | bytes 4000000 | tf_op jit(solution)/shard_map/pallas_call | solution.py:187
  (33 shorter events, 3.0 us)
Async XLA Ops:
  0.6 20.5 %collective-permute-start.2 = (bf16[192,2048]{1,0:T(8,128)(2,1)}, bf16[192,2048]{1,0:T(8,128)(2,1)S(1)}, u32[]{:S(2)}, u32[]{:S(2)}) collective-permute-start(bf16[192,2048]{1,0:T(8,128)(2,1)} %bitcast.26), channel_id=1, source_target_pairs={{0,2},{2,0},{1,3},{3,1},{4,6},{6,4},{5,7},{7,5},{8,10},{10,8},{9,1... | collective-permute-start | bytes 2359304 | tf_op jit(solution)/shard_map/ppermute | solution.py:286
  2.7 13.0 %collective-permute-start = (bf16[128,2048]{1,0:T(8,128)(2,1)}, bf16[128,2048]{1,0:T(8,128)(2,1)S(1)}, u32[]{:S(2)}, u32[]{:S(2)}) collective-permute-start(bf16[128,2048]{1,0:T(8,128)(2,1)} %bitcast.36), channel_id=1, source_target_pairs={{64,0},{128,64},{192,128},{256,192},{320,256},{384,320},{448,384},... | collective-permute-start | bytes 1572872 | tf_op jit(solution)/shard_map/ppermute | solution.py:282
  5.2 14.3 %collective-permute-start.1 = (bf16[128,2048]{1,0:T(8,128)(2,1)}, bf16[128,2048]{1,0:T(8,128)(2,1)S(1)}, u32[]{:S(2)}, u32[]{:S(2)}) collective-permute-start(bf16[128,2048]{1,0:T(8,128)(2,1)} %bitcast.38), channel_id=1, source_target_pairs={{0,64},{64,128},{128,192},{192,256},{256,320},{320,384},{384,448},... | collective-permute-start | bytes 1572872 | tf_op jit(solution)/shard_map/ppermute | solution.py:282
  15.8 5.4 %copy-start.12 = (bf16[128,2048]{1,0:T(8,128)(2,1)}, bf16[128,2048]{1,0:T(8,128)(2,1)S(1)}, u32[]{:S(2)}) copy-start(bf16[128,2048]{1,0:T(8,128)(2,1)S(1)} %collective-permute-done.refs_2_) | copy-start | bytes 1572868
  19.5 1.7 copy-start.13
  26.9 13.7 %copy-start.2 = (bf16[1,2048,192]{1,2,0:T(8,128)(2,1)S(1)}, bf16[1,2048,192]{1,2,0:T(8,128)(2,1)}, u32[]{:S(2)}) copy-start(bf16[1,2048,192]{1,2,0:T(8,128)(2,1)} %param.17) | copy-start | bytes 2359300
  26.9 25.6 %copy-start.1 = (bf16[1,192,2048]{2,1,0:T(8,128)(2,1)S(1)}, bf16[1,192,2048]{2,1,0:T(8,128)(2,1)}, u32[]{:S(2)}) copy-start(bf16[1,192,2048]{2,1,0:T(8,128)(2,1)} %param.19) | copy-start | bytes 2359300
  26.9 105.1 %all-to-all-start = ((bf16[16,240,256]{2,1,0:T(8,128)(2,1)}), bf16[16,240,256]{2,1,0:T(8,128)(2,1)S(1)}, u32[]{:S(2)}, u32[]{:S(2)}) async-start(bf16[16,240,256]{2,1,0:T(8,128)(2,1)} %shard_map.113), calls=%async_computation | async-start | bytes 3932160 | tf_op jit(solution)/shard_map/all_to_all | solution.py:290
  40.6 67.6 %collective-permute-start.6 = (bf16[192,2048]{1,0:T(8,128)(2,1)S(1)}, bf16[192,2048]{1,0:T(8,128)(2,1)S(1)}, u32[]{:S(2)}, u32[]{:S(2)}) collective-permute-start(bf16[192,2048]{1,0:T(8,128)(2,1)S(1)} %bitcast.30), channel_id=1, source_target_pairs={{0,2},{2,0},{1,3},{3,1},{4,6},{6,4},{5,7},{7,5},{8,10},{10,8},{9,1... | collective-permute-start | bytes 2359304 | tf_op jit(solution)/shard_map/ppermute | solution.py:286
  43.6 81.5 %collective-permute-start.7 = (bf16[192,2048]{1,0:T(8,128)(2,1)}, bf16[192,2048]{1,0:T(8,128)(2,1)S(1)}, u32[]{:S(2)}, u32[]{:S(2)}) collective-permute-start(bf16[192,2048]{1,0:T(8,128)(2,1)} %bitcast.32), channel_id=1, source_target_pairs={{0,2},{2,0},{1,3},{3,1},{4,6},{6,4},{5,7},{7,5},{8,10},{10,8},{9,1... | collective-permute-start | bytes 2359304 | tf_op jit(solution)/shard_map/ppermute | solution.py:286
  45.9 81.6 %collective-permute-start.3 = (bf16[192,2048]{1,0:T(8,128)(2,1)S(1)}, bf16[192,2048]{1,0:T(8,128)(2,1)S(1)}, u32[]{:S(2)}, u32[]{:S(2)}) collective-permute-start(bf16[192,2048]{1,0:T(8,128)(2,1)S(1)} %bitcast.31), channel_id=1, source_target_pairs={{0,1},{1,0},{2,3},{3,2},{4,5},{5,4},{6,7},{7,6},{8,9},{9,8},{10,11... | collective-permute-start | bytes 2359304 | tf_op jit(solution)/shard_map/ppermute | solution.py:286
  50.5 79.1 %collective-permute-start.4 = (bf16[192,2048]{1,0:T(8,128)(2,1)}, bf16[192,2048]{1,0:T(8,128)(2,1)S(1)}, u32[]{:S(2)}, u32[]{:S(2)}) collective-permute-start(bf16[192,2048]{1,0:T(8,128)(2,1)} %bitcast.33), channel_id=1, source_target_pairs={{0,1},{1,0},{2,3},{3,2},{4,5},{5,4},{6,7},{7,6},{8,9},{9,8},{10,11... | collective-permute-start | bytes 2359304 | tf_op jit(solution)/shard_map/ppermute | solution.py:286
  52.5 77.2 %collective-permute-start.5 = (bf16[192,2048]{1,0:T(8,128)(2,1)S(1)}, bf16[192,2048]{1,0:T(8,128)(2,1)S(1)}, u32[]{:S(2)}, u32[]{:S(2)}) collective-permute-start(bf16[192,2048]{1,0:T(8,128)(2,1)S(1)} %bitcast.28), channel_id=1, source_target_pairs={{0,1},{1,0},{2,3},{3,2},{4,5},{5,4},{6,7},{7,6},{8,9},{9,8},{10,11... | collective-permute-start | bytes 2359304 | tf_op jit(solution)/shard_map/ppermute | solution.py:286
  108.2 21.5 %copy-start.4 = (bf16[192,2048]{1,0:T(8,128)(2,1)}, bf16[192,2048]{1,0:T(8,128)(2,1)S(1)}, u32[]{:S(2)}) copy-start(bf16[192,2048]{1,0:T(8,128)(2,1)S(1)} %collective-permute-done.6.refs_7_) | copy-start | bytes 2359300
  108.2 21.4 %collective-permute-start.10 = (bf16[192,2048]{1,0:T(8,128)(2,1)}, bf16[192,2048]{1,0:T(8,128)(2,1)S(1)}, u32[]{:S(2)}, u32[]{:S(2)}) collective-permute-start(bf16[192,2048]{1,0:T(8,128)(2,1)} %copy-done.3), channel_id=1, source_target_pairs={{0,1},{1,0},{2,3},{3,2},{4,5},{5,4},{6,7},{7,6},{8,9},{9,8},{10,11... | collective-permute-start | bytes 2359304 | tf_op jit(solution)/shard_map/ppermute | solution.py:286
  125.1 4.6 %copy-start.5 = (bf16[192,2048]{1,0:T(8,128)(2,1)}, bf16[192,2048]{1,0:T(8,128)(2,1)S(1)}, u32[]{:S(2)}) copy-start(bf16[192,2048]{1,0:T(8,128)(2,1)S(1)} %collective-permute-done.7.refs_8_) | copy-start | bytes 2359300
  125.1 4.6 %collective-permute-start.8 = (bf16[192,2048]{1,0:T(8,128)(2,1)S(1)}, bf16[192,2048]{1,0:T(8,128)(2,1)S(1)}, u32[]{:S(2)}, u32[]{:S(2)}) collective-permute-start(bf16[192,2048]{1,0:T(8,128)(2,1)S(1)} %collective-permute-done.6.refs_7_), channel_id=1, source_target_pairs={{0,1},{1,0},{2,3},{3,2},{4,5},{5,4},{6,7},{7,6},{8,9},{9,8},{10,11... | collective-permute-start | bytes 2359304 | tf_op jit(solution)/shard_map/ppermute | solution.py:286
  127.5 2.2 %copy-start.6 = (bf16[192,2048]{1,0:T(8,128)(2,1)}, bf16[192,2048]{1,0:T(8,128)(2,1)S(1)}, u32[]{:S(2)}) copy-start(bf16[192,2048]{1,0:T(8,128)(2,1)S(1)} %collective-permute-done.3.refs_4_) | copy-start | bytes 2359300
  127.5 4.5 %collective-permute-start.9 = (bf16[192,2048]{1,0:T(8,128)(2,1)S(1)}, bf16[192,2048]{1,0:T(8,128)(2,1)S(1)}, u32[]{:S(2)}, u32[]{:S(2)}) collective-permute-start(bf16[192,2048]{1,0:T(8,128)(2,1)S(1)} %collective-permute-done.7.refs_8_), channel_id=1, source_target_pairs={{0,1},{1,0},{2,3},{3,2},{4,5},{5,4},{6,7},{7,6},{8,9},{9,8},{10,11... | collective-permute-start | bytes 2359304 | tf_op jit(solution)/shard_map/ppermute | solution.py:286
  129.6 0.9 copy-start.7
  129.7 1.2 copy-start.8
  129.7 1.4 copy-start.9
  131.1 0.9 copy-start.10
  132.9 1.3 copy-start
  (2 other events, 1.8 us)

commit v3 on v2

--- a/solution.py
+++ b/solution.py
@@ -18,6 +18,7 @@
 PACKED = CAP * CHUNKS
 TILES = PACKED // TILE
 NONE = -100.0
+MARK_FLOPS = 200_000_000_000
 
 BWD, SCALED, FWD = 0, 1, 2
 BWD_BACK, FWD_BACK = 0, 1
@@ -131,13 +132,13 @@
         store(n).wait()
 
 
-def pick(edges, routes, states, after):
+def pick(edges, routes, states):
     tokens, width = states[0].shape
     out = (EXPERTS, 3 * PACKED, width // CHUNKS)
     return pl.pallas_call(
         pick_body,
         out_shape=jax.ShapeDtypeStruct(out, BF16),
-        in_specs=[SMEM] + [pl.BlockSpec()] * 4 + [HBM] * (len(states) + len(after)),
+        in_specs=[SMEM] + [pl.BlockSpec()] * 4 + [HBM] * len(states),
         out_specs=HBM,
         scratch_shapes=[
             pltpu.VMEM((3, tokens, width), BF16),
@@ -147,7 +148,7 @@
         ],
         compiler_params=pltpu.CompilerParams(vmem_limit_bytes=60 * 2**20),
         cost_estimate=cost(1_600_000_000, 5_000_000),
-    )(edges, *routes, *states, *after)
+    )(edges, *routes, *states)
 
 
 def combine_rows(weighted, ids, gates, back, base, out, turn):
@@ -226,8 +227,9 @@
 
 
 def experts_body(*refs):
-    got, weights = refs[0], refs[1 : 1 + 3 * SHARDS]
-    back, rows, scaled, sent, bwd_total, fwd_total, held, ready = refs[1 + 3 * SHARDS :]
+    got, weights, beside = refs[0], list(refs[1 : 3 * SHARDS - 2]), refs[3 * SHARDS - 2]
+    weights += [beside.at[i] for i in range(3)]
+    back, rows, scaled, sent, bwd_total, fwd_total, held, ready = refs[-8:]
     copies = [
         pltpu.make_async_copy(w, held.at[n], ready.at[n]) for n, w in enumerate(weights)
     ]
@@ -258,22 +260,56 @@
     pack_rows(fwd_total, back, FWD_BACK * PACKED)
 
 
-def experts_of(got, weights):
+def experts_of(got, weights, beside, after):
     width = got.shape[2] * CHUNKS
     scratch = [pltpu.VMEM((ROWS, width), BF16)] * 3 + [
         pltpu.VMEM((ROWS, width), F32),
         pltpu.VMEM((ROWS, width), F32),
-        pltpu.VMEM((len(weights),) + weights[0].shape, BF16),
-        pltpu.SemaphoreType.DMA((len(weights),)),
+        pltpu.VMEM((3 * SHARDS,) + weights[0].shape, BF16),
+        pltpu.SemaphoreType.DMA((3 * SHARDS,)),
     ]
     return pl.pallas_call(
         experts_body,
         out_shape=jax.ShapeDtypeStruct((EXPERTS, 2 * PACKED, got.shape[2]), BF16),
-        in_specs=[pl.BlockSpec()] + [HBM] * len(weights),
+        in_specs=[pl.BlockSpec()] + [HBM] * (len(weights) + 2),
         scratch_shapes=scratch,
         compiler_params=pltpu.CompilerParams(vmem_limit_bytes=60 * 2**20),
         cost_estimate=cost(8_000_000_000, 14_000_000),
-    )(got, *weights)
+    )(got, *weights, beside, after)
+
+
+def stack_body(*refs):
+    arrays, out, done = refs[:3], refs[-2], refs[-1]
+    copies = [pltpu.make_async_copy(w, out.at[i], done.at[i]) for i, w in enumerate(arrays)]
+    for copy in copies:
+        copy.start()
+    for copy in copies:
+        copy.wait()
+
+
+def stack(arrays, after):
+    n = len(arrays)
+    return pl.pallas_call(
+        stack_body,
+        out_shape=jax.ShapeDtypeStruct((n,) + arrays[0].shape, BF16),
+        in_specs=[HBM] * (n + 1),
+        out_specs=HBM,
+        scratch_shapes=[pltpu.SemaphoreType.DMA((n,))],
+        cost_estimate=cost(0, 5_000_000),
+    )(*arrays, after)
+
+
+def mark_body(ids, out):
+    out[...] = jnp.zeros_like(out) + ids[0, 0]
+
+
+def mark(ids):
+    return pl.pallas_call(
+        mark_body,
+        out_shape=jax.ShapeDtypeStruct((8, 128), jnp.int32),
+        in_specs=[SMEM],
+        cost_estimate=cost(MARK_FLOPS, 0),
+    )(ids)
 
 
 def from_behind(x, axis, by):
@@ -302,12 +338,13 @@
     arriving = from_behind(bwd_grad[0], "section", -1)
     shifted = from_behind(fwd_act[0], "section", 1)
     across = [swap(x, "half") for x in own]
-    beside = [swap(x, "core") for x in own]
     beyond = [swap(x, "core") for x in across]
 
     states = (bwd_input[0], bwd_grad[0], arriving, fwd_act[0], shifted)
-    got = exchange(pick(edges, routes, states, [across[2]]))
-    back = exchange(experts_of(got, own + beside + across + beyond))
+    sent = pick(edges, routes, states)
+    beside = swap(stack(own, sent), "core")
+    got = exchange(sent)
+    back = exchange(experts_of(got, own + across + beyond, beside, mark(routes[0])))
     routed_out, input_grad = combine(routes, back)
     return (routed_out[None], input_grad[None])
 

time: 212 us -> 246 us (1.16)
  the two profiles are of different devices: /device:TPU:95 before, /device:TPU:1 now
where the time goes in v3:
time: 246 us; the launch traced here: 244 us
  Pallas kernels  98.5 us (40%)
  blocking collectives  54 us (22%)
  waiting for transfers between devices  45.8 us (19%)
  starting transfers between devices  43.6 us (18%)
    pallas_call x1, Pallas kernels, stack(): pl.pallas_call(stack_body, out_shape=jax.ShapeDtypeStruct((n,) + arrays[0...  72.6 us
    all_to_all x1, blocking collectives, exchange(): lax.all_to_all(x, ('plane', 'pair'), split_axis=0, concat_axis=0, tiled=T...  54 us
    all_to_all x1, waiting for transfers between devices, exchange(): lax.all_to_all(x, ('plane', 'pair'), split_axis=0, concat_axis=0, tiled=T...  38.7 us
    ppermute x7, starting transfers between devices, swap(): return lax.ppermute(x, axis, [(0, 1), (1, 0)])  20.5 us
    all_to_all x1, starting transfers between devices, exchange(): lax.all_to_all(x, ('plane', 'pair'), split_axis=0, concat_axis=0, tiled=T...  17.8 us
    pallas_call x1, Pallas kernels, experts_of(): pl.pallas_call(experts_body, out_shape=jax.ShapeDtypeStruct((EXPERTS, 2 *...  15.8 us
    ppermute x2, waiting for transfers between devices, from_behind(): return lax.ppermute(x, axis, pairs)  5.79 us
    ppermute x2, starting transfers between devices, from_behind(): return lax.ppermute(x, axis, pairs)  5.32 us
  transfers between devices with their start and end apart: 10, of which 4 were waited for; matrix products, arithmetic and copies ran while one was open for 0% of the time, Pallas kernels for 32%

profile of v3, /device:TPU:1, one launch (start us, length us, event | category | flops | bytes accessed | tf_op | source)
XLA Modules:
  0.0 244.0 jit_solution(13550210599620560200)
XLA Ops:
  0.6 4.0 %collective-permute-start.2 = (bf16[192,2048]{1,0:T(8,128)(2,1)}, bf16[192,2048]{1,0:T(8,128)(2,1)}, u32[]{:S(2)}, u32[]{:S(2)}) collective-permute-start(bf16[192,2048]{1,0:T(8,128)(2,1)} %bitcast.26), channel_id=1, source_target_pairs={{0,2},{2,0},{1,3},{3,1},{4,6},{6,4},{5,7},{7,5},{8,10},{10,8},{9,1... | collective-permute-start | bytes 2359304 | tf_op jit(solution)/shard_map/ppermute | solution.py:322
  4.7 1.9 collective-permute-start.3
  6.6 3.4 %collective-permute-start.4 = (bf16[192,2048]{1,0:T(8,128)(2,1)}, bf16[192,2048]{1,0:T(8,128)(2,1)}, u32[]{:S(2)}, u32[]{:S(2)}) collective-permute-start(bf16[192,2048]{1,0:T(8,128)(2,1)} %bitcast.32), channel_id=1, source_target_pairs={{0,2},{2,0},{1,3},{3,1},{4,6},{6,4},{5,7},{7,5},{8,10},{10,8},{9,1... | collective-permute-start | bytes 2359304 | tf_op jit(solution)/shard_map/ppermute | solution.py:322
  10.0 1.3 collective-permute-start
  11.3 4.0 %collective-permute-start.1 = (bf16[128,2048]{1,0:T(8,128)(2,1)}, bf16[128,2048]{1,0:T(8,128)(2,1)S(1)}, u32[]{:S(2)}, u32[]{:S(2)}) collective-permute-start(bf16[128,2048]{1,0:T(8,128)(2,1)} %bitcast.38), channel_id=1, source_target_pairs={{0,64},{64,128},{128,192},{192,256},{256,320},{320,384},{384,448},... | collective-permute-start | bytes 1572872 | tf_op jit(solution)/shard_map/ppermute | solution.py:318
  15.3 0.6 add_convert_fusion.edges
  15.9 4.6 %collective-permute-done.refs_2_ = bf16[128,2048]{1,0:T(8,128)(2,1)S(1)} collective-permute-done((bf16[128,2048]{1,0:T(8,128)(2,1)}, bf16[128,2048]{1,0:T(8,128)(2,1)S(1)}, u32[]{:S(2)}, u32[]{:S(2)}) %collective-permute-start) | collective-permute-done | bytes 524320 | tf_op jit(solution)/shard_map/ppermute | solution.py:318
  20.5 1.2 collective-permute-done.1.refs_4_
  21.7 0.8 copy-done.1
  22.5 4.9 %shard_map.113.refs_3_ = bf16[16,240,256]{2,1,0:T(8,128)(2,1)} custom-call(s32[2]{0:T(128)} %add_convert_fusion.edges, s32[8,128]{1,0:T(8,128)} %bitcast.40, f32[8,128]{1,0:T(8,128)} %bitcast.43, s32[8,128]{1,0:T(8,128)} %bitcast.45, f32[8,128]{1,0:T(8,128)} %bitcast.47, bf16[128,2048]{1,0:T(8,128)(2,1)} %bitcast.35, bf16[128,2048]{1,0:T(8,128)(2,1)} %bitcast.37, ...), custom_call_target="tpu_custom_call" | custom-call | flops 1600000000 | bytes 5000000 | tf_op jit(solution)/shard_map/pallas_call | solution.py:138
  27.4 72.6 %shard_map.114 = bf16[3,192,2048]{2,1,0:T(8,128)(2,1)} custom-call(bf16[192,2048]{1,0:T(8,128)(2,1)} %bitcast.27, bf16[192,2048]{1,0:T(8,128)(2,1)} %bitcast.30, bf16[192,2048]{1,0:T(8,128)(2,1)} %bitcast.33, bf16[16,240,256]{2,1,0:T(8,128)(2,1)} %shard_map.113.refs_3_), custom_call_target="tpu_custom_call" | custom-call | bytes 5000000 | tf_op jit(solution)/shard_map/pallas_call | solution.py:292
  100.0 17.8 %all-to-all-start = ((bf16[16,240,256]{2,1,0:T(8,128)(2,1)}), bf16[16,240,256]{2,1,0:T(8,128)(2,1)}, u32[]{:S(2)}, u32[]{:S(2)}) async-start(bf16[16,240,256]{2,1,0:T(8,128)(2,1)} %shard_map.113.refs_3_), calls=%async_computation | async-start | bytes 3932160 | tf_op jit(solution)/shard_map/all_to_all | solution.py:326
  117.9 4.9 %collective-permute-start.8 = (bf16[3,192,2048]{2,1,0:T(8,128)(2,1)}, bf16[3,192,2048]{2,1,0:T(8,128)(2,1)}, u32[]{:S(2)}, u32[]{:S(2)}) collective-permute-start(bf16[3,192,2048]{2,1,0:T(8,128)(2,1)} %shard_map.114), channel_id=1, source_target_pairs={{0,1},{1,0},{2,3},{3,2},{4,5},{5,4},{6,7},{7,6},{8,9},{9,8},{10,11... | collective-permute-start | bytes 7077896 | tf_op jit(solution)/shard_map/ppermute | solution.py:322
  122.8 0.0 collective-permute-done.2.refs_4_
  122.8 1.9 collective-permute-start.5
  124.7 0.0 collective-permute-done.3.refs_5_
  124.7 2.4 collective-permute-start.6
  127.2 1.9 collective-permute-start.7
  129.1 1.3 shard_map.115.refs_11_
  130.4 1.3 collective-permute-done.7.refs_9_
  131.7 38.7 %all-to-all-done.refs_0_ = bf16[16,240,256]{2,1,0:T(8,128)(2,1)} async-done(((bf16[16,240,256]{2,1,0:T(8,128)(2,1)}), bf16[16,240,256]{2,1,0:T(8,128)(2,1)}, u32[]{:S(2)}, u32[]{:S(2)}) %all-to-all-start) | async-done | bytes 1966112 | tf_op jit(solution)/shard_map/all_to_all | solution.py:326
  170.4 15.8 %shard_map.116 = bf16[16,160,256]{2,1,0:T(8,128)(2,1)} custom-call(bf16[16,240,256]{2,1,0:T(8,128)(2,1)} %all-to-all-done.refs_0_, bf16[192,2048]{1,0:T(8,128)(2,1)} %bitcast.28, bf16[192,2048]{1,0:T(8,128)(2,1)} %bitcast.31, bf16[192,2048]{1,0:T(8,128)(2,1)} %bitcast.34, bf16[192,2048]{1,0:T(8,128)(2,1)} %collective-permute-done.2.refs_4_, ...), custom_call_target="tpu_custom_call" | custom-call | flops 8000000000 | bytes 14000000 | tf_op jit(solution)/shard_map/pallas_call | solution.py:271
  186.2 54.0 %all_to_all.10.back = bf16[16,160,256]{2,1,0:T(8,128)(2,1)} all-to-all(bf16[16,160,256]{2,1,0:T(8,128)(2,1)} %shard_map.116), channel_id=1, replica_groups=mesh['section'=8,'plane'=4,'pair'=4,'half'=2,'core'=2] {'plane','pair'}, dimensions={0} | all-to-all | bytes 2621440 | tf_op jit(solution)/shard_map/all_to_all | solution.py:326
  240.2 3.8 %shard_map.117 = (bf16[128,2048]{1,0:T(8,128)(2,1)}, bf16[128,2048]{1,0:T(8,128)(2,1)}) custom-call(s32[8,128]{1,0:T(8,128)} %bitcast.42, f32[8,128]{1,0:T(8,128)} %bitcast.44, s32[8,128]{1,0:T(8,128)} %bitcast.46, f32[8,128]{1,0:T(8,128)} %bitcast.48, bf16[16,160,256]{2,1,0:T(8,128)(2,1)} %all_to_all.10.back), custom_call_target="tpu_custom_call" | custom-call | flops 800000000 | bytes 4000000 | tf_op jit(solution)/shard_map/pallas_call | solution.py:188
  (7 shorter events, 0.0 us)
Async XLA Ops:
  0.6 122.2 %collective-permute-start.2 = (bf16[192,2048]{1,0:T(8,128)(2,1)}, bf16[192,2048]{1,0:T(8,128)(2,1)}, u32[]{:S(2)}, u32[]{:S(2)}) collective-permute-start(bf16[192,2048]{1,0:T(8,128)(2,1)} %bitcast.26), channel_id=1, source_target_pairs={{0,2},{2,0},{1,3},{3,1},{4,6},{6,4},{5,7},{7,5},{8,10},{10,8},{9,1... | collective-permute-start | bytes 2359304 | tf_op jit(solution)/shard_map/ppermute | solution.py:322
  4.7 120.1 %collective-permute-start.3 = (bf16[192,2048]{1,0:T(8,128)(2,1)}, bf16[192,2048]{1,0:T(8,128)(2,1)}, u32[]{:S(2)}, u32[]{:S(2)}) collective-permute-start(bf16[192,2048]{1,0:T(8,128)(2,1)} %bitcast.29), channel_id=1, source_target_pairs={{0,2},{2,0},{1,3},{3,1},{4,6},{6,4},{5,7},{7,5},{8,10},{10,8},{9,1... | collective-permute-start | bytes 2359304 | tf_op jit(solution)/shard_map/ppermute | solution.py:322
  6.6 120.6 %collective-permute-start.4 = (bf16[192,2048]{1,0:T(8,128)(2,1)}, bf16[192,2048]{1,0:T(8,128)(2,1)}, u32[]{:S(2)}, u32[]{:S(2)}) collective-permute-start(bf16[192,2048]{1,0:T(8,128)(2,1)} %bitcast.32), channel_id=1, source_target_pairs={{0,2},{2,0},{1,3},{3,1},{4,6},{6,4},{5,7},{7,5},{8,10},{10,8},{9,1... | collective-permute-start | bytes 2359304 | tf_op jit(solution)/shard_map/ppermute | solution.py:322
  10.0 10.5 %collective-permute-start = (bf16[128,2048]{1,0:T(8,128)(2,1)}, bf16[128,2048]{1,0:T(8,128)(2,1)S(1)}, u32[]{:S(2)}, u32[]{:S(2)}) collective-permute-start(bf16[128,2048]{1,0:T(8,128)(2,1)} %bitcast.36), channel_id=1, source_target_pairs={{64,0},{128,64},{192,128},{256,192},{320,256},{384,320},{448,384},... | collective-permute-start | bytes 1572872 | tf_op jit(solution)/shard_map/ppermute | solution.py:318
  11.3 10.4 %collective-permute-start.1 = (bf16[128,2048]{1,0:T(8,128)(2,1)}, bf16[128,2048]{1,0:T(8,128)(2,1)S(1)}, u32[]{:S(2)}, u32[]{:S(2)}) collective-permute-start(bf16[128,2048]{1,0:T(8,128)(2,1)} %bitcast.38), channel_id=1, source_target_pairs={{0,64},{64,128},{128,192},{192,256},{256,320},{320,384},{384,448},... | collective-permute-start | bytes 1572872 | tf_op jit(solution)/shard_map/ppermute | solution.py:318
  20.5 1.2 copy-start
  21.7 0.8 copy-start.1
  100.0 70.3 %all-to-all-start = ((bf16[16,240,256]{2,1,0:T(8,128)(2,1)}), bf16[16,240,256]{2,1,0:T(8,128)(2,1)}, u32[]{:S(2)}, u32[]{:S(2)}) async-start(bf16[16,240,256]{2,1,0:T(8,128)(2,1)} %shard_map.113.refs_3_), calls=%async_computation | async-start | bytes 3932160 | tf_op jit(solution)/shard_map/all_to_all | solution.py:326
  117.9 13.8 %collective-permute-start.8 = (bf16[3,192,2048]{2,1,0:T(8,128)(2,1)}, bf16[3,192,2048]{2,1,0:T(8,128)(2,1)}, u32[]{:S(2)}, u32[]{:S(2)}) collective-permute-start(bf16[3,192,2048]{2,1,0:T(8,128)(2,1)} %shard_map.114), channel_id=1, source_target_pairs={{0,1},{1,0},{2,3},{3,2},{4,5},{5,4},{6,7},{7,6},{8,9},{9,8},{10,11... | collective-permute-start | bytes 7077896 | tf_op jit(solution)/shard_map/ppermute | solution.py:322
  122.8 7.6 %collective-permute-start.5 = (bf16[192,2048]{1,0:T(8,128)(2,1)}, bf16[192,2048]{1,0:T(8,128)(2,1)}, u32[]{:S(2)}, u32[]{:S(2)}) collective-permute-start(bf16[192,2048]{1,0:T(8,128)(2,1)} %collective-permute-done.2.refs_4_), channel_id=1, source_target_pairs={{0,1},{1,0},{2,3},{3,2},{4,5},{5,4},{6,7},{7,6},{8,9},{9,8},{10,11... | collective-permute-start | bytes 2359304 | tf_op jit(solution)/shard_map/ppermute | solution.py:322
  124.7 5.7 %collective-permute-start.6 = (bf16[192,2048]{1,0:T(8,128)(2,1)}, bf16[192,2048]{1,0:T(8,128)(2,1)}, u32[]{:S(2)}, u32[]{:S(2)}) collective-permute-start(bf16[192,2048]{1,0:T(8,128)(2,1)} %collective-permute-done.3.refs_5_), channel_id=1, source_target_pairs={{0,1},{1,0},{2,3},{3,2},{4,5},{5,4},{6,7},{7,6},{8,9},{9,8},{10,11... | collective-permute-start | bytes 2359304 | tf_op jit(solution)/shard_map/ppermute | solution.py:322
  127.2 4.5 %collective-permute-start.7 = (bf16[192,2048]{1,0:T(8,128)(2,1)}, bf16[192,2048]{1,0:T(8,128)(2,1)}, u32[]{:S(2)}, u32[]{:S(2)}) collective-permute-start(bf16[192,2048]{1,0:T(8,128)(2,1)} %collective-permute-done.4.refs_6_), channel_id=1, source_target_pairs={{0,1},{1,0},{2,3},{3,2},{4,5},{5,4},{6,7},{7,6},{8,9},{9,8},{10,11... | collective-permute-start | bytes 2359304 | tf_op jit(solution)/shard_map/ppermute | solution.py:322

commit v4 on v3

--- a/solution.py
+++ b/solution.py
@@ -220,7 +220,7 @@
         for _, c, shift in [m for m in MEETS if m[0] == j]:
             slot = line + shift
             hit = (at == source * CAP + slot) & (slot >= 0) & (slot < CAP)
-            piece = rows[:, c * width : (c + 1) * width].astype(BF16)
+            piece = rows[:, c * width : (c + 1) * width]
             total = total + dot(hit.astype(F32).astype(BF16), piece)
         lines = slice(base + j * TILE, base + (j + 1) * TILE)
         packed[:, lines, :] = total.astype(BF16).reshape(EXPERTS, TILE, width)
@@ -229,43 +229,43 @@
 def experts_body(*refs):
     got, weights, beside = refs[0], list(refs[1 : 3 * SHARDS - 2]), refs[3 * SHARDS - 2]
     weights += [beside.at[i] for i in range(3)]
-    back, rows, scaled, sent, bwd_total, fwd_total, held, ready = refs[-8:]
-    copies = [
-        pltpu.make_async_copy(w, held.at[n], ready.at[n]) for n, w in enumerate(weights)
-    ]
+    back, rows, scaled, bwd_total, fwd_total, held, ready = refs[-7:]
+    hidden = weights[0].shape[0]
+    copies = []
+    for n, w in enumerate(weights):
+        units = pl.ds(n // 3 * hidden, hidden)
+        copies.append(pltpu.make_async_copy(w, held.at[n % 3, units], ready.at[n]))
     for copy in copies:
         copy.start()
-    unpack_rows(got, rows, BWD * PACKED)
+    unpack_rows(got, rows.at[:ROWS], BWD * PACKED)
+    unpack_rows(got, rows.at[ROWS:], FWD * PACKED)
     unpack_rows(got, scaled, SCALED * PACKED)
-    unpack_rows(got, sent, FWD * PACKED)
-    for n in range(SHARDS):
-        for copy in copies[3 * n : 3 * n + 3]:
-            copy.wait()
-        gate, up, down = held.at[3 * n], held.at[3 * n + 1], held.at[3 * n + 2]
-        gate_back = dot_nt(rows[...], gate[...])
-        up_back = dot_nt(rows[...], up[...])
-        dact = dot_nt(scaled[...], down[...])
-        sigma = 1.0 / (1.0 + jnp.exp(-gate_back))
-        dgate = (dact * up_back * sigma * (1.0 + gate_back * (1.0 - sigma))).astype(BF16)
-        dup = (dact * (gate_back * sigma)).astype(BF16)
-        part = dot(dgate, gate[...]) + dot(dup, up[...])
-        bwd_total[...] = part if n == 0 else bwd_total[...] + part
-
-        gate_pre = dot_nt(sent[...], gate[...])
-        up_pre = dot_nt(sent[...], up[...])
-        act = (gate_pre / (1.0 + jnp.exp(-gate_pre)) * up_pre).astype(BF16)
-        part = dot(act, down[...])
-        fwd_total[...] = part if n == 0 else fwd_total[...] + part
+    for copy in copies:
+        copy.wait()
+    gate, up, down = held.at[0], held.at[1], held.at[2]
+    gates = dot_nt(rows[...], gate[...])
+    ups = dot_nt(rows[...], up[...])
+    gate_back, gate_pre = gates[:ROWS], gates[ROWS:]
+    up_back, up_pre = ups[:ROWS], ups[ROWS:]
+    act = (gate_pre / (1.0 + jnp.exp(-gate_pre)) * up_pre).astype(BF16)
+    dact = dot_nt(scaled[...], down[...])
+    sigma = 1.0 / (1.0 + jnp.exp(-gate_back))
+    dgate = (dact * up_back * sigma * (1.0 + gate_back * (1.0 - sigma))).astype(BF16)
+    dup = (dact * (gate_back * sigma)).astype(BF16)
+    bwd_total[...] = (dot(dgate, gate[...]) + dot(dup, up[...])).astype(BF16)
+    fwd_total[...] = dot(act, down[...]).astype(BF16)
     pack_rows(bwd_total, back, BWD_BACK * PACKED)
     pack_rows(fwd_total, back, FWD_BACK * PACKED)
 
 
 def experts_of(got, weights, beside, after):
     width = got.shape[2] * CHUNKS
-    scratch = [pltpu.VMEM((ROWS, width), BF16)] * 3 + [
-        pltpu.VMEM((ROWS, width), F32),
-        pltpu.VMEM((ROWS, width), F32),
-        pltpu.VMEM((3 * SHARDS,) + weights[0].shape, BF16),
+    scratch = [
+        pltpu.VMEM((2 * ROWS, width), BF16),
+        pltpu.VMEM((ROWS, width), BF16),
+        pltpu.VMEM((ROWS, width), BF16),
+        pltpu.VMEM((ROWS, width), BF16),
+        pltpu.VMEM((3, SHARDS * weights[0].shape[0], width), BF16),
         pltpu.SemaphoreType.DMA((3 * SHARDS,)),
     ]
     return pl.pallas_call(
@@ -278,23 +278,19 @@
     )(got, *weights, beside, after)
 
 
-def stack_body(*refs):
-    arrays, out, done = refs[:3], refs[-2], refs[-1]
-    copies = [pltpu.make_async_copy(w, out.at[i], done.at[i]) for i, w in enumerate(arrays)]
-    for copy in copies:
-        copy.start()
-    for copy in copies:
-        copy.wait()
+def stack_body(gate, up, down, after, out):
+    del after
+    out[0] = gate[...]
+    out[1] = up[...]
+    out[2] = down[...]
 
 
 def stack(arrays, after):
-    n = len(arrays)
     return pl.pallas_call(
         stack_body,
-        out_shape=jax.ShapeDtypeStruct((n,) + arrays[0].shape, BF16),
-        in_specs=[HBM] * (n + 1),
-        out_specs=HBM,
-        scratch_shapes=[pltpu.SemaphoreType.DMA((n,))],
+        out_shape=jax.ShapeDtypeStruct((3,) + arrays[0].shape, BF16),
+        in_specs=[pl.BlockSpec()] * 3 + [HBM],
+        compiler_params=pltpu.CompilerParams(vmem_limit_bytes=60 * 2**20),
         cost_estimate=cost(0, 5_000_000),
     )(*arrays, after)
 

time: 246 us -> 171 us (0.70)
  Pallas kernels: 98.5 us -> 25.8 us
  starting transfers between devices: 43.6 us -> 63 us
  blocking collectives: 54 us -> 39.9 us
  waiting for transfers between devices: 45.8 us -> 38.2 us
    pallas_call x1, Pallas kernels: 72.6 us -> 3.17 us  [stack(): pl.pallas_call(stack_body, out_shape=jax.ShapeDtypeStruct((3,) + arrays[0...]
    ppermute x7, starting transfers between devices: 20.5 us -> 39.9 us  [swap(): return lax.ppermute(x, axis, [(0, 1), (1, 0)])]
    all_to_all x1, blocking collectives: 54 us -> 39.9 us  [exchange(): lax.all_to_all(x, ('plane', 'pair'), split_axis=0, concat_axis=0, tiled=T...]
    all_to_all x1, waiting for transfers between devices: 38.7 us -> 31.5 us  [exchange(): lax.all_to_all(x, ('plane', 'pair'), split_axis=0, concat_axis=0, tiled=T...]
    pallas_call x1, Pallas kernels: 15.8 us -> 12.5 us  [experts_of(): pl.pallas_call(experts_body, out_shape=jax.ShapeDtypeStruct((EXPERTS, 2 *...]
  transfers between devices with their start and end apart: 10 -> 10, of which waited for: 4 -> 4; matrix products, arithmetic and copies ran while one was open for 0% -> 0% of each run, Pallas kernels for 32% -> 6%
where the time goes in v4:
time: 171 us; the launch traced here: 169 us
  starting transfers between devices  63 us (37%)
  blocking collectives  39.9 us (23%)
  waiting for transfers between devices  38.2 us (22%)
  Pallas kernels  25.8 us (15%)
    all_to_all x1, blocking collectives, exchange(): lax.all_to_all(x, ('plane', 'pair'), split_axis=0, concat_axis=0, tiled=T...  39.9 us
    ppermute x7, starting transfers between devices, swap(): return lax.ppermute(x, axis, [(0, 1), (1, 0)])  39.9 us
    all_to_all x1, waiting for transfers between devices, exchange(): lax.all_to_all(x, ('plane', 'pair'), split_axis=0, concat_axis=0, tiled=T...  31.5 us
    all_to_all x1, starting transfers between devices, exchange(): lax.all_to_all(x, ('plane', 'pair'), split_axis=0, concat_axis=0, tiled=T...  17.8 us
    pallas_call x1, Pallas kernels, experts_of(): pl.pallas_call(experts_body, out_shape=jax.ShapeDtypeStruct((EXPERTS, 2 *...  12.5 us
    ppermute x2, waiting for transfers between devices, from_behind(): return lax.ppermute(x, axis, pairs)  5.79 us
    ppermute x2, starting transfers between devices, from_behind(): return lax.ppermute(x, axis, pairs)  5.32 us
    pallas_call x1, Pallas kernels, pick(): pl.pallas_call(pick_body, out_shape=jax.ShapeDtypeStruct(out, BF16), in_s...  4.91 us
  transfers between devices with their start and end apart: 10, of which 4 were waited for; matrix products, arithmetic and copies ran while one was open for 0% of the time, Pallas kernels for 6%

profile of v4, /device:TPU:1, one launch (start us, length us, event | category | flops | bytes accessed | tf_op | source)
XLA Modules:
  0.0 169.0 jit_solution(5170906192953280030)
XLA Ops:
  0.6 4.0 %collective-permute-start.2 = (bf16[192,2048]{1,0:T(8,128)(2,1)}, bf16[192,2048]{1,0:T(8,128)(2,1)}, u32[]{:S(2)}, u32[]{:S(2)}) collective-permute-start(bf16[192,2048]{1,0:T(8,128)(2,1)} %bitcast.26), channel_id=1, source_target_pairs={{0,2},{2,0},{1,3},{3,1},{4,6},{6,4},{5,7},{7,5},{8,10},{10,8},{9,1... | collective-permute-start | bytes 2359304 | tf_op jit(solution)/shard_map/ppermute | solution.py:318
  4.7 1.9 %collective-permute-start.3 = (bf16[192,2048]{1,0:T(8,128)(2,1)}, bf16[192,2048]{1,0:T(8,128)(2,1)}, u32[]{:S(2)}, u32[]{:S(2)}) collective-permute-start(bf16[192,2048]{1,0:T(8,128)(2,1)} %bitcast.29), channel_id=1, source_target_pairs={{0,2},{2,0},{1,3},{3,1},{4,6},{6,4},{5,7},{7,5},{8,10},{10,8},{9,1... | collective-permute-start | bytes 2359304 | tf_op jit(solution)/shard_map/ppermute | solution.py:318
  6.6 3.4 %collective-permute-start.4 = (bf16[192,2048]{1,0:T(8,128)(2,1)}, bf16[192,2048]{1,0:T(8,128)(2,1)}, u32[]{:S(2)}, u32[]{:S(2)}) collective-permute-start(bf16[192,2048]{1,0:T(8,128)(2,1)} %bitcast.32), channel_id=1, source_target_pairs={{0,2},{2,0},{1,3},{3,1},{4,6},{6,4},{5,7},{7,5},{8,10},{10,8},{9,1... | collective-permute-start | bytes 2359304 | tf_op jit(solution)/shard_map/ppermute | solution.py:318
  10.0 1.3 collective-permute-start
  11.3 4.0 %collective-permute-start.1 = (bf16[128,2048]{1,0:T(8,128)(2,1)}, bf16[128,2048]{1,0:T(8,128)(2,1)S(1)}, u32[]{:S(2)}, u32[]{:S(2)}) collective-permute-start(bf16[128,2048]{1,0:T(8,128)(2,1)} %bitcast.38), channel_id=1, source_target_pairs={{0,64},{64,128},{128,192},{192,256},{256,320},{320,384},{384,448},... | collective-permute-start | bytes 1572872 | tf_op jit(solution)/shard_map/ppermute | solution.py:314
  15.3 0.6 add_convert_fusion.edges
  15.9 4.6 %collective-permute-done.refs_2_ = bf16[128,2048]{1,0:T(8,128)(2,1)S(1)} collective-permute-done((bf16[128,2048]{1,0:T(8,128)(2,1)}, bf16[128,2048]{1,0:T(8,128)(2,1)S(1)}, u32[]{:S(2)}, u32[]{:S(2)}) %collective-permute-start) | collective-permute-done | bytes 524320 | tf_op jit(solution)/shard_map/ppermute | solution.py:314
  20.5 1.2 collective-permute-done.1.refs_4_
  21.7 0.8 copy-done.1
  22.5 4.9 %shard_map.113.after = bf16[16,240,256]{2,1,0:T(8,128)(2,1)} custom-call(s32[2]{0:T(128)} %add_convert_fusion.edges, s32[8,128]{1,0:T(8,128)} %bitcast.40, f32[8,128]{1,0:T(8,128)} %bitcast.43, s32[8,128]{1,0:T(8,128)} %bitcast.45, f32[8,128]{1,0:T(8,128)} %bitcast.47, bf16[128,2048]{1,0:T(8,128)(2,1)} %bitcast.35, bf16[128,2048]{1,0:T(8,128)(2,1)} %bitcast.37, ...), custom_call_target="tpu_custom_call" | custom-call | flops 1600000000 | bytes 5000000 | tf_op jit(solution)/shard_map/pallas_call | solution.py:138
  27.4 3.2 %shard_map.114 = bf16[3,192,2048]{2,1,0:T(8,128)(2,1)} custom-call(bf16[192,2048]{1,0:T(8,128)(2,1)} %bitcast.27, bf16[192,2048]{1,0:T(8,128)(2,1)} %bitcast.30, bf16[192,2048]{1,0:T(8,128)(2,1)} %bitcast.33, bf16[16,240,256]{2,1,0:T(8,128)(2,1)} %shard_map.113.after), custom_call_target="tpu_custom_call" | custom-call | bytes 5000000 | tf_op jit(solution)/shard_map/pallas_call | solution.py:289
  30.6 17.8 %all-to-all-start = ((bf16[16,240,256]{2,1,0:T(8,128)(2,1)}), bf16[16,240,256]{2,1,0:T(8,128)(2,1)}, u32[]{:S(2)}, u32[]{:S(2)}) async-start(bf16[16,240,256]{2,1,0:T(8,128)(2,1)} %shard_map.113.after), calls=%async_computation | async-start | bytes 3932160 | tf_op jit(solution)/shard_map/all_to_all | solution.py:322
  48.4 4.9 %collective-permute-start.8 = (bf16[3,192,2048]{2,1,0:T(8,128)(2,1)}, bf16[3,192,2048]{2,1,0:T(8,128)(2,1)}, u32[]{:S(2)}, u32[]{:S(2)}) collective-permute-start(bf16[3,192,2048]{2,1,0:T(8,128)(2,1)} %shard_map.114), channel_id=1, source_target_pairs={{0,1},{1,0},{2,3},{3,2},{4,5},{5,4},{6,7},{7,6},{8,9},{9,8},{10,11... | collective-permute-start | bytes 7077896 | tf_op jit(solution)/shard_map/ppermute | solution.py:318
  53.3 0.0 collective-permute-done.2.refs_4_
  53.4 1.9 %collective-permute-start.5 = (bf16[192,2048]{1,0:T(8,128)(2,1)}, bf16[192,2048]{1,0:T(8,128)(2,1)}, u32[]{:S(2)}, u32[]{:S(2)}) collective-permute-start(bf16[192,2048]{1,0:T(8,128)(2,1)} %collective-permute-done.2.refs_4_), channel_id=1, source_target_pairs={{0,1},{1,0},{2,3},{3,2},{4,5},{5,4},{6,7},{7,6},{8,9},{9,8},{10,11... | collective-permute-start | bytes 2359304 | tf_op jit(solution)/shard_map/ppermute | solution.py:318
  55.3 0.0 collective-permute-done.3.refs_5_
  55.3 2.4 %collective-permute-start.6 = (bf16[192,2048]{1,0:T(8,128)(2,1)}, bf16[192,2048]{1,0:T(8,128)(2,1)}, u32[]{:S(2)}, u32[]{:S(2)}) collective-permute-start(bf16[192,2048]{1,0:T(8,128)(2,1)} %collective-permute-done.3.refs_5_), channel_id=1, source_target_pairs={{0,1},{1,0},{2,3},{3,2},{4,5},{5,4},{6,7},{7,6},{8,9},{9,8},{10,11... | collective-permute-start | bytes 2359304 | tf_op jit(solution)/shard_map/ppermute | solution.py:318
  57.7 21.3 %collective-permute-start.7 = (bf16[192,2048]{1,0:T(8,128)(2,1)}, bf16[192,2048]{1,0:T(8,128)(2,1)}, u32[]{:S(2)}, u32[]{:S(2)}) collective-permute-start(bf16[192,2048]{1,0:T(8,128)(2,1)} %collective-permute-done.4.refs_6_), channel_id=1, source_target_pairs={{0,1},{1,0},{2,3},{3,2},{4,5},{5,4},{6,7},{7,6},{8,9},{9,8},{10,11... | collective-permute-start | bytes 2359304 | tf_op jit(solution)/shard_map/ppermute | solution.py:318
  79.0 1.3 shard_map.115.refs_11_
  80.4 0.9 collective-permute-done.7.refs_9_
  81.3 31.5 %all-to-all-done.refs_0_ = bf16[16,240,256]{2,1,0:T(8,128)(2,1)} async-done(((bf16[16,240,256]{2,1,0:T(8,128)(2,1)}), bf16[16,240,256]{2,1,0:T(8,128)(2,1)}, u32[]{:S(2)}, u32[]{:S(2)}) %all-to-all-start) | async-done | bytes 1966112 | tf_op jit(solution)/shard_map/all_to_all | solution.py:322
  112.8 12.5 %shard_map.116 = bf16[16,160,256]{2,1,0:T(8,128)(2,1)} custom-call(bf16[16,240,256]{2,1,0:T(8,128)(2,1)} %all-to-all-done.refs_0_, bf16[192,2048]{1,0:T(8,128)(2,1)} %bitcast.28, bf16[192,2048]{1,0:T(8,128)(2,1)} %bitcast.31, bf16[192,2048]{1,0:T(8,128)(2,1)} %bitcast.34, bf16[192,2048]{1,0:T(8,128)(2,1)} %collective-permute-done.2.refs_4_, ...), custom_call_target="tpu_custom_call" | custom-call | flops 8000000000 | bytes 14000000 | tf_op jit(solution)/shard_map/pallas_call | solution.py:271
  125.3 39.9 %all_to_all.10.back = bf16[16,160,256]{2,1,0:T(8,128)(2,1)} all-to-all(bf16[16,160,256]{2,1,0:T(8,128)(2,1)} %shard_map.116), channel_id=1, replica_groups=mesh['section'=8,'plane'=4,'pair'=4,'half'=2,'core'=2] {'plane','pair'}, dimensions={0} | all-to-all | bytes 2621440 | tf_op jit(solution)/shard_map/all_to_all | solution.py:322
  165.2 3.8 %shard_map.117 = (bf16[128,2048]{1,0:T(8,128)(2,1)}, bf16[128,2048]{1,0:T(8,128)(2,1)}) custom-call(s32[8,128]{1,0:T(8,128)} %bitcast.42, f32[8,128]{1,0:T(8,128)} %bitcast.44, s32[8,128]{1,0:T(8,128)} %bitcast.46, f32[8,128]{1,0:T(8,128)} %bitcast.48, bf16[16,160,256]{2,1,0:T(8,128)(2,1)} %all_to_all.10.back), custom_call_target="tpu_custom_call" | custom-call | flops 800000000 | bytes 4000000 | tf_op jit(solution)/shard_map/pallas_call | solution.py:188
  (7 shorter events, 0.0 us)
Async XLA Ops:
  0.6 52.7 %collective-permute-start.2 = (bf16[192,2048]{1,0:T(8,128)(2,1)}, bf16[192,2048]{1,0:T(8,128)(2,1)}, u32[]{:S(2)}, u32[]{:S(2)}) collective-permute-start(bf16[192,2048]{1,0:T(8,128)(2,1)} %bitcast.26), channel_id=1, source_target_pairs={{0,2},{2,0},{1,3},{3,1},{4,6},{6,4},{5,7},{7,5},{8,10},{10,8},{9,1... | collective-permute-start | bytes 2359304 | tf_op jit(solution)/shard_map/ppermute | solution.py:318
  4.7 50.6 %collective-permute-start.3 = (bf16[192,2048]{1,0:T(8,128)(2,1)}, bf16[192,2048]{1,0:T(8,128)(2,1)}, u32[]{:S(2)}, u32[]{:S(2)}) collective-permute-start(bf16[192,2048]{1,0:T(8,128)(2,1)} %bitcast.29), channel_id=1, source_target_pairs={{0,2},{2,0},{1,3},{3,1},{4,6},{6,4},{5,7},{7,5},{8,10},{10,8},{9,1... | collective-permute-start | bytes 2359304 | tf_op jit(solution)/shard_map/ppermute | solution.py:318
  6.6 51.1 %collective-permute-start.4 = (bf16[192,2048]{1,0:T(8,128)(2,1)}, bf16[192,2048]{1,0:T(8,128)(2,1)}, u32[]{:S(2)}, u32[]{:S(2)}) collective-permute-start(bf16[192,2048]{1,0:T(8,128)(2,1)} %bitcast.32), channel_id=1, source_target_pairs={{0,2},{2,0},{1,3},{3,1},{4,6},{6,4},{5,7},{7,5},{8,10},{10,8},{9,1... | collective-permute-start | bytes 2359304 | tf_op jit(solution)/shard_map/ppermute | solution.py:318
  10.0 10.5 %collective-permute-start = (bf16[128,2048]{1,0:T(8,128)(2,1)}, bf16[128,2048]{1,0:T(8,128)(2,1)S(1)}, u32[]{:S(2)}, u32[]{:S(2)}) collective-permute-start(bf16[128,2048]{1,0:T(8,128)(2,1)} %bitcast.36), channel_id=1, source_target_pairs={{64,0},{128,64},{192,128},{256,192},{320,256},{384,320},{448,384},... | collective-permute-start | bytes 1572872 | tf_op jit(solution)/shard_map/ppermute | solution.py:314
  11.3 10.4 %collective-permute-start.1 = (bf16[128,2048]{1,0:T(8,128)(2,1)}, bf16[128,2048]{1,0:T(8,128)(2,1)S(1)}, u32[]{:S(2)}, u32[]{:S(2)}) collective-permute-start(bf16[128,2048]{1,0:T(8,128)(2,1)} %bitcast.38), channel_id=1, source_target_pairs={{0,64},{64,128},{128,192},{192,256},{256,320},{320,384},{384,448},... | collective-permute-start | bytes 1572872 | tf_op jit(solution)/shard_map/ppermute | solution.py:314
  20.5 1.2 copy-start
  21.7 0.8 copy-start.1
  30.6 82.2 %all-to-all-start = ((bf16[16,240,256]{2,1,0:T(8,128)(2,1)}), bf16[16,240,256]{2,1,0:T(8,128)(2,1)}, u32[]{:S(2)}, u32[]{:S(2)}) async-start(bf16[16,240,256]{2,1,0:T(8,128)(2,1)} %shard_map.113.after), calls=%async_computation | async-start | bytes 3932160 | tf_op jit(solution)/shard_map/all_to_all | solution.py:322
  48.4 32.9 %collective-permute-start.8 = (bf16[3,192,2048]{2,1,0:T(8,128)(2,1)}, bf16[3,192,2048]{2,1,0:T(8,128)(2,1)}, u32[]{:S(2)}, u32[]{:S(2)}) collective-permute-start(bf16[3,192,2048]{2,1,0:T(8,128)(2,1)} %shard_map.114), channel_id=1, source_target_pairs={{0,1},{1,0},{2,3},{3,2},{4,5},{5,4},{6,7},{7,6},{8,9},{9,8},{10,11... | collective-permute-start | bytes 7077896 | tf_op jit(solution)/shard_map/ppermute | solution.py:318
  53.4 27.0 %collective-permute-start.5 = (bf16[192,2048]{1,0:T(8,128)(2,1)}, bf16[192,2048]{1,0:T(8,128)(2,1)}, u32[]{:S(2)}, u32[]{:S(2)}) collective-permute-start(bf16[192,2048]{1,0:T(8,128)(2,1)} %collective-permute-done.2.refs_4_), channel_id=1, source_target_pairs={{0,1},{1,0},{2,3},{3,2},{4,5},{5,4},{6,7},{7,6},{8,9},{9,8},{10,11... | collective-permute-start | bytes 2359304 | tf_op jit(solution)/shard_map/ppermute | solution.py:318
  55.3 25.1 %collective-permute-start.6 = (bf16[192,2048]{1,0:T(8,128)(2,1)}, bf16[192,2048]{1,0:T(8,128)(2,1)}, u32[]{:S(2)}, u32[]{:S(2)}) collective-permute-start(bf16[192,2048]{1,0:T(8,128)(2,1)} %collective-permute-done.3.refs_5_), channel_id=1, source_target_pairs={{0,1},{1,0},{2,3},{3,2},{4,5},{5,4},{6,7},{7,6},{8,9},{9,8},{10,11... | collective-permute-start | bytes 2359304 | tf_op jit(solution)/shard_map/ppermute | solution.py:318
  57.7 23.6 %collective-permute-start.7 = (bf16[192,2048]{1,0:T(8,128)(2,1)}, bf16[192,2048]{1,0:T(8,128)(2,1)}, u32[]{:S(2)}, u32[]{:S(2)}) collective-permute-start(bf16[192,2048]{1,0:T(8,128)(2,1)} %collective-permute-done.4.refs_6_), channel_id=1, source_target_pairs={{0,1},{1,0},{2,3},{3,2},{4,5},{5,4},{6,7},{7,6},{8,9},{9,8},{10,11... | collective-permute-start | bytes 2359304 | tf_op jit(solution)/shard_map/ppermute | solution.py:318

commit v5 on v4

--- a/solution.py
+++ b/solution.py
@@ -47,6 +47,10 @@
 
 def dot_nt(a, b):
     return lax.dot_general(a, b, NT, preferred_element_type=F32)
+
+
+def one_where(place, shift):
+    return jnp.where(place == float(shift), 1.0, 0.0).astype(BF16)
 
 
 def halves(values):
@@ -80,7 +84,7 @@
 
 def pick_rows(key, gate, states, out):
     key = spread_rows(key)
-    row = lax.rem(iota(key.shape, 0), TILE).astype(F32)
+    place = key - lax.rem(iota(key.shape, 0), TILE).astype(F32)
     parts = [1.0]
     if gate is not None:
         parts = [h.astype(F32) for h in halves(spread_rows(gate))]
@@ -88,7 +92,7 @@
     for j in range(TILES):
         total = jnp.zeros((SPAN, width), F32)
         for _, c, shift in [m for m in MEETS if m[0] == j]:
-            hit = key == row + float(shift)
+            hit = place == float(shift)
             piece = states[:, c * width : (c + 1) * width]
             for part in parts:
                 total = total + dot(jnp.where(hit, part, 0.0).astype(BF16), piece)
@@ -161,7 +165,7 @@
     column, source = iota((128, SPAN), 0), iota((128, SPAN), 1) // TILE
     key = dot(turned.astype(BF16), (column == source).astype(F32).astype(BF16))
     widen = (column == source + EXPERTS).astype(F32).astype(BF16)
-    row = lax.rem(iota(key.shape, 1), TILE).astype(F32)
+    place = key - lax.rem(iota(key.shape, 1), TILE).astype(F32)
     parts = [1.0]
     if weighted:
         parts = [dot(h, widen) for h in halves(turned)]
@@ -169,7 +173,7 @@
     for c in range(CHUNKS):
         total = jnp.zeros((tokens, width), F32)
         for j, _, shift in [m for m in MEETS if m[1] == c]:
-            hit = key == row + float(shift)
+            hit = place == float(shift)
             lines = slice(base + j * TILE, base + (j + 1) * TILE)
             rows = back[:, lines, :].reshape(SPAN, width)
             for part in parts:
@@ -194,52 +198,52 @@
     )(*routes, back)
 
 
-def unpack_rows(packed, rows, base):
+def places(source, line, at):
+    slot = at - source * CAP
+    return jnp.where((slot >= 0) & (slot < CAP), slot - line, int(NONE)).astype(F32)
+
+
+def unpack_rows(packed, arrays):
     width = packed.shape[2]
-    at = iota((ROWS, SPAN), 0)
     lane = iota((ROWS, SPAN), 1)
-    source, line = lane // TILE, lax.rem(lane, TILE)
+    place = places(lane // TILE, lax.rem(lane, TILE), iota((ROWS, SPAN), 0))
     for c in range(CHUNKS):
-        total = jnp.zeros((ROWS, width), F32)
+        totals = {n: jnp.zeros((ROWS, width), F32) for n in arrays}
         for j, _, shift in [m for m in MEETS if m[1] == c]:
-            slot = line + shift
-            hit = (at == source * CAP + slot) & (slot >= 0) & (slot < CAP)
-            lines = slice(base + j * TILE, base + (j + 1) * TILE)
-            tile = packed[:, lines, :].reshape(SPAN, width)
-            total = total + dot(hit.astype(F32).astype(BF16), tile)
-        rows[:, c * width : (c + 1) * width] = total.astype(BF16)
-
-
-def pack_rows(rows, packed, base):
+            hit = one_where(place, shift)
+            for n in arrays:
+                lines = slice(n * PACKED + j * TILE, n * PACKED + (j + 1) * TILE)
+                totals[n] = totals[n] + dot(hit, packed[:, lines, :].reshape(SPAN, width))
+        for n, rows in arrays.items():
+            rows[:, c * width : (c + 1) * width] = totals[n].astype(BF16)
+
+
+def pack_rows(arrays, packed):
     width = packed.shape[2]
-    at = iota((SPAN, ROWS), 1)
-    place = iota((SPAN, ROWS), 0)
-    source, line = place // TILE, lax.rem(place, TILE)
+    line = iota((SPAN, ROWS), 0)
+    place = places(line // TILE, lax.rem(line, TILE), iota((SPAN, ROWS), 1))
     for j in range(TILES):
-        total = jnp.zeros((SPAN, width), F32)
+        totals = {n: jnp.zeros((SPAN, width), F32) for n in arrays}
         for _, c, shift in [m for m in MEETS if m[0] == j]:
-            slot = line + shift
-            hit = (at == source * CAP + slot) & (slot >= 0) & (slot < CAP)
-            piece = rows[:, c * width : (c + 1) * width]
-            total = total + dot(hit.astype(F32).astype(BF16), piece)
-        lines = slice(base + j * TILE, base + (j + 1) * TILE)
-        packed[:, lines, :] = total.astype(BF16).reshape(EXPERTS, TILE, width)
+            hit = one_where(place, shift)
+            for n, rows in arrays.items():
+                totals[n] = totals[n] + dot(hit, rows[:, c * width : (c + 1) * width])
+        for n in arrays:
+            lines = slice(n * PACKED + j * TILE, n * PACKED + (j + 1) * TILE)
+            packed[:, lines, :] = totals[n].astype(BF16).reshape(EXPERTS, TILE, width)
 
 
 def experts_body(*refs):
-    got, weights, beside = refs[0], list(refs[1 : 3 * SHARDS - 2]), refs[3 * SHARDS - 2]
-    weights += [beside.at[i] for i in range(3)]
+    got, weights = refs[0], refs[1 : 1 + SHARDS]
     back, rows, scaled, bwd_total, fwd_total, held, ready = refs[-7:]
-    hidden = weights[0].shape[0]
-    copies = []
-    for n, w in enumerate(weights):
-        units = pl.ds(n // 3 * hidden, hidden)
-        copies.append(pltpu.make_async_copy(w, held.at[n % 3, units], ready.at[n]))
+    hidden = weights[0].shape[1]
+    copies = [
+        pltpu.make_async_copy(w, held.at[:, pl.ds(n * hidden, hidden)], ready.at[n])
+        for n, w in enumerate(weights)
+    ]
     for copy in copies:
         copy.start()
-    unpack_rows(got, rows.at[:ROWS], BWD * PACKED)
-    unpack_rows(got, rows.at[ROWS:], FWD * PACKED)
-    unpack_rows(got, scaled, SCALED * PACKED)
+    unpack_rows(got, {BWD: rows.at[:ROWS], FWD: rows.at[ROWS:], SCALED: scaled})
     for copy in copies:
         copy.wait()
     gate, up, down = held.at[0], held.at[1], held.at[2]
@@ -254,45 +258,42 @@
     dup = (dact * (gate_back * sigma)).astype(BF16)
     bwd_total[...] = (dot(dgate, gate[...]) + dot(dup, up[...])).astype(BF16)
     fwd_total[...] = dot(act, down[...]).astype(BF16)
-    pack_rows(bwd_total, back, BWD_BACK * PACKED)
-    pack_rows(fwd_total, back, FWD_BACK * PACKED)
-
-
-def experts_of(got, weights, beside, after):
+    pack_rows({BWD_BACK: bwd_total, FWD_BACK: fwd_total}, back)
+
+
+def experts_of(got, weights, after):
     width = got.shape[2] * CHUNKS
     scratch = [
         pltpu.VMEM((2 * ROWS, width), BF16),
         pltpu.VMEM((ROWS, width), BF16),
         pltpu.VMEM((ROWS, width), BF16),
         pltpu.VMEM((ROWS, width), BF16),
-        pltpu.VMEM((3, SHARDS * weights[0].shape[0], width), BF16),
-        pltpu.SemaphoreType.DMA((3 * SHARDS,)),
+        pltpu.VMEM((3, SHARDS * weights[0].shape[1], width), BF16),
+        pltpu.SemaphoreType.DMA((SHARDS,)),
     ]
     return pl.pallas_call(
         experts_body,
         out_shape=jax.ShapeDtypeStruct((EXPERTS, 2 * PACKED, got.shape[2]), BF16),
-        in_specs=[pl.BlockSpec()] + [HBM] * (len(weights) + 2),
+        in_specs=[pl.BlockSpec()] + [HBM] * (len(weights) + 1),
         scratch_shapes=scratch,
         compiler_params=pltpu.CompilerParams(vmem_limit_bytes=60 * 2**20),
         cost_estimate=cost(8_000_000_000, 14_000_000),
-    )(got, *weights, beside, after)
-
-
-def stack_body(gate, up, down, after, out):
-    del after
+    )(got, *weights, after)
+
+
+def stack_body(gate, up, down, out):
     out[0] = gate[...]
     out[1] = up[...]
     out[2] = down[...]
 
 
-def stack(arrays, after):
+def stack(*arrays):
     return pl.pallas_call(
         stack_body,
         out_shape=jax.ShapeDtypeStruct((3,) + arrays[0].shape, BF16),
-        in_specs=[pl.BlockSpec()] * 3 + [HBM],
         compiler_params=pltpu.CompilerParams(vmem_limit_bytes=60 * 2**20),
         cost_estimate=cost(0, 5_000_000),
-    )(*arrays, after)
+    )(*arrays)
 
 
 def mark_body(ids, out):
@@ -329,18 +330,15 @@
     sections = lax.axis_size("section")
     edges = jnp.stack([section_at == 0, section_at == sections - 1]).astype(jnp.int32)
     routes = (bwd_ids[0].T, bwd_gates[0].T, fwd_ids[0].T, fwd_gates[0].T)
-    own = [w_gate[0].T, w_up[0].T, w_down[0]]
-
     arriving = from_behind(bwd_grad[0], "section", -1)
     shifted = from_behind(fwd_act[0], "section", 1)
-    across = [swap(x, "half") for x in own]
-    beyond = [swap(x, "core") for x in across]
+    own = stack(w_gate[0].T, w_up[0].T, w_down[0])
+    across = swap(own, "half")
+    weights = [own, swap(own, "core"), across, swap(across, "core")]
 
     states = (bwd_input[0], bwd_grad[0], arriving, fwd_act[0], shifted)
-    sent = pick(edges, routes, states)
-    beside = swap(stack(own, sent), "core")
-    got = exchange(sent)
-    back = exchange(experts_of(got, own + across + beyond, beside, mark(routes[0])))
+    got = exchange(pick(edges, routes, states))
+    back = exchange(experts_of(got, weights, mark(routes[0])))
     routed_out, input_grad = combine(routes, back)
     return (routed_out[None], input_grad[None])
 

time: 171 us -> 173 us (1.012); the launches traced: 169 us -> 173 us
  waiting for transfers between devices: 38.2 us -> 53.1 us
  starting transfers between devices: 63 us -> 51.4 us
    ppermute x7 -> x3, waiting for transfers between devices: 0.92 us -> 19.3 us  [swap(): return lax.ppermute(x, axis, [(0, 1), (1, 0)])]
    ppermute x7 -> x3, starting transfers between devices: 39.9 us -> 30.7 us  [swap(): return lax.ppermute(x, axis, [(0, 1), (1, 0)])]
    all_to_all x1, waiting for transfers between devices: 31.5 us -> 28.1 us  [exchange(): lax.all_to_all(x, ('plane', 'pair'), split_axis=0, concat_axis=0, tiled=T...]
  transfers between devices with their start and end apart: 10 -> 6, of which waited for: 4 -> 4; matrix products, arithmetic and copies ran while one was open for 0% -> 0% of each run, Pallas kernels for 6% -> 4%
where the time goes in v5:
time: 173 us
  waiting for transfers between devices  53.1 us (31%)
  starting transfers between devices  51.4 us (30%)
  blocking collectives  40.5 us (23%)
  Pallas kernels  25.6 us (15%)
    all_to_all x1, blocking collectives, exchange(): lax.all_to_all(x, ('plane', 'pair'), split_axis=0, concat_axis=0, tiled=T...  40.5 us
    ppermute x3, starting transfers between devices, swap(): return lax.ppermute(x, axis, [(0, 1), (1, 0)])  30.7 us
    all_to_all x1, waiting for transfers between devices, exchange(): lax.all_to_all(x, ('plane', 'pair'), split_axis=0, concat_axis=0, tiled=T...  28.1 us
    ppermute x3, waiting for transfers between devices, swap(): return lax.ppermute(x, axis, [(0, 1), (1, 0)])  19.3 us
    all_to_all x1, starting transfers between devices, exchange(): lax.all_to_all(x, ('plane', 'pair'), split_axis=0, concat_axis=0, tiled=T...  16.2 us
    pallas_call x1, Pallas kernels, experts_of(): pl.pallas_call(experts_body, out_shape=jax.ShapeDtypeStruct((EXPERTS, 2 *...  12.6 us
    ppermute x2, waiting for transfers between devices, from_behind(): return lax.ppermute(x, axis, pairs)  5.66 us
    pallas_call x1, Pallas kernels, pick(): pl.pallas_call(pick_body, out_shape=jax.ShapeDtypeStruct(out, BF16), in_s...  4.86 us
  transfers between devices with their start and end apart: 6, of which 4 were waited for; matrix products, arithmetic and copies ran while one was open for 0% of the time, Pallas kernels for 4%

profile of v5, /device:TPU:1, one launch (start us, length us, event | category | flops | bytes accessed | tf_op | source)
XLA Modules:
  0.0 172.8 jit_solution(3071026740256193228)
XLA Ops:
  0.6 0.0 copy-start.1
  0.6 0.0 copy-start
  0.7 3.3 %shard_map.114.refs_1_ = bf16[3,192,2048]{2,1,0:T(8,128)(2,1)} custom-call(bf16[192,2048]{1,0:T(8,128)(2,1)} %bitcast.26, bf16[192,2048]{1,0:T(8,128)(2,1)} %bitcast.27, bf16[192,2048]{1,0:T(8,128)(2,1)} %bitcast.28), custom_call_target="tpu_custom_call" | custom-call | bytes 5000000 | tf_op jit(solution)/shard_map/pallas_call | solution.py:291
  3.9 4.0 %collective-permute-start.3 = (bf16[3,192,2048]{2,1,0:T(8,128)(2,1)}, bf16[3,192,2048]{2,1,0:T(8,128)(2,1)}, u32[]{:S(2)}, u32[]{:S(2)}) collective-permute-start(bf16[3,192,2048]{2,1,0:T(8,128)(2,1)} %shard_map.114.refs_1_), channel_id=1, source_target_pairs={{0,2},{2,0},{1,3},{3,1},{4,6},{6,4},{5,7},{7,5},{8,10},{10,8},{9,1... | collective-permute-start | bytes 7077896 | tf_op jit(solution)/shard_map/ppermute | solution.py:319
  7.9 0.0 copy-done.1
  7.9 3.1 %collective-permute-start.1 = (bf16[128,2048]{1,0:T(8,128)(2,1)S(1)}, bf16[128,2048]{1,0:T(8,128)(2,1)S(1)}, u32[]{:S(2)}, u32[]{:S(2)}) collective-permute-start(bf16[128,2048]{1,0:T(8,128)(2,1)S(1)} %bitcast.33), channel_id=1, source_target_pairs={{0,64},{64,128},{128,192},{192,256},{256,320},{320,384},{384,448},... | collective-permute-start | bytes 1572872 | tf_op jit(solution)/shard_map/ppermute | solution.py:315
  11.1 0.0 copy-done
  11.1 1.3 collective-permute-start
  12.4 4.8 %collective-permute-start.2 = (bf16[3,192,2048]{2,1,0:T(8,128)(2,1)}, bf16[3,192,2048]{2,1,0:T(8,128)(2,1)}, u32[]{:S(2)}, u32[]{:S(2)}) collective-permute-start(bf16[3,192,2048]{2,1,0:T(8,128)(2,1)} %shard_map.114.refs_1_), channel_id=1, source_target_pairs={{0,1},{1,0},{2,3},{3,2},{4,5},{5,4},{6,7},{7,6},{8,9},{9,8},{10,11... | collective-permute-start | bytes 7077896 | tf_op jit(solution)/shard_map/ppermute | solution.py:319
  17.3 0.6 add_convert_fusion.edges
  17.9 1.7 collective-permute-done.1.refs_4_
  19.6 4.0 %collective-permute-done.refs_2_ = bf16[128,2048]{1,0:T(8,128)(2,1)S(1)} collective-permute-done((bf16[128,2048]{1,0:T(8,128)(2,1)S(1)}, bf16[128,2048]{1,0:T(8,128)(2,1)S(1)}, u32[]{:S(2)}, u32[]{:S(2)}) %collective-permute-start) | collective-permute-done | bytes 524320 | tf_op jit(solution)/shard_map/ppermute | solution.py:315
  23.6 0.8 copy-done.3
  24.4 4.9 %shard_map.113 = bf16[16,240,256]{2,1,0:T(8,128)(2,1)} custom-call(s32[2]{0:T(128)} %add_convert_fusion.edges, s32[8,128]{1,0:T(8,128)} %bitcast.34, f32[8,128]{1,0:T(8,128)} %bitcast.37, s32[8,128]{1,0:T(8,128)} %bitcast.39, f32[8,128]{1,0:T(8,128)} %bitcast.41, bf16[128,2048]{1,0:T(8,128)(2,1)} %bitcast.29, bf16[128,2048]{1,0:T(8,128)(2,1)} %bitcast.30, ...), custom_call_target="tpu_custom_call" | custom-call | flops 1600000000 | bytes 5000000 | tf_op jit(solution)/shard_map/pallas_call | solution.py:142
  29.3 16.2 %all-to-all-start = ((bf16[16,240,256]{2,1,0:T(8,128)(2,1)}), bf16[16,240,256]{2,1,0:T(8,128)(2,1)}, u32[]{:S(2)}, u32[]{:S(2)}) async-start(bf16[16,240,256]{2,1,0:T(8,128)(2,1)} %shard_map.113), calls=%async_computation | async-start | bytes 3932160 | tf_op jit(solution)/shard_map/all_to_all | solution.py:323
  45.5 19.3 %collective-permute-done.3.refs_3_ = bf16[3,192,2048]{2,1,0:T(8,128)(2,1)} collective-permute-done((bf16[3,192,2048]{2,1,0:T(8,128)(2,1)}, bf16[3,192,2048]{2,1,0:T(8,128)(2,1)}, u32[]{:S(2)}, u32[]{:S(2)}) %collective-permute-start.3) | collective-permute-done | bytes 2359328 | tf_op jit(solution)/shard_map/ppermute | solution.py:319
  64.8 21.8 %collective-permute-start.4 = (bf16[3,192,2048]{2,1,0:T(8,128)(2,1)}, bf16[3,192,2048]{2,1,0:T(8,128)(2,1)}, u32[]{:S(2)}, u32[]{:S(2)}) collective-permute-start(bf16[3,192,2048]{2,1,0:T(8,128)(2,1)} %collective-permute-done.3.refs_3_), channel_id=1, source_target_pairs={{0,1},{1,0},{2,3},{3,2},{4,5},{5,4},{6,7},{7,6},{8,9},{9,8},{10,11... | collective-permute-start | bytes 7077896 | tf_op jit(solution)/shard_map/ppermute | solution.py:319
  86.6 1.3 shard_map.115.refs_5_
  87.9 0.0 collective-permute-done.2.refs_2_
  87.9 28.1 %all-to-all-done.refs_0_ = bf16[16,240,256]{2,1,0:T(8,128)(2,1)} async-done(((bf16[16,240,256]{2,1,0:T(8,128)(2,1)}), bf16[16,240,256]{2,1,0:T(8,128)(2,1)}, u32[]{:S(2)}, u32[]{:S(2)}) %all-to-all-start) | async-done | bytes 1966112 | tf_op jit(solution)/shard_map/all_to_all | solution.py:323
  116.1 0.0 collective-permute-done.4.refs_4_
  116.1 12.6 %shard_map.116 = bf16[16,160,256]{2,1,0:T(8,128)(2,1)} custom-call(bf16[16,240,256]{2,1,0:T(8,128)(2,1)} %all-to-all-done.refs_0_, bf16[3,192,2048]{2,1,0:T(8,128)(2,1)} %shard_map.114.refs_1_, bf16[3,192,2048]{2,1,0:T(8,128)(2,1)} %collective-permute-done.2.refs_2_, bf16[3,192,2048]{2,1,0:T(8,128)(2,1)} %collective-permute-done.3.refs_3_, ...), custom_call_target="tpu_custom_call" | custom-call | flops 8000000000 | bytes 14000000 | tf_op jit(solution)/shard_map/pallas_call | solution.py:274
  128.7 40.5 %all_to_all.10.back = bf16[16,160,256]{2,1,0:T(8,128)(2,1)} all-to-all(bf16[16,160,256]{2,1,0:T(8,128)(2,1)} %shard_map.116), channel_id=1, replica_groups=mesh['section'=8,'plane'=4,'pair'=4,'half'=2,'core'=2] {'plane','pair'}, dimensions={0} | all-to-all | bytes 2621440 | tf_op jit(solution)/shard_map/all_to_all | solution.py:323
  169.2 3.6 %shard_map.117 = (bf16[128,2048]{1,0:T(8,128)(2,1)}, bf16[128,2048]{1,0:T(8,128)(2,1)}) custom-call(s32[8,128]{1,0:T(8,128)} %bitcast.36, f32[8,128]{1,0:T(8,128)} %bitcast.38, s32[8,128]{1,0:T(8,128)} %bitcast.40, f32[8,128]{1,0:T(8,128)} %bitcast.42, bf16[16,160,256]{2,1,0:T(8,128)(2,1)} %all_to_all.10.back), custom_call_target="tpu_custom_call" | custom-call | flops 800000000 | bytes 4000000 | tf_op jit(solution)/shard_map/pallas_call | solution.py:192
  (3 shorter events, 0.0 us)
Async XLA Ops:
  0.6 7.3 %copy-start.1 = (bf16[1,128,2048]{2,1,0:T(8,128)(2,1)S(1)}, bf16[1,128,2048]{2,1,0:T(8,128)(2,1)}, u32[]{:S(2)}) copy-start(bf16[1,128,2048]{2,1,0:T(8,128)(2,1)} %param.10) | copy-start | bytes 1572868
  0.6 10.5 %copy-start = (bf16[1,128,2048]{2,1,0:T(8,128)(2,1)S(1)}, bf16[1,128,2048]{2,1,0:T(8,128)(2,1)}, u32[]{:S(2)}) copy-start(bf16[1,128,2048]{2,1,0:T(8,128)(2,1)} %param.16) | copy-start | bytes 1572868
  3.9 60.9 %collective-permute-start.3 = (bf16[3,192,2048]{2,1,0:T(8,128)(2,1)}, bf16[3,192,2048]{2,1,0:T(8,128)(2,1)}, u32[]{:S(2)}, u32[]{:S(2)}) collective-permute-start(bf16[3,192,2048]{2,1,0:T(8,128)(2,1)} %shard_map.114.refs_1_), channel_id=1, source_target_pairs={{0,2},{2,0},{1,3},{3,1},{4,6},{6,4},{5,7},{7,5},{8,10},{10,8},{9,1... | collective-permute-start | bytes 7077896 | tf_op jit(solution)/shard_map/ppermute | solution.py:319
  7.9 11.7 %collective-permute-start.1 = (bf16[128,2048]{1,0:T(8,128)(2,1)S(1)}, bf16[128,2048]{1,0:T(8,128)(2,1)S(1)}, u32[]{:S(2)}, u32[]{:S(2)}) collective-permute-start(bf16[128,2048]{1,0:T(8,128)(2,1)S(1)} %bitcast.33), channel_id=1, source_target_pairs={{0,64},{64,128},{128,192},{192,256},{256,320},{320,384},{384,448},... | collective-permute-start | bytes 1572872 | tf_op jit(solution)/shard_map/ppermute | solution.py:315
  11.1 12.5 %collective-permute-start = (bf16[128,2048]{1,0:T(8,128)(2,1)S(1)}, bf16[128,2048]{1,0:T(8,128)(2,1)S(1)}, u32[]{:S(2)}, u32[]{:S(2)}) collective-permute-start(bf16[128,2048]{1,0:T(8,128)(2,1)S(1)} %bitcast.31), channel_id=1, source_target_pairs={{64,0},{128,64},{192,128},{256,192},{320,256},{384,320},{448,384},... | collective-permute-start | bytes 1572872 | tf_op jit(solution)/shard_map/ppermute | solution.py:315
  12.4 75.5 %collective-permute-start.2 = (bf16[3,192,2048]{2,1,0:T(8,128)(2,1)}, bf16[3,192,2048]{2,1,0:T(8,128)(2,1)}, u32[]{:S(2)}, u32[]{:S(2)}) collective-permute-start(bf16[3,192,2048]{2,1,0:T(8,128)(2,1)} %shard_map.114.refs_1_), channel_id=1, source_target_pairs={{0,1},{1,0},{2,3},{3,2},{4,5},{5,4},{6,7},{7,6},{8,9},{9,8},{10,11... | collective-permute-start | bytes 7077896 | tf_op jit(solution)/shard_map/ppermute | solution.py:319
  19.6 4.0 %copy-start.2 = (bf16[128,2048]{1,0:T(8,128)(2,1)}, bf16[128,2048]{1,0:T(8,128)(2,1)S(1)}, u32[]{:S(2)}) copy-start(bf16[128,2048]{1,0:T(8,128)(2,1)S(1)} %collective-permute-done.1.refs_4_) | copy-start | bytes 1572868
  23.6 0.8 copy-start.3
  29.3 86.8 %all-to-all-start = ((bf16[16,240,256]{2,1,0:T(8,128)(2,1)}), bf16[16,240,256]{2,1,0:T(8,128)(2,1)}, u32[]{:S(2)}, u32[]{:S(2)}) async-start(bf16[16,240,256]{2,1,0:T(8,128)(2,1)} %shard_map.113), calls=%async_computation | async-start | bytes 3932160 | tf_op jit(solution)/shard_map/all_to_all | solution.py:323
  64.8 51.3 %collective-permute-start.4 = (bf16[3,192,2048]{2,1,0:T(8,128)(2,1)}, bf16[3,192,2048]{2,1,0:T(8,128)(2,1)}, u32[]{:S(2)}, u32[]{:S(2)}) collective-permute-start(bf16[3,192,2048]{2,1,0:T(8,128)(2,1)} %collective-permute-done.3.refs_3_), channel_id=1, source_target_pairs={{0,1},{1,0},{2,3},{3,2},{4,5},{5,4},{6,7},{7,6},{8,9},{9,8},{10,11... | collective-permute-start | bytes 7077896 | tf_op jit(solution)/shard_map/ppermute | solution.py:319

commit v6 on v5

--- a/solution.py
+++ b/solution.py
@@ -20,7 +20,7 @@
 NONE = -100.0
 MARK_FLOPS = 200_000_000_000
 
-BWD, SCALED, FWD = 0, 1, 2
+SCALED, FWD = 0, 1
 BWD_BACK, FWD_BACK = 0, 1
 
 MEETS = [
@@ -99,8 +99,23 @@
         out[:, j * TILE : (j + 1) * TILE, :] = total.astype(BF16).reshape(EXPERTS, TILE, width)
 
 
+def pick_first_body(ids, gates, states, out):
+    key, _ = keys_by_expert(ids, gates)
+    pick_rows(key, None, states, out)
+
+
+def pick_first(routes, states):
+    out = (EXPERTS, PACKED, states.shape[1] // CHUNKS)
+    return pl.pallas_call(
+        pick_first_body,
+        out_shape=jax.ShapeDtypeStruct(out, BF16),
+        compiler_params=pltpu.CompilerParams(vmem_limit_bytes=60 * 2**20),
+        cost_estimate=cost(400_000_000, 1_500_000),
+    )(*routes, states)
+
+
 def pick_body(edges, bwd_ids, bwd_gates, fwd_ids, fwd_gates, *refs):
-    bwd_input, bwd_grad, arriving, fwd_act, shifted = refs[:5]
+    bwd_grad, arriving, fwd_act, shifted = refs[:4]
     out, states, packed, read, written = refs[-5:]
 
     def fetch(source, n):
@@ -119,40 +134,35 @@
         lines = pl.ds(n * PACKED, PACKED)
         return pltpu.make_async_copy(packed.at[n], out.at[:, lines, :], written.at[n])
 
-    fetch(bwd_input, BWD).start()
     fetch_one_of(edges[1], bwd_grad, arriving, SCALED)
     fetch_one_of(edges[0], fwd_act, shifted, FWD)
     bwd_key, bwd_gate = keys_by_expert(bwd_ids, bwd_gates)
     fwd_key, _ = keys_by_expert(fwd_ids, fwd_gates)
-    for n, key, gate in (
-        (BWD, bwd_key, None),
-        (SCALED, bwd_key, bwd_gate),
-        (FWD, fwd_key, None),
-    ):
-        fetch(bwd_input, n).wait()
+    for n, key, gate in ((SCALED, bwd_key, bwd_gate), (FWD, fwd_key, None)):
+        fetch(bwd_grad, n).wait()
         pick_rows(key, gate, states.at[n], packed.at[n])
         store(n).start()
-    for n in (BWD, SCALED, FWD):
+    for n in (SCALED, FWD):
         store(n).wait()
 
 
-def pick(edges, routes, states):
+def pick(edges, routes, states, after):
     tokens, width = states[0].shape
-    out = (EXPERTS, 3 * PACKED, width // CHUNKS)
+    out = (EXPERTS, 2 * PACKED, width // CHUNKS)
     return pl.pallas_call(
         pick_body,
         out_shape=jax.ShapeDtypeStruct(out, BF16),
-        in_specs=[SMEM] + [pl.BlockSpec()] * 4 + [HBM] * len(states),
+        in_specs=[SMEM] + [pl.BlockSpec()] * 4 + [HBM] * (len(states) + 1),
         out_specs=HBM,
         scratch_shapes=[
-            pltpu.VMEM((3, tokens, width), BF16),
-            pltpu.VMEM((3, EXPERTS, PACKED, width // CHUNKS), BF16),
-            pltpu.SemaphoreType.DMA((3,)),
-            pltpu.SemaphoreType.DMA((3,)),
+            pltpu.VMEM((2, tokens, width), BF16),
+            pltpu.VMEM((2, EXPERTS, PACKED, width // CHUNKS), BF16),
+            pltpu.SemaphoreType.DMA((2,)),
+            pltpu.SemaphoreType.DMA((2,)),
         ],
         compiler_params=pltpu.CompilerParams(vmem_limit_bytes=60 * 2**20),
-        cost_estimate=cost(1_600_000_000, 5_000_000),
-    )(edges, *routes, *states)
+        cost_estimate=cost(1_200_000_000, 4_000_000),
+    )(edges, *routes, *states, after)
 
 
 def combine_rows(weighted, ids, gates, back, base, out, turn):
@@ -203,19 +213,19 @@
     return jnp.where((slot >= 0) & (slot < CAP), slot - line, int(NONE)).astype(F32)
 
 
-def unpack_rows(packed, arrays):
-    width = packed.shape[2]
+def unpack_rows(parts):
+    width = parts[0][0].shape[2]
     lane = iota((ROWS, SPAN), 1)
     place = places(lane // TILE, lax.rem(lane, TILE), iota((ROWS, SPAN), 0))
     for c in range(CHUNKS):
-        totals = {n: jnp.zeros((ROWS, width), F32) for n in arrays}
+        totals = [jnp.zeros((ROWS, width), F32) for _ in parts]
         for j, _, shift in [m for m in MEETS if m[1] == c]:
             hit = one_where(place, shift)
-            for n in arrays:
+            for i, (packed, n, _) in enumerate(parts):
                 lines = slice(n * PACKED + j * TILE, n * PACKED + (j + 1) * TILE)
-                totals[n] = totals[n] + dot(hit, packed[:, lines, :].reshape(SPAN, width))
-        for n, rows in arrays.items():
-            rows[:, c * width : (c + 1) * width] = totals[n].astype(BF16)
+                totals[i] = totals[i] + dot(hit, packed[:, lines, :].reshape(SPAN, width))
+        for total, (_, _, rows) in zip(totals, parts):
+            rows[:, c * width : (c + 1) * width] = total.astype(BF16)
 
 
 def pack_rows(arrays, packed):
@@ -234,16 +244,20 @@
 
 
 def experts_body(*refs):
-    got, weights = refs[0], refs[1 : 1 + SHARDS]
+    first, got, beside = refs[0], refs[1], refs[3 * SHARDS - 1]
+    weights = list(refs[2 : 3 * SHARDS - 1])
+    weights += [beside.at[i] for i in range(3)]
     back, rows, scaled, bwd_total, fwd_total, held, ready = refs[-7:]
-    hidden = weights[0].shape[1]
-    copies = [
-        pltpu.make_async_copy(w, held.at[:, pl.ds(n * hidden, hidden)], ready.at[n])
-        for n, w in enumerate(weights)
-    ]
+    hidden = weights[0].shape[0]
+    copies = []
+    for n, w in enumerate(weights):
+        units = pl.ds(n // 3 * hidden, hidden)
+        copies.append(pltpu.make_async_copy(w, held.at[n % 3, units], ready.at[n]))
     for copy in copies:
         copy.start()
-    unpack_rows(got, {BWD: rows.at[:ROWS], FWD: rows.at[ROWS:], SCALED: scaled})
+    unpack_rows(
+        [(first, 0, rows.at[:ROWS]), (got, SCALED, scaled), (got, FWD, rows.at[ROWS:])]
+    )
     for copy in copies:
         copy.wait()
     gate, up, down = held.at[0], held.at[1], held.at[2]
@@ -261,39 +275,58 @@
     pack_rows({BWD_BACK: bwd_total, FWD_BACK: fwd_total}, back)
 
 
-def experts_of(got, weights, after):
+def experts_of(first, got, weights, beside, after):
     width = got.shape[2] * CHUNKS
     scratch = [
         pltpu.VMEM((2 * ROWS, width), BF16),
         pltpu.VMEM((ROWS, width), BF16),
         pltpu.VMEM((ROWS, width), BF16),
         pltpu.VMEM((ROWS, width), BF16),
-        pltpu.VMEM((3, SHARDS * weights[0].shape[1], width), BF16),
-        pltpu.SemaphoreType.DMA((SHARDS,)),
+        pltpu.VMEM((3, SHARDS * weights[0].shape[0], width), BF16),
+        pltpu.SemaphoreType.DMA((3 * SHARDS,)),
     ]
     return pl.pallas_call(
         experts_body,
         out_shape=jax.ShapeDtypeStruct((EXPERTS, 2 * PACKED, got.shape[2]), BF16),
-        in_specs=[pl.BlockSpec()] + [HBM] * (len(weights) + 1),
+        in_specs=[pl.BlockSpec()] * 2 + [HBM] * (len(weights) + 2),
         scratch_shapes=scratch,
         compiler_params=pltpu.CompilerParams(vmem_limit_bytes=60 * 2**20),
         cost_estimate=cost(8_000_000_000, 14_000_000),
-    )(got, *weights, after)
-
-
-def stack_body(gate, up, down, out):
+    )(first, got, *weights, beside, after)
+
+
+def hold_body(*refs):
+    del refs
+
+
+def hold(arrays, first):
+    n = len(arrays)
+    return list(
+        pl.pallas_call(
+            hold_body,
+            out_shape=[jax.ShapeDtypeStruct(x.shape, x.dtype) for x in arrays],
+            in_specs=[HBM] * (n + 1),
+            out_specs=[HBM] * n,
+            input_output_aliases={i: i for i in range(n)},
+        )(*arrays, first)
+    )
+
+
+def stack_body(gate, up, down, after, out):
+    del after
     out[0] = gate[...]
     out[1] = up[...]
     out[2] = down[...]
 
 
-def stack(*arrays):
+def stack(arrays, after):
     return pl.pallas_call(
         stack_body,
         out_shape=jax.ShapeDtypeStruct((3,) + arrays[0].shape, BF16),
+        in_specs=[pl.BlockSpec()] * 3 + [HBM],
         compiler_params=pltpu.CompilerParams(vmem_limit_bytes=60 * 2**20),
         cost_estimate=cost(0, 5_000_000),
-    )(*arrays)
+    )(*arrays, after)
 
 
 def mark_body(ids, out):
@@ -332,13 +365,17 @@
     routes = (bwd_ids[0].T, bwd_gates[0].T, fwd_ids[0].T, fwd_gates[0].T)
     arriving = from_behind(bwd_grad[0], "section", -1)
     shifted = from_behind(fwd_act[0], "section", 1)
-    own = stack(w_gate[0].T, w_up[0].T, w_down[0])
-    across = swap(own, "half")
-    weights = [own, swap(own, "core"), across, swap(across, "core")]
-
-    states = (bwd_input[0], bwd_grad[0], arriving, fwd_act[0], shifted)
-    got = exchange(pick(edges, routes, states))
-    back = exchange(experts_of(got, weights, mark(routes[0])))
+    own = [w_gate[0].T, w_up[0].T, w_down[0]]
+    sending = mark(routes[0])
+    across = hold([swap(x, "half") for x in own], sending)
+    beyond = [swap(x, "core") for x in across]
+
+    first = exchange(pick_first(routes[:2], bwd_input[0]))
+    states = (bwd_grad[0], arriving, fwd_act[0], shifted)
+    sent = pick(edges, routes, states, mark(routes[2]))
+    beside = swap(stack(own, sent), "core")
+    got = exchange(sent)
+    back = exchange(experts_of(first, got, own + across + beyond, beside, sending))
     routed_out, input_grad = combine(routes, back)
     return (routed_out[None], input_grad[None])
 

time: 173 us -> 194 us (1.12)
  the two profiles are of different devices: /device:TPU:1 before, /device:TPU:40 now
where the time goes in v6:
time: 194 us; the launch traced here: 193 us
  waiting for transfers between devices  68.5 us (35%)
  starting transfers between devices  50 us (26%)
  blocking collectives  44.6 us (23%)
  Pallas kernels  28.9 us (15%)
    all_to_all x2, waiting for transfers between devices, exchange(): lax.all_to_all(x, ('plane', 'pair'), split_axis=0, concat_axis=0, tiled=T...  66.1 us
    all_to_all x1, blocking collectives, exchange(): lax.all_to_all(x, ('plane', 'pair'), split_axis=0, concat_axis=0, tiled=T...  44.6 us
    all_to_all x2, starting transfers between devices, exchange(): lax.all_to_all(x, ('plane', 'pair'), split_axis=0, concat_axis=0, tiled=T...  26.1 us
    ppermute x7, starting transfers between devices, swap(): return lax.ppermute(x, axis, [(0, 1), (1, 0)])  17.3 us
    pallas_call x1, Pallas kernels, experts_of(): pl.pallas_call(experts_body, out_shape=jax.ShapeDtypeStruct((EXPERTS, 2 *...  12.5 us
    ppermute x2, starting transfers between devices, from_behind(): return lax.ppermute(x, axis, pairs)  6.63 us
    pallas_call x1, Pallas kernels, pick(): pl.pallas_call(pick_body, out_shape=jax.ShapeDtypeStruct(out, BF16), in_s...  4.32 us
  transfers between devices with their start and end apart: 11, of which 4 were waited for; matrix products, arithmetic and copies ran while one was open for 0% of the time, Pallas kernels for 7%

profile of v6, /device:TPU:40, one launch (start us, length us, event | category | flops | bytes accessed | tf_op | source)
XLA Modules:
  0.0 193.4 jit_solution(15706921004488064932)
XLA Ops:
  0.6 1.3 collective-permute-start
  1.9 5.3 %collective-permute-start.1 = (bf16[128,2048]{1,0:T(8,128)(2,1)}, bf16[128,2048]{1,0:T(8,128)(2,1)}, u32[]{:S(2)}, u32[]{:S(2)}) collective-permute-start(bf16[128,2048]{1,0:T(8,128)(2,1)} %bitcast.38), channel_id=1, source_target_pairs={{0,64},{64,128},{128,192},{192,256},{256,320},{320,384},{384,448},... | collective-permute-start | bytes 1572872 | tf_op jit(solution)/shard_map/ppermute | solution.py:348
  7.3 3.2 %collective-permute-start.2 = (bf16[192,2048]{1,0:T(8,128)(2,1)}, bf16[192,2048]{1,0:T(8,128)(2,1)}, u32[]{:S(2)}, u32[]{:S(2)}) collective-permute-start(bf16[192,2048]{1,0:T(8,128)(2,1)} %bitcast.26), channel_id=1, source_target_pairs={{0,2},{2,0},{1,3},{3,1},{4,6},{6,4},{5,7},{7,5},{8,10},{10,8},{9,1... | collective-permute-start | bytes 2359304 | tf_op jit(solution)/shard_map/ppermute | solution.py:352
  10.5 2.6 %collective-permute-start.3 = (bf16[192,2048]{1,0:T(8,128)(2,1)}, bf16[192,2048]{1,0:T(8,128)(2,1)}, u32[]{:S(2)}, u32[]{:S(2)}) collective-permute-start(bf16[192,2048]{1,0:T(8,128)(2,1)} %bitcast.29), channel_id=1, source_target_pairs={{0,2},{2,0},{1,3},{3,1},{4,6},{6,4},{5,7},{7,5},{8,10},{10,8},{9,1... | collective-permute-start | bytes 2359304 | tf_op jit(solution)/shard_map/ppermute | solution.py:352
  13.1 3.3 %collective-permute-start.4 = (bf16[192,2048]{1,0:T(8,128)(2,1)}, bf16[192,2048]{1,0:T(8,128)(2,1)}, u32[]{:S(2)}, u32[]{:S(2)}) collective-permute-start(bf16[192,2048]{1,0:T(8,128)(2,1)} %bitcast.32), channel_id=1, source_target_pairs={{0,2},{2,0},{1,3},{3,1},{4,6},{6,4},{5,7},{7,5},{8,10},{10,8},{9,1... | collective-permute-start | bytes 2359304 | tf_op jit(solution)/shard_map/ppermute | solution.py:352
  16.4 2.6 %shard_map.113 = bf16[16,80,256]{2,1,0:T(8,128)(2,1)} custom-call(s32[8,128]{1,0:T(8,128)} %bitcast.40, f32[8,128]{1,0:T(8,128)} %bitcast.44, bf16[128,2048]{1,0:T(8,128)(2,1)} %bitcast.35), custom_call_target="tpu_custom_call" | custom-call | flops 400000000 | bytes 1500000 | tf_op jit(solution)/shard_map/pallas_call | solution.py:109
  19.0 15.7 %all-to-all-start = ((bf16[16,80,256]{2,1,0:T(8,128)(2,1)}), bf16[16,80,256]{2,1,0:T(8,128)(2,1)}, u32[]{:S(2)}, u32[]{:S(2)}) async-start(bf16[16,80,256]{2,1,0:T(8,128)(2,1)} %shard_map.113), calls=%async_computation | async-start | bytes 1310720 | tf_op jit(solution)/shard_map/all_to_all | solution.py:356
  34.7 1.3 shard_map.114.refs_4_
  36.0 0.7 add_convert_fusion.edges
  36.7 4.3 %shard_map.115.after = bf16[16,160,256]{2,1,0:T(8,128)(2,1)} custom-call(s32[2]{0:T(128)} %add_convert_fusion.edges, s32[8,128]{1,0:T(8,128)} %bitcast.41, f32[8,128]{1,0:T(8,128)} %bitcast.45, s32[8,128]{1,0:T(8,128)} %bitcast.48, f32[8,128]{1,0:T(8,128)} %bitcast.50, bf16[128,2048]{1,0:T(8,128)(2,1)} %bitcast.37, ...), custom_call_target="tpu_custom_call" | custom-call | flops 1200000000 | bytes 4000000 | tf_op jit(solution)/shard_map/pallas_call | solution.py:152
  41.0 3.2 %shard_map.118 = bf16[3,192,2048]{2,1,0:T(8,128)(2,1)} custom-call(bf16[192,2048]{1,0:T(8,128)(2,1)} %bitcast.27, bf16[192,2048]{1,0:T(8,128)(2,1)} %bitcast.30, bf16[192,2048]{1,0:T(8,128)(2,1)} %bitcast.33, bf16[16,160,256]{2,1,0:T(8,128)(2,1)} %shard_map.115.after), custom_call_target="tpu_custom_call" | custom-call | bytes 5000000 | tf_op jit(solution)/shard_map/pallas_call | solution.py:323
  44.2 1.9 collective-permute-start.8
  46.1 37.1 %all-to-all-done.refs_0_ = bf16[16,80,256]{2,1,0:T(8,128)(2,1)} async-done(((bf16[16,80,256]{2,1,0:T(8,128)(2,1)}), bf16[16,80,256]{2,1,0:T(8,128)(2,1)}, u32[]{:S(2)}, u32[]{:S(2)}) %all-to-all-start) | async-done | bytes 655392 | tf_op jit(solution)/shard_map/all_to_all | solution.py:356
  83.2 10.4 %all-to-all-start.1 = ((bf16[16,160,256]{2,1,0:T(8,128)(2,1)}), bf16[16,160,256]{2,1,0:T(8,128)(2,1)}, u32[]{:S(2)}, u32[]{:S(2)}) async-start(bf16[16,160,256]{2,1,0:T(8,128)(2,1)} %shard_map.115.after), calls=%async_computation.1 | async-start | bytes 2621440 | tf_op jit(solution)/shard_map/all_to_all | solution.py:356
  93.6 1.3 shard_map.116.refs_3_.refs_12_
  94.9 1.9 collective-permute-start.5
  96.9 2.4 %collective-permute-start.6 = (bf16[192,2048]{1,0:T(8,128)(2,1)}, bf16[192,2048]{1,0:T(8,128)(2,1)S(1)}, u32[]{:S(2)}, u32[]{:S(2)}) collective-permute-start(bf16[192,2048]{1,0:T(8,128)(2,1)} %get-tuple-element.8.refs_6_), channel_id=1, source_target_pairs={{0,1},{1,0},{2,3},{3,2},{4,5},{5,4},{6,7},{7,6},{8,9},{9,8},{10,11... | collective-permute-start | bytes 2359304 | tf_op jit(solution)/shard_map/ppermute | solution.py:352
  99.3 1.9 collective-permute-start.7
  101.2 0.2 collective-permute-done.6.refs_9_
  101.4 2.3 %collective-permute-done.7.refs_10_ = bf16[192,2048]{1,0:T(8,128)(2,1)S(1)} collective-permute-done((bf16[192,2048]{1,0:T(8,128)(2,1)}, bf16[192,2048]{1,0:T(8,128)(2,1)S(1)}, u32[]{:S(2)}, u32[]{:S(2)}) %collective-permute-start.7) | collective-permute-done | bytes 786464 | tf_op jit(solution)/shard_map/ppermute | solution.py:352
  103.7 28.9 %all-to-all-done.1.refs_1_ = bf16[16,160,256]{2,1,0:T(8,128)(2,1)} async-done(((bf16[16,160,256]{2,1,0:T(8,128)(2,1)}), bf16[16,160,256]{2,1,0:T(8,128)(2,1)}, u32[]{:S(2)}, u32[]{:S(2)}) %all-to-all-start.1) | async-done | bytes 1310752 | tf_op jit(solution)/shard_map/all_to_all | solution.py:356
  132.6 12.5 %shard_map.119 = bf16[16,160,256]{2,1,0:T(8,128)(2,1)} custom-call(bf16[16,80,256]{2,1,0:T(8,128)(2,1)} %all-to-all-done.refs_0_, bf16[16,160,256]{2,1,0:T(8,128)(2,1)} %all-to-all-done.1.refs_1_, bf16[192,2048]{1,0:T(8,128)(2,1)} %bitcast.28, bf16[192,2048]{1,0:T(8,128)(2,1)} %bitcast.31, bf16[192,2048]{1,0:T(8,128)(2,1)} %bitcast.34, ...), custom_call_target="tpu_custom_call" | custom-call | flops 8000000000 | bytes 14000000 | tf_op jit(solution)/shard_map/pallas_call | solution.py:288
  145.2 44.6 %all_to_all.15.back = bf16[16,160,256]{2,1,0:T(8,128)(2,1)} all-to-all(bf16[16,160,256]{2,1,0:T(8,128)(2,1)} %shard_map.119), channel_id=1, replica_groups=mesh['section'=8,'plane'=4,'pair'=4,'half'=2,'core'=2] {'plane','pair'}, dimensions={0} | all-to-all | bytes 2621440 | tf_op jit(solution)/shard_map/all_to_all | solution.py:356
  189.8 3.6 %shard_map.120 = (bf16[128,2048]{1,0:T(8,128)(2,1)}, bf16[128,2048]{1,0:T(8,128)(2,1)}) custom-call(s32[8,128]{1,0:T(8,128)} %bitcast.43, f32[8,128]{1,0:T(8,128)} %bitcast.46, s32[8,128]{1,0:T(8,128)} %bitcast.49, f32[8,128]{1,0:T(8,128)} %bitcast.51, bf16[16,160,256]{2,1,0:T(8,128)(2,1)} %all_to_all.15.back), custom_call_target="tpu_custom_call" | custom-call | flops 800000000 | bytes 4000000 | tf_op jit(solution)/shard_map/pallas_call | solution.py:202
  (14 shorter events, 0.0 us)
Async XLA Ops:
  0.6 36.0 %collective-permute-start = (bf16[128,2048]{1,0:T(8,128)(2,1)}, bf16[128,2048]{1,0:T(8,128)(2,1)}, u32[]{:S(2)}, u32[]{:S(2)}) collective-permute-start(bf16[128,2048]{1,0:T(8,128)(2,1)} %bitcast.36), channel_id=1, source_target_pairs={{64,0},{128,64},{192,128},{256,192},{320,256},{384,320},{448,384},... | collective-permute-start | bytes 1572872 | tf_op jit(solution)/shard_map/ppermute | solution.py:348
  1.9 34.7 %collective-permute-start.1 = (bf16[128,2048]{1,0:T(8,128)(2,1)}, bf16[128,2048]{1,0:T(8,128)(2,1)}, u32[]{:S(2)}, u32[]{:S(2)}) collective-permute-start(bf16[128,2048]{1,0:T(8,128)(2,1)} %bitcast.38), channel_id=1, source_target_pairs={{0,64},{64,128},{128,192},{192,256},{256,320},{320,384},{384,448},... | collective-permute-start | bytes 1572872 | tf_op jit(solution)/shard_map/ppermute | solution.py:348
  7.3 87.6 %collective-permute-start.2 = (bf16[192,2048]{1,0:T(8,128)(2,1)}, bf16[192,2048]{1,0:T(8,128)(2,1)}, u32[]{:S(2)}, u32[]{:S(2)}) collective-permute-start(bf16[192,2048]{1,0:T(8,128)(2,1)} %bitcast.26), channel_id=1, source_target_pairs={{0,2},{2,0},{1,3},{3,1},{4,6},{6,4},{5,7},{7,5},{8,10},{10,8},{9,1... | collective-permute-start | bytes 2359304 | tf_op jit(solution)/shard_map/ppermute | solution.py:352
  10.5 84.4 %collective-permute-start.3 = (bf16[192,2048]{1,0:T(8,128)(2,1)}, bf16[192,2048]{1,0:T(8,128)(2,1)}, u32[]{:S(2)}, u32[]{:S(2)}) collective-permute-start(bf16[192,2048]{1,0:T(8,128)(2,1)} %bitcast.29), channel_id=1, source_target_pairs={{0,2},{2,0},{1,3},{3,1},{4,6},{6,4},{5,7},{7,5},{8,10},{10,8},{9,1... | collective-permute-start | bytes 2359304 | tf_op jit(solution)/shard_map/ppermute | solution.py:352
  13.1 81.8 %collective-permute-start.4 = (bf16[192,2048]{1,0:T(8,128)(2,1)}, bf16[192,2048]{1,0:T(8,128)(2,1)}, u32[]{:S(2)}, u32[]{:S(2)}) collective-permute-start(bf16[192,2048]{1,0:T(8,128)(2,1)} %bitcast.32), channel_id=1, source_target_pairs={{0,2},{2,0},{1,3},{3,1},{4,6},{6,4},{5,7},{7,5},{8,10},{10,8},{9,1... | collective-permute-start | bytes 2359304 | tf_op jit(solution)/shard_map/ppermute | solution.py:352
  19.0 64.2 %all-to-all-start = ((bf16[16,80,256]{2,1,0:T(8,128)(2,1)}), bf16[16,80,256]{2,1,0:T(8,128)(2,1)}, u32[]{:S(2)}, u32[]{:S(2)}) async-start(bf16[16,80,256]{2,1,0:T(8,128)(2,1)} %shard_map.113), calls=%async_computation | async-start | bytes 1310720 | tf_op jit(solution)/shard_map/all_to_all | solution.py:356
  44.2 59.5 %collective-permute-start.8 = (bf16[3,192,2048]{2,1,0:T(8,128)(2,1)}, bf16[3,192,2048]{2,1,0:T(8,128)(2,1)}, u32[]{:S(2)}, u32[]{:S(2)}) collective-permute-start(bf16[3,192,2048]{2,1,0:T(8,128)(2,1)} %shard_map.118), channel_id=1, source_target_pairs={{0,1},{1,0},{2,3},{3,2},{4,5},{5,4},{6,7},{7,6},{8,9},{9,8},{10,11... | collective-permute-start | bytes 7077896 | tf_op jit(solution)/shard_map/ppermute | solution.py:352
  83.2 49.4 %all-to-all-start.1 = ((bf16[16,160,256]{2,1,0:T(8,128)(2,1)}), bf16[16,160,256]{2,1,0:T(8,128)(2,1)}, u32[]{:S(2)}, u32[]{:S(2)}) async-start(bf16[16,160,256]{2,1,0:T(8,128)(2,1)} %shard_map.115.after), calls=%async_computation.1 | async-start | bytes 2621440 | tf_op jit(solution)/shard_map/all_to_all | solution.py:356
  94.9 6.3 %collective-permute-start.5 = (bf16[192,2048]{1,0:T(8,128)(2,1)}, bf16[192,2048]{1,0:T(8,128)(2,1)S(1)}, u32[]{:S(2)}, u32[]{:S(2)}) collective-permute-start(bf16[192,2048]{1,0:T(8,128)(2,1)} %get-tuple-element.7.refs_5_), channel_id=1, source_target_pairs={{0,1},{1,0},{2,3},{3,2},{4,5},{5,4},{6,7},{7,6},{8,9},{9,8},{10,11... | collective-permute-start | bytes 2359304 | tf_op jit(solution)/shard_map/ppermute | solution.py:352
  96.9 4.5 %collective-permute-start.6 = (bf16[192,2048]{1,0:T(8,128)(2,1)}, bf16[192,2048]{1,0:T(8,128)(2,1)S(1)}, u32[]{:S(2)}, u32[]{:S(2)}) collective-permute-start(bf16[192,2048]{1,0:T(8,128)(2,1)} %get-tuple-element.8.refs_6_), channel_id=1, source_target_pairs={{0,1},{1,0},{2,3},{3,2},{4,5},{5,4},{6,7},{7,6},{8,9},{9,8},{10,11... | collective-permute-start | bytes 2359304 | tf_op jit(solution)/shard_map/ppermute | solution.py:352
  99.3 4.4 %collective-permute-start.7 = (bf16[192,2048]{1,0:T(8,128)(2,1)}, bf16[192,2048]{1,0:T(8,128)(2,1)S(1)}, u32[]{:S(2)}, u32[]{:S(2)}) collective-permute-start(bf16[192,2048]{1,0:T(8,128)(2,1)} %get-tuple-element.9.refs_7_), channel_id=1, source_target_pairs={{0,1},{1,0},{2,3},{3,2},{4,5},{5,4},{6,7},{7,6},{8,9},{9,8},{10,11... | collective-permute-start | bytes 2359304 | tf_op jit(solution)/shard_map/ppermute | solution.py:352
  101.2 31.4 %copy-start = (bf16[192,2048]{1,0:T(8,128)(2,1)}, bf16[192,2048]{1,0:T(8,128)(2,1)S(1)}, u32[]{:S(2)}) copy-start(bf16[192,2048]{1,0:T(8,128)(2,1)S(1)} %collective-permute-done.5.refs_8_) | copy-start | bytes 2359300
  101.4 31.2 %copy-start.1 = (bf16[192,2048]{1,0:T(8,128)(2,1)}, bf16[192,2048]{1,0:T(8,128)(2,1)S(1)}, u32[]{:S(2)}) copy-start(bf16[192,2048]{1,0:T(8,128)(2,1)S(1)} %collective-permute-done.6.refs_9_) | copy-start | bytes 2359300
  103.7 29.0 %copy-start.2 = (bf16[192,2048]{1,0:T(8,128)(2,1)}, bf16[192,2048]{1,0:T(8,128)(2,1)S(1)}, u32[]{:S(2)}) copy-start(bf16[192,2048]{1,0:T(8,128)(2,1)S(1)} %collective-permute-done.7.refs_10_) | copy-start | bytes 2359300

commit v7 on v5

--- a/solution.py
+++ b/solution.py
@@ -234,13 +234,14 @@
 
 
 def experts_body(*refs):
-    got, weights = refs[0], refs[1 : 1 + SHARDS]
+    got, weights, beside = refs[0], list(refs[1 : 3 * SHARDS - 2]), refs[3 * SHARDS - 2]
+    weights += [beside.at[i] for i in range(3)]
     back, rows, scaled, bwd_total, fwd_total, held, ready = refs[-7:]
-    hidden = weights[0].shape[1]
-    copies = [
-        pltpu.make_async_copy(w, held.at[:, pl.ds(n * hidden, hidden)], ready.at[n])
-        for n, w in enumerate(weights)
-    ]
+    hidden = weights[0].shape[0]
+    copies = []
+    for n, w in enumerate(weights):
+        units = pl.ds(n // 3 * hidden, hidden)
+        copies.append(pltpu.make_async_copy(w, held.at[n % 3, units], ready.at[n]))
     for copy in copies:
         copy.start()
     unpack_rows(got, {BWD: rows.at[:ROWS], FWD: rows.at[ROWS:], SCALED: scaled})
@@ -261,39 +262,41 @@
     pack_rows({BWD_BACK: bwd_total, FWD_BACK: fwd_total}, back)
 
 
-def experts_of(got, weights, after):
+def experts_of(got, weights, beside, after):
     width = got.shape[2] * CHUNKS
     scratch = [
         pltpu.VMEM((2 * ROWS, width), BF16),
         pltpu.VMEM((ROWS, width), BF16),
         pltpu.VMEM((ROWS, width), BF16),
         pltpu.VMEM((ROWS, width), BF16),
-        pltpu.VMEM((3, SHARDS * weights[0].shape[1], width), BF16),
-        pltpu.SemaphoreType.DMA((SHARDS,)),
+        pltpu.VMEM((3, SHARDS * weights[0].shape[0], width), BF16),
+        pltpu.SemaphoreType.DMA((3 * SHARDS,)),
     ]
     return pl.pallas_call(
         experts_body,
         out_shape=jax.ShapeDtypeStruct((EXPERTS, 2 * PACKED, got.shape[2]), BF16),
-        in_specs=[pl.BlockSpec()] + [HBM] * (len(weights) + 1),
+        in_specs=[pl.BlockSpec()] + [HBM] * (len(weights) + 2),
         scratch_shapes=scratch,
         compiler_params=pltpu.CompilerParams(vmem_limit_bytes=60 * 2**20),
         cost_estimate=cost(8_000_000_000, 14_000_000),
-    )(got, *weights, after)
-
-
-def stack_body(gate, up, down, out):
+    )(got, *weights, beside, after)
+
+
+def stack_body(gate, up, down, after, out):
+    del after
     out[0] = gate[...]
     out[1] = up[...]
     out[2] = down[...]
 
 
-def stack(*arrays):
+def stack(arrays, after):
     return pl.pallas_call(
         stack_body,
         out_shape=jax.ShapeDtypeStruct((3,) + arrays[0].shape, BF16),
+        in_specs=[pl.BlockSpec()] * 3 + [HBM],
         compiler_params=pltpu.CompilerParams(vmem_limit_bytes=60 * 2**20),
         cost_estimate=cost(0, 5_000_000),
-    )(*arrays)
+    )(*arrays, after)
 
 
 def mark_body(ids, out):
@@ -332,13 +335,15 @@
     routes = (bwd_ids[0].T, bwd_gates[0].T, fwd_ids[0].T, fwd_gates[0].T)
     arriving = from_behind(bwd_grad[0], "section", -1)
     shifted = from_behind(fwd_act[0], "section", 1)
-    own = stack(w_gate[0].T, w_up[0].T, w_down[0])
-    across = swap(own, "half")
-    weights = [own, swap(own, "core"), across, swap(across, "core")]
+    own = [w_gate[0].T, w_up[0].T, w_down[0]]
+    across = [swap(x, "half") for x in own]
+    beyond = [swap(x, "core") for x in across]
 
     states = (bwd_input[0], bwd_grad[0], arriving, fwd_act[0], shifted)
-    got = exchange(pick(edges, routes, states))
-    back = exchange(experts_of(got, weights, mark(routes[0])))
+    sent = pick(edges, routes, states)
+    beside = swap(stack(own, across[0]), "core")
+    got = exchange(sent)
+    back = exchange(experts_of(got, own + across + beyond, beside, mark(routes[0])))
     routed_out, input_grad = combine(routes, back)
     return (routed_out[None], input_grad[None])
 

time: 173 us -> 170 us (0.983)
  waiting for transfers between devices: 53.1 us -> 37.2 us
  starting transfers between devices: 51.4 us -> 63.2 us
    ppermute x3 -> x7, waiting for transfers between devices: 19.3 us -> 4.14 us  [swap(): return lax.ppermute(x, axis, [(0, 1), (1, 0)])]
    ppermute x3 -> x7, starting transfers between devices: 30.7 us -> 40.1 us  [swap(): return lax.ppermute(x, axis, [(0, 1), (1, 0)])]
  transfers between devices with their start and end apart: 6 -> 10, of which waited for: 4 -> 5; matrix products, arithmetic and copies ran while one was open for 0% -> 0% of each run, Pallas kernels for 4% -> 6%
where the time goes in v7:
time: 170 us; the launch traced here: 169 us
  starting transfers between devices  63.2 us (37%)
  blocking collectives  40.4 us (24%)
  waiting for transfers between devices  37.2 us (22%)
  Pallas kernels  25.5 us (15%)
    all_to_all x1, blocking collectives, exchange(): lax.all_to_all(x, ('plane', 'pair'), split_axis=0, concat_axis=0, tiled=T...  40.4 us
    ppermute x7, starting transfers between devices, swap(): return lax.ppermute(x, axis, [(0, 1), (1, 0)])  40.1 us
    all_to_all x1, waiting for transfers between devices, exchange(): lax.all_to_all(x, ('plane', 'pair'), split_axis=0, concat_axis=0, tiled=T...  27.3 us
    all_to_all x1, starting transfers between devices, exchange(): lax.all_to_all(x, ('plane', 'pair'), split_axis=0, concat_axis=0, tiled=T...  17.8 us
    pallas_call x1, Pallas kernels, experts_of(): pl.pallas_call(experts_body, out_shape=jax.ShapeDtypeStruct((EXPERTS, 2 *...  12.6 us
    ppermute x2, waiting for transfers between devices, from_behind(): return lax.ppermute(x, axis, pairs)  5.76 us
    ppermute x2, starting transfers between devices, from_behind(): return lax.ppermute(x, axis, pairs)  5.32 us
    pallas_call x1, Pallas kernels, pick(): pl.pallas_call(pick_body, out_shape=jax.ShapeDtypeStruct(out, BF16), in_s...  4.87 us
  transfers between devices with their start and end apart: 10, of which 5 were waited for; matrix products, arithmetic and copies ran while one was open for 0% of the time, Pallas kernels for 6%

profile of v7, /device:TPU:1, one launch (start us, length us, event | category | flops | bytes accessed | tf_op | source)
XLA Modules:
  0.0 169.3 jit_solution(11574953775954072353)
XLA Ops:
  0.6 4.0 %collective-permute-start.2 = (bf16[192,2048]{1,0:T(8,128)(2,1)}, bf16[192,2048]{1,0:T(8,128)(2,1)S(1)}, u32[]{:S(2)}, u32[]{:S(2)}) collective-permute-start(bf16[192,2048]{1,0:T(8,128)(2,1)} %bitcast.26), channel_id=1, source_target_pairs={{0,2},{2,0},{1,3},{3,1},{4,6},{6,4},{5,7},{7,5},{8,10},{10,8},{9,1... | collective-permute-start | bytes 2359304 | tf_op jit(solution)/shard_map/ppermute | solution.py:322
  4.7 1.9 %collective-permute-start.3 = (bf16[192,2048]{1,0:T(8,128)(2,1)}, bf16[192,2048]{1,0:T(8,128)(2,1)}, u32[]{:S(2)}, u32[]{:S(2)}) collective-permute-start(bf16[192,2048]{1,0:T(8,128)(2,1)} %bitcast.29), channel_id=1, source_target_pairs={{0,2},{2,0},{1,3},{3,1},{4,6},{6,4},{5,7},{7,5},{8,10},{10,8},{9,1... | collective-permute-start | bytes 2359304 | tf_op jit(solution)/shard_map/ppermute | solution.py:322
  6.6 3.4 %collective-permute-start.4 = (bf16[192,2048]{1,0:T(8,128)(2,1)}, bf16[192,2048]{1,0:T(8,128)(2,1)}, u32[]{:S(2)}, u32[]{:S(2)}) collective-permute-start(bf16[192,2048]{1,0:T(8,128)(2,1)} %bitcast.32), channel_id=1, source_target_pairs={{0,2},{2,0},{1,3},{3,1},{4,6},{6,4},{5,7},{7,5},{8,10},{10,8},{9,1... | collective-permute-start | bytes 2359304 | tf_op jit(solution)/shard_map/ppermute | solution.py:322
  10.0 1.3 collective-permute-start
  11.3 4.0 %collective-permute-start.1 = (bf16[128,2048]{1,0:T(8,128)(2,1)}, bf16[128,2048]{1,0:T(8,128)(2,1)S(1)}, u32[]{:S(2)}, u32[]{:S(2)}) collective-permute-start(bf16[128,2048]{1,0:T(8,128)(2,1)} %bitcast.38), channel_id=1, source_target_pairs={{0,64},{64,128},{128,192},{192,256},{256,320},{320,384},{384,448},... | collective-permute-start | bytes 1572872 | tf_op jit(solution)/shard_map/ppermute | solution.py:318
  15.3 0.6 add_convert_fusion.edges
  15.9 4.5 %collective-permute-done.refs_2_ = bf16[128,2048]{1,0:T(8,128)(2,1)S(1)} collective-permute-done((bf16[128,2048]{1,0:T(8,128)(2,1)}, bf16[128,2048]{1,0:T(8,128)(2,1)S(1)}, u32[]{:S(2)}, u32[]{:S(2)}) %collective-permute-start) | collective-permute-done | bytes 524320 | tf_op jit(solution)/shard_map/ppermute | solution.py:318
  20.4 1.3 collective-permute-done.1.refs_4_
  21.7 0.8 copy-done.2
  22.5 4.9 %shard_map.113 = bf16[16,240,256]{2,1,0:T(8,128)(2,1)} custom-call(s32[2]{0:T(128)} %add_convert_fusion.edges, s32[8,128]{1,0:T(8,128)} %bitcast.40, f32[8,128]{1,0:T(8,128)} %bitcast.43, s32[8,128]{1,0:T(8,128)} %bitcast.45, f32[8,128]{1,0:T(8,128)} %bitcast.47, bf16[128,2048]{1,0:T(8,128)(2,1)} %bitcast.35, bf16[128,2048]{1,0:T(8,128)(2,1)} %bitcast.37, ...), custom_call_target="tpu_custom_call" | custom-call | flops 1600000000 | bytes 5000000 | tf_op jit(solution)/shard_map/pallas_call | solution.py:142
  27.4 17.8 %all-to-all-start = ((bf16[16,240,256]{2,1,0:T(8,128)(2,1)}), bf16[16,240,256]{2,1,0:T(8,128)(2,1)}, u32[]{:S(2)}, u32[]{:S(2)}) async-start(bf16[16,240,256]{2,1,0:T(8,128)(2,1)} %shard_map.113), calls=%async_computation | async-start | bytes 3932160 | tf_op jit(solution)/shard_map/all_to_all | solution.py:326
  45.2 0.9 copy-done
  46.1 3.2 %shard_map.114 = bf16[3,192,2048]{2,1,0:T(8,128)(2,1)} custom-call(bf16[192,2048]{1,0:T(8,128)(2,1)} %bitcast.27, bf16[192,2048]{1,0:T(8,128)(2,1)} %bitcast.30, bf16[192,2048]{1,0:T(8,128)(2,1)} %bitcast.33, bf16[192,2048]{1,0:T(8,128)(2,1)} %copy-done), custom_call_target="tpu_custom_call" | custom-call | bytes 5000000 | tf_op jit(solution)/shard_map/pallas_call | solution.py:293
  49.3 4.9 %collective-permute-start.8 = (bf16[3,192,2048]{2,1,0:T(8,128)(2,1)}, bf16[3,192,2048]{2,1,0:T(8,128)(2,1)}, u32[]{:S(2)}, u32[]{:S(2)}) collective-permute-start(bf16[3,192,2048]{2,1,0:T(8,128)(2,1)} %shard_map.114), channel_id=1, source_target_pairs={{0,1},{1,0},{2,3},{3,2},{4,5},{5,4},{6,7},{7,6},{8,9},{9,8},{10,11... | collective-permute-start | bytes 7077896 | tf_op jit(solution)/shard_map/ppermute | solution.py:322
  54.2 1.9 %collective-permute-start.5 = (bf16[192,2048]{1,0:T(8,128)(2,1)}, bf16[192,2048]{1,0:T(8,128)(2,1)}, u32[]{:S(2)}, u32[]{:S(2)}) collective-permute-start(bf16[192,2048]{1,0:T(8,128)(2,1)} %copy-done), channel_id=1, source_target_pairs={{0,1},{1,0},{2,3},{3,2},{4,5},{5,4},{6,7},{7,6},{8,9},{9,8},{10,11... | collective-permute-start | bytes 2359304 | tf_op jit(solution)/shard_map/ppermute | solution.py:322
  56.1 2.4 %collective-permute-start.6 = (bf16[192,2048]{1,0:T(8,128)(2,1)}, bf16[192,2048]{1,0:T(8,128)(2,1)}, u32[]{:S(2)}, u32[]{:S(2)}) collective-permute-start(bf16[192,2048]{1,0:T(8,128)(2,1)} %collective-permute-done.3.refs_5_), channel_id=1, source_target_pairs={{0,1},{1,0},{2,3},{3,2},{4,5},{5,4},{6,7},{7,6},{8,9},{9,8},{10,11... | collective-permute-start | bytes 2359304 | tf_op jit(solution)/shard_map/ppermute | solution.py:322
  58.5 3.2 %collective-permute-done.4.refs_6_ = bf16[192,2048]{1,0:T(8,128)(2,1)} collective-permute-done((bf16[192,2048]{1,0:T(8,128)(2,1)}, bf16[192,2048]{1,0:T(8,128)(2,1)}, u32[]{:S(2)}, u32[]{:S(2)}) %collective-permute-start.4) | collective-permute-done | bytes 786464 | tf_op jit(solution)/shard_map/ppermute | solution.py:322
  61.8 21.5 %collective-permute-start.7 = (bf16[192,2048]{1,0:T(8,128)(2,1)}, bf16[192,2048]{1,0:T(8,128)(2,1)}, u32[]{:S(2)}, u32[]{:S(2)}) collective-permute-start(bf16[192,2048]{1,0:T(8,128)(2,1)} %collective-permute-done.4.refs_6_), channel_id=1, source_target_pairs={{0,1},{1,0},{2,3},{3,2},{4,5},{5,4},{6,7},{7,6},{8,9},{9,8},{10,11... | collective-permute-start | bytes 2359304 | tf_op jit(solution)/shard_map/ppermute | solution.py:322
  83.3 1.3 shard_map.115.refs_11_
  84.6 0.9 collective-permute-done.7.refs_9_
  85.5 27.3 %all-to-all-done.refs_0_ = bf16[16,240,256]{2,1,0:T(8,128)(2,1)} async-done(((bf16[16,240,256]{2,1,0:T(8,128)(2,1)}), bf16[16,240,256]{2,1,0:T(8,128)(2,1)}, u32[]{:S(2)}, u32[]{:S(2)}) %all-to-all-start) | async-done | bytes 1966112 | tf_op jit(solution)/shard_map/all_to_all | solution.py:326
  112.8 12.6 %shard_map.116 = bf16[16,160,256]{2,1,0:T(8,128)(2,1)} custom-call(bf16[16,240,256]{2,1,0:T(8,128)(2,1)} %all-to-all-done.refs_0_, bf16[192,2048]{1,0:T(8,128)(2,1)} %bitcast.28, bf16[192,2048]{1,0:T(8,128)(2,1)} %bitcast.31, bf16[192,2048]{1,0:T(8,128)(2,1)} %bitcast.34, bf16[192,2048]{1,0:T(8,128)(2,1)} %copy-done, ...), custom_call_target="tpu_custom_call" | custom-call | flops 8000000000 | bytes 14000000 | tf_op jit(solution)/shard_map/pallas_call | solution.py:275
  125.4 40.4 %all_to_all.10.back = bf16[16,160,256]{2,1,0:T(8,128)(2,1)} all-to-all(bf16[16,160,256]{2,1,0:T(8,128)(2,1)} %shard_map.116), channel_id=1, replica_groups=mesh['section'=8,'plane'=4,'pair'=4,'half'=2,'core'=2] {'plane','pair'}, dimensions={0} | all-to-all | bytes 2621440 | tf_op jit(solution)/shard_map/all_to_all | solution.py:326
  165.7 3.6 %shard_map.117 = (bf16[128,2048]{1,0:T(8,128)(2,1)}, bf16[128,2048]{1,0:T(8,128)(2,1)}) custom-call(s32[8,128]{1,0:T(8,128)} %bitcast.42, f32[8,128]{1,0:T(8,128)} %bitcast.44, s32[8,128]{1,0:T(8,128)} %bitcast.46, f32[8,128]{1,0:T(8,128)} %bitcast.48, bf16[16,160,256]{2,1,0:T(8,128)(2,1)} %all_to_all.10.back), custom_call_target="tpu_custom_call" | custom-call | flops 800000000 | bytes 4000000 | tf_op jit(solution)/shard_map/pallas_call | solution.py:192
  (9 shorter events, 0.0 us)
Async XLA Ops:
  0.6 44.6 %collective-permute-start.2 = (bf16[192,2048]{1,0:T(8,128)(2,1)}, bf16[192,2048]{1,0:T(8,128)(2,1)S(1)}, u32[]{:S(2)}, u32[]{:S(2)}) collective-permute-start(bf16[192,2048]{1,0:T(8,128)(2,1)} %bitcast.26), channel_id=1, source_target_pairs={{0,2},{2,0},{1,3},{3,1},{4,6},{6,4},{5,7},{7,5},{8,10},{10,8},{9,1... | collective-permute-start | bytes 2359304 | tf_op jit(solution)/shard_map/ppermute | solution.py:322
  4.7 51.4 %collective-permute-start.3 = (bf16[192,2048]{1,0:T(8,128)(2,1)}, bf16[192,2048]{1,0:T(8,128)(2,1)}, u32[]{:S(2)}, u32[]{:S(2)}) collective-permute-start(bf16[192,2048]{1,0:T(8,128)(2,1)} %bitcast.29), channel_id=1, source_target_pairs={{0,2},{2,0},{1,3},{3,1},{4,6},{6,4},{5,7},{7,5},{8,10},{10,8},{9,1... | collective-permute-start | bytes 2359304 | tf_op jit(solution)/shard_map/ppermute | solution.py:322
  6.6 55.2 %collective-permute-start.4 = (bf16[192,2048]{1,0:T(8,128)(2,1)}, bf16[192,2048]{1,0:T(8,128)(2,1)}, u32[]{:S(2)}, u32[]{:S(2)}) collective-permute-start(bf16[192,2048]{1,0:T(8,128)(2,1)} %bitcast.32), channel_id=1, source_target_pairs={{0,2},{2,0},{1,3},{3,1},{4,6},{6,4},{5,7},{7,5},{8,10},{10,8},{9,1... | collective-permute-start | bytes 2359304 | tf_op jit(solution)/shard_map/ppermute | solution.py:322
  10.0 10.4 %collective-permute-start = (bf16[128,2048]{1,0:T(8,128)(2,1)}, bf16[128,2048]{1,0:T(8,128)(2,1)S(1)}, u32[]{:S(2)}, u32[]{:S(2)}) collective-permute-start(bf16[128,2048]{1,0:T(8,128)(2,1)} %bitcast.36), channel_id=1, source_target_pairs={{64,0},{128,64},{192,128},{256,192},{320,256},{384,320},{448,384},... | collective-permute-start | bytes 1572872 | tf_op jit(solution)/shard_map/ppermute | solution.py:318
  11.3 10.4 %collective-permute-start.1 = (bf16[128,2048]{1,0:T(8,128)(2,1)}, bf16[128,2048]{1,0:T(8,128)(2,1)S(1)}, u32[]{:S(2)}, u32[]{:S(2)}) collective-permute-start(bf16[128,2048]{1,0:T(8,128)(2,1)} %bitcast.38), channel_id=1, source_target_pairs={{0,64},{64,128},{128,192},{192,256},{256,320},{320,384},{384,448},... | collective-permute-start | bytes 1572872 | tf_op jit(solution)/shard_map/ppermute | solution.py:318
  20.4 1.3 copy-start.1
  21.7 0.8 copy-start.2
  27.4 85.4 %all-to-all-start = ((bf16[16,240,256]{2,1,0:T(8,128)(2,1)}), bf16[16,240,256]{2,1,0:T(8,128)(2,1)}, u32[]{:S(2)}, u32[]{:S(2)}) async-start(bf16[16,240,256]{2,1,0:T(8,128)(2,1)} %shard_map.113), calls=%async_computation | async-start | bytes 3932160 | tf_op jit(solution)/shard_map/all_to_all | solution.py:326
  45.2 0.9 copy-start
  49.3 36.2 %collective-permute-start.8 = (bf16[3,192,2048]{2,1,0:T(8,128)(2,1)}, bf16[3,192,2048]{2,1,0:T(8,128)(2,1)}, u32[]{:S(2)}, u32[]{:S(2)}) collective-permute-start(bf16[3,192,2048]{2,1,0:T(8,128)(2,1)} %shard_map.114), channel_id=1, source_target_pairs={{0,1},{1,0},{2,3},{3,2},{4,5},{5,4},{6,7},{7,6},{8,9},{9,8},{10,11... | collective-permute-start | bytes 7077896 | tf_op jit(solution)/shard_map/ppermute | solution.py:322
  54.2 30.4 %collective-permute-start.5 = (bf16[192,2048]{1,0:T(8,128)(2,1)}, bf16[192,2048]{1,0:T(8,128)(2,1)}, u32[]{:S(2)}, u32[]{:S(2)}) collective-permute-start(bf16[192,2048]{1,0:T(8,128)(2,1)} %copy-done), channel_id=1, source_target_pairs={{0,1},{1,0},{2,3},{3,2},{4,5},{5,4},{6,7},{7,6},{8,9},{9,8},{10,11... | collective-permute-start | bytes 2359304 | tf_op jit(solution)/shard_map/ppermute | solution.py:322
  56.1 28.5 %collective-permute-start.6 = (bf16[192,2048]{1,0:T(8,128)(2,1)}, bf16[192,2048]{1,0:T(8,128)(2,1)}, u32[]{:S(2)}, u32[]{:S(2)}) collective-permute-start(bf16[192,2048]{1,0:T(8,128)(2,1)} %collective-permute-done.3.refs_5_), channel_id=1, source_target_pairs={{0,1},{1,0},{2,3},{3,2},{4,5},{5,4},{6,7},{7,6},{8,9},{9,8},{10,11... | collective-permute-start | bytes 2359304 | tf_op jit(solution)/shard_map/ppermute | solution.py:322
  61.8 23.8 %collective-permute-start.7 = (bf16[192,2048]{1,0:T(8,128)(2,1)}, bf16[192,2048]{1,0:T(8,128)(2,1)}, u32[]{:S(2)}, u32[]{:S(2)}) collective-permute-start(bf16[192,2048]{1,0:T(8,128)(2,1)} %collective-permute-done.4.refs_6_), channel_id=1, source_target_pairs={{0,1},{1,0},{2,3},{3,2},{4,5},{5,4},{6,7},{7,6},{8,9},{9,8},{10,11... | collective-permute-start | bytes 2359304 | tf_op jit(solution)/shard_map/ppermute | solution.py:322

commit v8 on v7

--- a/solution.py
+++ b/solution.py
@@ -242,17 +242,24 @@
     for n, w in enumerate(weights):
         units = pl.ds(n // 3 * hidden, hidden)
         copies.append(pltpu.make_async_copy(w, held.at[n % 3, units], ready.at[n]))
-    for copy in copies:
-        copy.start()
+    for kind in range(3):
+        for copy in copies[kind::3]:
+            copy.start()
+
+    def arrived(kind):
+        for copy in copies[kind::3]:
+            copy.wait()
+
     unpack_rows(got, {BWD: rows.at[:ROWS], FWD: rows.at[ROWS:], SCALED: scaled})
-    for copy in copies:
-        copy.wait()
     gate, up, down = held.at[0], held.at[1], held.at[2]
+    arrived(0)
     gates = dot_nt(rows[...], gate[...])
+    arrived(1)
     ups = dot_nt(rows[...], up[...])
     gate_back, gate_pre = gates[:ROWS], gates[ROWS:]
     up_back, up_pre = ups[:ROWS], ups[ROWS:]
     act = (gate_pre / (1.0 + jnp.exp(-gate_pre)) * up_pre).astype(BF16)
+    arrived(2)
     dact = dot_nt(scaled[...], down[...])
     sigma = 1.0 / (1.0 + jnp.exp(-gate_back))
     dgate = (dact * up_back * sigma * (1.0 + gate_back * (1.0 - sigma))).astype(BF16)

time: 170 us -> 169 us (level)
  no operation moved by 1% of the time
where the time goes in v8:
time: 169 us
  starting transfers between devices  63.2 us (37%)
  blocking collectives  40.3 us (24%)
  waiting for transfers between devices  37.2 us (22%)
  Pallas kernels  24.8 us (15%)
    all_to_all x1, blocking collectives, exchange(): lax.all_to_all(x, ('plane', 'pair'), split_axis=0, concat_axis=0, tiled=T...  40.3 us
    ppermute x7, starting transfers between devices, swap(): return lax.ppermute(x, axis, [(0, 1), (1, 0)])  40.1 us
    all_to_all x1, waiting for transfers between devices, exchange(): lax.all_to_all(x, ('plane', 'pair'), split_axis=0, concat_axis=0, tiled=T...  27.3 us
    all_to_all x1, starting transfers between devices, exchange(): lax.all_to_all(x, ('plane', 'pair'), split_axis=0, concat_axis=0, tiled=T...  17.8 us
    pallas_call x1, Pallas kernels, experts_of(): pl.pallas_call(experts_body, out_shape=jax.ShapeDtypeStruct((EXPERTS, 2 *...  11.8 us
    ppermute x2, waiting for transfers between devices, from_behind(): return lax.ppermute(x, axis, pairs)  5.76 us
    ppermute x2, starting transfers between devices, from_behind(): return lax.ppermute(x, axis, pairs)  5.32 us
    pallas_call x1, Pallas kernels, pick(): pl.pallas_call(pick_body, out_shape=jax.ShapeDtypeStruct(out, BF16), in_s...  4.87 us
  transfers between devices with their start and end apart: 10, of which 5 were waited for; matrix products, arithmetic and copies ran while one was open for 0% of the time, Pallas kernels for 6%

profile of v8, /device:TPU:1, one launch (start us, length us, event | category | flops | bytes accessed | tf_op | source)
XLA Modules:
  0.0 168.5 jit_solution(919709073858295090)
XLA Ops:
  0.6 4.0 %collective-permute-start.2 = (bf16[192,2048]{1,0:T(8,128)(2,1)}, bf16[192,2048]{1,0:T(8,128)(2,1)S(1)}, u32[]{:S(2)}, u32[]{:S(2)}) collective-permute-start(bf16[192,2048]{1,0:T(8,128)(2,1)} %bitcast.26), channel_id=1, source_target_pairs={{0,2},{2,0},{1,3},{3,1},{4,6},{6,4},{5,7},{7,5},{8,10},{10,8},{9,1... | collective-permute-start | bytes 2359304 | tf_op jit(solution)/shard_map/ppermute | solution.py:329
  4.7 1.9 %collective-permute-start.3 = (bf16[192,2048]{1,0:T(8,128)(2,1)}, bf16[192,2048]{1,0:T(8,128)(2,1)}, u32[]{:S(2)}, u32[]{:S(2)}) collective-permute-start(bf16[192,2048]{1,0:T(8,128)(2,1)} %bitcast.29), channel_id=1, source_target_pairs={{0,2},{2,0},{1,3},{3,1},{4,6},{6,4},{5,7},{7,5},{8,10},{10,8},{9,1... | collective-permute-start | bytes 2359304 | tf_op jit(solution)/shard_map/ppermute | solution.py:329
  6.6 3.4 %collective-permute-start.4 = (bf16[192,2048]{1,0:T(8,128)(2,1)}, bf16[192,2048]{1,0:T(8,128)(2,1)}, u32[]{:S(2)}, u32[]{:S(2)}) collective-permute-start(bf16[192,2048]{1,0:T(8,128)(2,1)} %bitcast.32), channel_id=1, source_target_pairs={{0,2},{2,0},{1,3},{3,1},{4,6},{6,4},{5,7},{7,5},{8,10},{10,8},{9,1... | collective-permute-start | bytes 2359304 | tf_op jit(solution)/shard_map/ppermute | solution.py:329
  10.0 1.3 collective-permute-start
  11.3 4.0 %collective-permute-start.1 = (bf16[128,2048]{1,0:T(8,128)(2,1)}, bf16[128,2048]{1,0:T(8,128)(2,1)S(1)}, u32[]{:S(2)}, u32[]{:S(2)}) collective-permute-start(bf16[128,2048]{1,0:T(8,128)(2,1)} %bitcast.38), channel_id=1, source_target_pairs={{0,64},{64,128},{128,192},{192,256},{256,320},{320,384},{384,448},... | collective-permute-start | bytes 1572872 | tf_op jit(solution)/shard_map/ppermute | solution.py:325
  15.3 0.6 add_convert_fusion.edges
  15.9 4.5 %collective-permute-done.refs_2_ = bf16[128,2048]{1,0:T(8,128)(2,1)S(1)} collective-permute-done((bf16[128,2048]{1,0:T(8,128)(2,1)}, bf16[128,2048]{1,0:T(8,128)(2,1)S(1)}, u32[]{:S(2)}, u32[]{:S(2)}) %collective-permute-start) | collective-permute-done | bytes 524320 | tf_op jit(solution)/shard_map/ppermute | solution.py:325
  20.4 1.3 collective-permute-done.1.refs_4_
  21.7 0.8 copy-done.2
  22.5 4.9 %shard_map.113 = bf16[16,240,256]{2,1,0:T(8,128)(2,1)} custom-call(s32[2]{0:T(128)} %add_convert_fusion.edges, s32[8,128]{1,0:T(8,128)} %bitcast.40, f32[8,128]{1,0:T(8,128)} %bitcast.43, s32[8,128]{1,0:T(8,128)} %bitcast.45, f32[8,128]{1,0:T(8,128)} %bitcast.47, bf16[128,2048]{1,0:T(8,128)(2,1)} %bitcast.35, bf16[128,2048]{1,0:T(8,128)(2,1)} %bitcast.37, ...), custom_call_target="tpu_custom_call" | custom-call | flops 1600000000 | bytes 5000000 | tf_op jit(solution)/shard_map/pallas_call | solution.py:142
  27.4 17.8 %all-to-all-start = ((bf16[16,240,256]{2,1,0:T(8,128)(2,1)}), bf16[16,240,256]{2,1,0:T(8,128)(2,1)}, u32[]{:S(2)}, u32[]{:S(2)}) async-start(bf16[16,240,256]{2,1,0:T(8,128)(2,1)} %shard_map.113), calls=%async_computation | async-start | bytes 3932160 | tf_op jit(solution)/shard_map/all_to_all | solution.py:333
  45.2 0.9 copy-done
  46.1 3.2 %shard_map.114 = bf16[3,192,2048]{2,1,0:T(8,128)(2,1)} custom-call(bf16[192,2048]{1,0:T(8,128)(2,1)} %bitcast.27, bf16[192,2048]{1,0:T(8,128)(2,1)} %bitcast.30, bf16[192,2048]{1,0:T(8,128)(2,1)} %bitcast.33, bf16[192,2048]{1,0:T(8,128)(2,1)} %copy-done), custom_call_target="tpu_custom_call" | custom-call | bytes 5000000 | tf_op jit(solution)/shard_map/pallas_call | solution.py:300
  49.3 4.9 %collective-permute-start.8 = (bf16[3,192,2048]{2,1,0:T(8,128)(2,1)}, bf16[3,192,2048]{2,1,0:T(8,128)(2,1)}, u32[]{:S(2)}, u32[]{:S(2)}) collective-permute-start(bf16[3,192,2048]{2,1,0:T(8,128)(2,1)} %shard_map.114), channel_id=1, source_target_pairs={{0,1},{1,0},{2,3},{3,2},{4,5},{5,4},{6,7},{7,6},{8,9},{9,8},{10,11... | collective-permute-start | bytes 7077896 | tf_op jit(solution)/shard_map/ppermute | solution.py:329
  54.2 1.9 %collective-permute-start.5 = (bf16[192,2048]{1,0:T(8,128)(2,1)}, bf16[192,2048]{1,0:T(8,128)(2,1)}, u32[]{:S(2)}, u32[]{:S(2)}) collective-permute-start(bf16[192,2048]{1,0:T(8,128)(2,1)} %copy-done), channel_id=1, source_target_pairs={{0,1},{1,0},{2,3},{3,2},{4,5},{5,4},{6,7},{7,6},{8,9},{9,8},{10,11... | collective-permute-start | bytes 2359304 | tf_op jit(solution)/shard_map/ppermute | solution.py:329
  56.1 2.4 %collective-permute-start.6 = (bf16[192,2048]{1,0:T(8,128)(2,1)}, bf16[192,2048]{1,0:T(8,128)(2,1)}, u32[]{:S(2)}, u32[]{:S(2)}) collective-permute-start(bf16[192,2048]{1,0:T(8,128)(2,1)} %collective-permute-done.3.refs_5_), channel_id=1, source_target_pairs={{0,1},{1,0},{2,3},{3,2},{4,5},{5,4},{6,7},{7,6},{8,9},{9,8},{10,11... | collective-permute-start | bytes 2359304 | tf_op jit(solution)/shard_map/ppermute | solution.py:329
  58.5 3.2 %collective-permute-done.4.refs_6_ = bf16[192,2048]{1,0:T(8,128)(2,1)} collective-permute-done((bf16[192,2048]{1,0:T(8,128)(2,1)}, bf16[192,2048]{1,0:T(8,128)(2,1)}, u32[]{:S(2)}, u32[]{:S(2)}) %collective-permute-start.4) | collective-permute-done | bytes 786464 | tf_op jit(solution)/shard_map/ppermute | solution.py:329
  61.8 21.5 %collective-permute-start.7 = (bf16[192,2048]{1,0:T(8,128)(2,1)}, bf16[192,2048]{1,0:T(8,128)(2,1)}, u32[]{:S(2)}, u32[]{:S(2)}) collective-permute-start(bf16[192,2048]{1,0:T(8,128)(2,1)} %collective-permute-done.4.refs_6_), channel_id=1, source_target_pairs={{0,1},{1,0},{2,3},{3,2},{4,5},{5,4},{6,7},{7,6},{8,9},{9,8},{10,11... | collective-permute-start | bytes 2359304 | tf_op jit(solution)/shard_map/ppermute | solution.py:329
  83.3 1.3 shard_map.115.refs_11_
  84.6 0.9 collective-permute-done.7.refs_9_
  85.5 27.3 %all-to-all-done.refs_0_ = bf16[16,240,256]{2,1,0:T(8,128)(2,1)} async-done(((bf16[16,240,256]{2,1,0:T(8,128)(2,1)}), bf16[16,240,256]{2,1,0:T(8,128)(2,1)}, u32[]{:S(2)}, u32[]{:S(2)}) %all-to-all-start) | async-done | bytes 1966112 | tf_op jit(solution)/shard_map/all_to_all | solution.py:333
  112.8 11.8 %shard_map.116 = bf16[16,160,256]{2,1,0:T(8,128)(2,1)} custom-call(bf16[16,240,256]{2,1,0:T(8,128)(2,1)} %all-to-all-done.refs_0_, bf16[192,2048]{1,0:T(8,128)(2,1)} %bitcast.28, bf16[192,2048]{1,0:T(8,128)(2,1)} %bitcast.31, bf16[192,2048]{1,0:T(8,128)(2,1)} %bitcast.34, bf16[192,2048]{1,0:T(8,128)(2,1)} %copy-done, ...), custom_call_target="tpu_custom_call" | custom-call | flops 8000000000 | bytes 14000000 | tf_op jit(solution)/shard_map/pallas_call | solution.py:282
  124.6 40.3 %all_to_all.10.back = bf16[16,160,256]{2,1,0:T(8,128)(2,1)} all-to-all(bf16[16,160,256]{2,1,0:T(8,128)(2,1)} %shard_map.116), channel_id=1, replica_groups=mesh['section'=8,'plane'=4,'pair'=4,'half'=2,'core'=2] {'plane','pair'}, dimensions={0} | all-to-all | bytes 2621440 | tf_op jit(solution)/shard_map/all_to_all | solution.py:333
  164.9 3.6 %shard_map.117 = (bf16[128,2048]{1,0:T(8,128)(2,1)}, bf16[128,2048]{1,0:T(8,128)(2,1)}) custom-call(s32[8,128]{1,0:T(8,128)} %bitcast.42, f32[8,128]{1,0:T(8,128)} %bitcast.44, s32[8,128]{1,0:T(8,128)} %bitcast.46, f32[8,128]{1,0:T(8,128)} %bitcast.48, bf16[16,160,256]{2,1,0:T(8,128)(2,1)} %all_to_all.10.back), custom_call_target="tpu_custom_call" | custom-call | flops 800000000 | bytes 4000000 | tf_op jit(solution)/shard_map/pallas_call | solution.py:192
  (9 shorter events, 0.0 us)
Async XLA Ops:
  0.6 44.6 %collective-permute-start.2 = (bf16[192,2048]{1,0:T(8,128)(2,1)}, bf16[192,2048]{1,0:T(8,128)(2,1)S(1)}, u32[]{:S(2)}, u32[]{:S(2)}) collective-permute-start(bf16[192,2048]{1,0:T(8,128)(2,1)} %bitcast.26), channel_id=1, source_target_pairs={{0,2},{2,0},{1,3},{3,1},{4,6},{6,4},{5,7},{7,5},{8,10},{10,8},{9,1... | collective-permute-start | bytes 2359304 | tf_op jit(solution)/shard_map/ppermute | solution.py:329
  4.7 51.4 %collective-permute-start.3 = (bf16[192,2048]{1,0:T(8,128)(2,1)}, bf16[192,2048]{1,0:T(8,128)(2,1)}, u32[]{:S(2)}, u32[]{:S(2)}) collective-permute-start(bf16[192,2048]{1,0:T(8,128)(2,1)} %bitcast.29), channel_id=1, source_target_pairs={{0,2},{2,0},{1,3},{3,1},{4,6},{6,4},{5,7},{7,5},{8,10},{10,8},{9,1... | collective-permute-start | bytes 2359304 | tf_op jit(solution)/shard_map/ppermute | solution.py:329
  6.6 55.2 %collective-permute-start.4 = (bf16[192,2048]{1,0:T(8,128)(2,1)}, bf16[192,2048]{1,0:T(8,128)(2,1)}, u32[]{:S(2)}, u32[]{:S(2)}) collective-permute-start(bf16[192,2048]{1,0:T(8,128)(2,1)} %bitcast.32), channel_id=1, source_target_pairs={{0,2},{2,0},{1,3},{3,1},{4,6},{6,4},{5,7},{7,5},{8,10},{10,8},{9,1... | collective-permute-start | bytes 2359304 | tf_op jit(solution)/shard_map/ppermute | solution.py:329
  10.0 10.4 %collective-permute-start = (bf16[128,2048]{1,0:T(8,128)(2,1)}, bf16[128,2048]{1,0:T(8,128)(2,1)S(1)}, u32[]{:S(2)}, u32[]{:S(2)}) collective-permute-start(bf16[128,2048]{1,0:T(8,128)(2,1)} %bitcast.36), channel_id=1, source_target_pairs={{64,0},{128,64},{192,128},{256,192},{320,256},{384,320},{448,384},... | collective-permute-start | bytes 1572872 | tf_op jit(solution)/shard_map/ppermute | solution.py:325
  11.3 10.4 %collective-permute-start.1 = (bf16[128,2048]{1,0:T(8,128)(2,1)}, bf16[128,2048]{1,0:T(8,128)(2,1)S(1)}, u32[]{:S(2)}, u32[]{:S(2)}) collective-permute-start(bf16[128,2048]{1,0:T(8,128)(2,1)} %bitcast.38), channel_id=1, source_target_pairs={{0,64},{64,128},{128,192},{192,256},{256,320},{320,384},{384,448},... | collective-permute-start | bytes 1572872 | tf_op jit(solution)/shard_map/ppermute | solution.py:325
  20.4 1.3 copy-start.1
  21.7 0.8 copy-start.2
  27.4 85.4 %all-to-all-start = ((bf16[16,240,256]{2,1,0:T(8,128)(2,1)}), bf16[16,240,256]{2,1,0:T(8,128)(2,1)}, u32[]{:S(2)}, u32[]{:S(2)}) async-start(bf16[16,240,256]{2,1,0:T(8,128)(2,1)} %shard_map.113), calls=%async_computation | async-start | bytes 3932160 | tf_op jit(solution)/shard_map/all_to_all | solution.py:333
  45.2 0.9 copy-start
  49.3 36.2 %collective-permute-start.8 = (bf16[3,192,2048]{2,1,0:T(8,128)(2,1)}, bf16[3,192,2048]{2,1,0:T(8,128)(2,1)}, u32[]{:S(2)}, u32[]{:S(2)}) collective-permute-start(bf16[3,192,2048]{2,1,0:T(8,128)(2,1)} %shard_map.114), channel_id=1, source_target_pairs={{0,1},{1,0},{2,3},{3,2},{4,5},{5,4},{6,7},{7,6},{8,9},{9,8},{10,11... | collective-permute-start | bytes 7077896 | tf_op jit(solution)/shard_map/ppermute | solution.py:329
  54.2 30.4 %collective-permute-start.5 = (bf16[192,2048]{1,0:T(8,128)(2,1)}, bf16[192,2048]{1,0:T(8,128)(2,1)}, u32[]{:S(2)}, u32[]{:S(2)}) collective-permute-start(bf16[192,2048]{1,0:T(8,128)(2,1)} %copy-done), channel_id=1, source_target_pairs={{0,1},{1,0},{2,3},{3,2},{4,5},{5,4},{6,7},{7,6},{8,9},{9,8},{10,11... | collective-permute-start | bytes 2359304 | tf_op jit(solution)/shard_map/ppermute | solution.py:329
  56.1 28.5 %collective-permute-start.6 = (bf16[192,2048]{1,0:T(8,128)(2,1)}, bf16[192,2048]{1,0:T(8,128)(2,1)}, u32[]{:S(2)}, u32[]{:S(2)}) collective-permute-start(bf16[192,2048]{1,0:T(8,128)(2,1)} %collective-permute-done.3.refs_5_), channel_id=1, source_target_pairs={{0,1},{1,0},{2,3},{3,2},{4,5},{5,4},{6,7},{7,6},{8,9},{9,8},{10,11... | collective-permute-start | bytes 2359304 | tf_op jit(solution)/shard_map/ppermute | solution.py:329
  61.8 23.8 %collective-permute-start.7 = (bf16[192,2048]{1,0:T(8,128)(2,1)}, bf16[192,2048]{1,0:T(8,128)(2,1)}, u32[]{:S(2)}, u32[]{:S(2)}) collective-permute-start(bf16[192,2048]{1,0:T(8,128)(2,1)} %collective-permute-done.4.refs_6_), channel_id=1, source_target_pairs={{0,1},{1,0},{2,3},{3,2},{4,5},{5,4},{6,7},{7,6},{8,9},{9,8},{10,11... | collective-permute-start | bytes 2359304 | tf_op jit(solution)/shard_map/ppermute | solution.py:329
